TPU v7x, 128 devices: a whole 4x4x4 slice. The times are simulated.
128 devices in a mesh: grp: 16 (over z, x_lo, core), sp: 8 (over x_hi, y).
Axes of the slice: x: 4 (x_hi: 2, x_lo: 2; x = x_hi * 2 + x_lo), y: 4, z: 4, core: 2. Of those that a mesh axis runs over, the one named last changes fastest.
Arguments:
- hidden_in: bfloat16 [16, 1024, 4096], P('grp', 'sp'), may hold values from -6 to 6
- queries: bfloat16 [16, 1024, 4096], P('grp', 'sp'), may hold values from -5 to 5
- key_heads: bfloat16 [16, 1024, 1024], P('grp', 'sp'), may hold values from -5 to 5
- saved_value_heads: bfloat16 [16, 1024, 1024], P('grp', 'sp'), may hold values from -6 to 6
- out_grads: bfloat16 [16, 1024, 4096], P('grp', 'sp'), may hold values from -24 to 24
- doc_ids: int32 [16, 1024], P('grp', 'sp'), may hold values from 0 to 2, never falling along the last dimension, each value on 1 to 512 neighbouring positions
Outputs:
- query_weight_grad: float32 [4096, 4096], P('grp', 'sp')
- key_weight_grad: float32 [4096, 1024], P('grp', 'sp')
- value_weight_grad: float32 [4096, 1024], P('grp', 'sp')
Inputs may be any that keep to these rules, and one draw needn't show every extreme that they name: `doc_ids`: within each group's 1024 tokens the ids never fall; a document holds 1 to 512 tokens.
All inputs are finite; a program needn't handle non-finite values.
Results may differ from a plain program's by a relative error of at most 0.011.
Values may be sent and summed in bfloat16 or wider, within the bound.
No kernel may reach another device: no remote copies, remote signals or barrier semaphores. Data moves between devices by JAX's collectives and lax.ppermute only.
A program may use at most 128 MiB of HBM per device.

v0:
```python
import math

import jax
import jax.numpy as jnp
from jax import lax
from jax.experimental import pallas as pl
from jax.experimental.pallas import tpu as pltpu
from jax.sharding import PartitionSpec as P

HEAD = 128
NEG = -1e30
SCALE = 1.0 / math.sqrt(HEAD)
FACTOR = 16384 ** -0.5
NJ = 1
BW = 256 // NJ
VM = 60 * 1024 * 1024
F32 = jnp.float32
BF16 = jnp.bfloat16
ANY = pl.BlockSpec(memory_space=pl.ANY)
VMEM = pl.BlockSpec(memory_space=pltpu.VMEM)


def place():
    g = lax.axis_index("grp")
    s = lax.axis_index("sp")
    return dict(
        z=g // 4, x=(s // 4) * 2 + (g // 2) % 2, c=lax.rem(g, 2), y=lax.rem(s, 4), xh=s // 4
    )


def pairs(dx=0, dy=0, dz=0, dc=0, only_half=None):
    out = []
    for z in range(4):
        for x in range(4):
            for y in range(4):
                for c in range(2):
                    if only_half is not None and x // 2 != only_half:
                        continue

                    def flat(z, x, y, c):
                        return (z * 4 + (x % 2) * 2 + c) * 8 + (x // 2) * 4 + y

                    out.append(
                        (
                            flat(z, x, y, c),
                            flat((z + dz) % 4, (x + dx) % 4, (y + dy) % 4, (c + dc) % 2),
                        )
                    )
    return out


def send(a, **k):
    return lax.ppermute(a, ("grp", "sp"), pairs(**k))


def call(body, outs, scratch, flops, nbytes, in_specs, out_specs):
    return pl.pallas_call(
        body,
        out_shape=outs,
        in_specs=in_specs,
        out_specs=out_specs,
        scratch_shapes=scratch,
        compiler_params=pltpu.CompilerParams(vmem_limit_bytes=VM),
        cost_estimate=pl.CostEstimate(flops=flops, bytes_accessed=nbytes, transcendentals=0),
    )


def run_copies(todo, sems):
    made = [pltpu.make_async_copy(a, b, sems.at[i]) for i, (a, b) in enumerate(todo)]
    for m in made:
        m.start()
    for m in made:
        m.wait()


def mult(i, n):
    return pl.multiple_of(i * n, n)


def pack_heads(h, queries, keys, values, grads, ids):
    extra = 128 if h == 0 else 0

    def body(q, k, v, g, i, o1, o2, o3, o0, sems):
        y = place()["y"]
        todo = []
        for d, o in ((1, o1), (2, o2), (3, o3), (0, o0)):
            s = h * 4 + lax.rem(y + d, 4)
            at = 0
            if d:
                todo += [
                    (q.at[0, :, pl.ds(mult(s, 512), 512)], o.at[:, 0:512]),
                    (g.at[0, :, pl.ds(mult(s, 512), 512)], o.at[:, 512:1024]),
                ]
                at = 1024
            todo += [
                (k.at[0, :, pl.ds(mult(s, 128), 128)], o.at[:, at : at + 128]),
                (v.at[0, :, pl.ds(mult(s, 128), 128)], o.at[:, at + 128 : at + 256]),
            ]
            if h == 0:
                todo.append((i, o.at[:, at + 256 : at + 384]))
        run_copies(todo, sems)

    shape = jax.ShapeDtypeStruct((128, 1280 + extra), BF16)
    return call(
        body,
        [shape] * 3 + [jax.ShapeDtypeStruct((128, 256 + extra), BF16)],
        [pltpu.SemaphoreType.DMA((19,))],
        0,
        4 * 10**6,
        [ANY] * 5,
        [VMEM] * 4,
    )(queries, keys, values, grads, ids)


def pack_inputs(hidden):
    def body(x, *refs):
        keep, give, sems = refs[:NJ], refs[NJ : 2 * NJ], refs[2 * NJ]
        c = place()["c"]
        todo = []
        for j in range(NJ):
            for b in range(8):
                for o, cc in ((keep[j], c), (give[j], 1 - c)):
                    col = pl.multiple_of((b * 2 + cc) * 256 + j * BW, BW)
                    todo.append((x.at[0, :, pl.ds(col, BW)], o.at[:, b * BW : (b + 1) * BW]))
        run_copies(todo, sems)

    shape = jax.ShapeDtypeStruct((128, 8 * BW), BF16)
    return call(
        body,
        [shape] * (2 * NJ),
        [pltpu.SemaphoreType.DMA((16 * NJ,))],
        0,
        4 * 10**6,
        [ANY],
        [VMEM] * (2 * NJ),
    )(hidden)


def attention(h, queries, grads, own, pieces, before, own0, pieces0, before0):
    def body(q, g, kv, p1, p2, p3, pv, kv0, i1, i2, i3, pv0, dq, dkv, dprev, qs, gs, ks, vs, ids, bias, acck, accv, sems):
        here = place()
        y, xh = here["y"], here["xh"]
        s = h * 4 + y
        row = mult(y, 128)
        todo = [
            (q.at[0, :, pl.ds(mult(s, 512), 512)], qs.at[pl.ds(row, 128), :]),
            (g.at[0, :, pl.ds(mult(s, 512), 512)], gs.at[pl.ds(row, 128), :]),
            (kv.at[:, 0:128], ks.at[pl.ds(row + 512, 128), :]),
            (kv.at[:, 128:256], vs.at[pl.ds(row + 512, 128), :]),
            (kv0.at[:, 256:384], ids.at[pl.ds(row + 512, 128), :]),
        ]
        for d, p, i in ((1, p1, i1), (2, p2, i2), (3, p3, i3)):
            r = mult(lax.rem(y - d + 4, 4), 128)
            todo += [
                (p.at[:, 0:512], qs.at[pl.ds(r, 128), :]),
                (p.at[:, 512:1024], gs.at[pl.ds(r, 128), :]),
                (p.at[:, 1024:1152], ks.at[pl.ds(r + 512, 128), :]),
                (p.at[:, 1152:1280], vs.at[pl.ds(r + 512, 128), :]),
                (i.at[:, 1280:1408], ids.at[pl.ds(r + 512, 128), :]),
            ]
        for d in range(4):
            r = mult(lax.rem(y - d + 4, 4), 128)
            here_rows = pl.ds(d * 128, 128)
            todo += [
                (pv.at[here_rows, 0:128], ks.at[pl.ds(r, 128), :]),
                (pv.at[here_rows, 128:256], vs.at[pl.ds(r, 128), :]),
                (pv0.at[here_rows, 256:384], ids.at[pl.ds(r, 128), :]),
            ]
        run_copies(todo, sems)

        low = xh * 512
        own_ids = ids[512:1024, :].astype(F32)
        prev_ids = ids[0:512, :].astype(F32)
        second = xh.astype(F32)

        def count(top):
            a = jnp.sum(jnp.where(own_ids <= top, 1.0, 0.0), axis=0, keepdims=True)
            b = jnp.sum(jnp.where(prev_ids <= top, 1.0, 0.0), axis=0, keepdims=True)
            return (a + second * b)[:, 0:1].astype(jnp.int32)

        first, both = count(0.5), count(1.5)
        acck[...] = jnp.zeros_like(acck)
        accv[...] = jnp.zeros_like(accv)
        for blk in range(2):
            lo = blk * 256
            t = lax.broadcasted_iota(jnp.int32, (1, 256), 1) + lo
            ta = t + low
            start = jnp.where(ta < first, 0, jnp.where(ta < both, first, both)) - low
            u = lax.broadcasted_iota(jnp.int32, (768, 256), 0) + (lo - 512)
            bias[blk] = jnp.where((u <= t) & (u >= start), 0.0, NEG)

        def head(hq, _):
            cols = pl.ds(mult(hq, 128), 128)
            for blk in range(2):
                lo = blk * 256
                keys = ks[lo : lo + 768, :]
                vals = vs[lo : lo + 768, :]
                qq = qs[lo : lo + 256, cols]
                gg = gs[lo : lo + 256, cols]
                nt = (((1,), (1,)), ((), ()))
                sc = lax.dot_general(keys, qq, nt, preferred_element_type=F32) * SCALE + bias[blk]
                e = jnp.exp(sc - jnp.max(sc, axis=0, keepdims=True))
                p = e * (1.0 / jnp.sum(e, axis=0, keepdims=True))
                p_low = p.astype(BF16)
                dp = lax.dot_general(vals, gg, nt, preferred_element_type=F32)
                delta = jnp.sum(p_low.astype(F32) * dp, axis=0, keepdims=True)
                ds = (p * (dp - delta) * SCALE).astype(BF16)
                tn = (((0,), (0,)), ((), ()))
                dqt = lax.dot_general(keys, ds, tn, preferred_element_type=F32)
                dq[cols, lo : lo + 256] = dqt.astype(BF16)
                acck[lo : lo + 768, :] += jnp.dot(ds, qq, preferred_element_type=F32)
                accv[lo : lo + 768, :] += jnp.dot(p_low, gg, preferred_element_type=F32)
            return 0

        lax.fori_loop(0, 4, head, 0)
        dkv[0:128, :] = acck[512:1024, :].T
        dkv[128:256, :] = accv[512:1024, :].T
        dprev[0:128, :] = acck[0:512, :].astype(BF16).T
        dprev[128:256, :] = accv[0:512, :].astype(BF16).T

    return call(
        body,
        [
            jax.ShapeDtypeStruct((512, 512), BF16),
            jax.ShapeDtypeStruct((256, 512), F32),
            jax.ShapeDtypeStruct((256, 512), BF16),
        ],
        [
            pltpu.VMEM((512, 512), BF16),
            pltpu.VMEM((512, 512), BF16),
            pltpu.VMEM((1024, 128), BF16),
            pltpu.VMEM((1024, 128), BF16),
            pltpu.VMEM((1024, 128), BF16),
            pltpu.VMEM((2, 768, 256), F32),
            pltpu.VMEM((1024, 128), F32),
            pltpu.VMEM((1024, 128), F32),
            pltpu.SemaphoreType.DMA((32,)),
        ],
        4 * 10**9,
        4 * 10**6,
        [ANY] * 12,
        [VMEM] * 3,
    )(queries, grads, own, *pieces, before, own0, *pieces0, before0)


def load_inputs(refs, xs, y):
    own, r1, r3, r2a, r2b = refs

    def at(d, half):
        return xs.at[pl.ds(pl.multiple_of(lax.rem(y - d + 4, 4) * 128 + half * 512, 128), 128), :]

    todo = []
    for d, r in ((0, own), (1, r1), (3, r3)):
        todo += [(r.at[0:128, :], at(d, 0)), (r.at[128:256, :], at(d, 1))]
    return todo + [(r2a, at(2, 0)), (r2b, at(2, 1))]


def weights_a(gt, inputs):
    def body(a0, b0, a1, b1, i0, i1, i2, i3, i4, o0, o1, o2, o3, xs, gs, sems):
        here = place()
        todo = load_inputs((i0, i1, i2, i3, i4), xs, here["y"])
        for h, (a, b) in enumerate(((a0, b0), (a1, b1))):
            todo += [
                (a.at[0:384, :], gs.at[h * 384 : (h + 1) * 384, 0:512]),
                (b.at[0:384, :], gs.at[h * 384 : (h + 1) * 384, 512:1024]),
            ]
        run_copies(todo, sems)
        for d, o in ((1, o1), (2, o2), (3, o3), (0, o0)):
            col = mult(lax.rem(here["z"] + d, 4), 2 * BW)
            o[...] = jnp.dot(
                gs[...], xs[:, pl.ds(col, 2 * BW)], preferred_element_type=F32
            ).astype(o.dtype)

    return call(
        body,
        [jax.ShapeDtypeStruct((768, 2 * BW), F32 if d == 0 else BF16) for d in range(4)],
        [
            pltpu.VMEM((1024, 8 * BW), BF16),
            pltpu.VMEM((768, 1024), BF16),
            pltpu.SemaphoreType.DMA((12,)),
        ],
        3 * 10**9 // NJ,
        8 * 10**6 // NJ,
        [ANY] * 9,
        [VMEM] * 4,
    )(*gt, *inputs)


def weights_b(gt, kvt, inputs):
    def body(a0, b0, a1, b1, k0, l0, k1, l1, i0, i1, i2, i3, i4, o0, o1, o2, o3, xs, gs, sems):
        here = place()
        todo = load_inputs((i0, i1, i2, i3, i4), xs, here["y"])
        for h, (a, b, k, l) in enumerate(((a0, b0, k0, l0), (a1, b1, k1, l1))):
            todo += [
                (a.at[384:512, :], gs.at[h, 0:128, 0:512]),
                (b.at[384:512, :], gs.at[h, 0:128, 512:1024]),
                (k, gs.at[h, 128:384, 0:512]),
                (l, gs.at[h, 128:384, 512:1024]),
            ]
        run_copies(todo, sems)
        for d, o in ((1, o1), (2, o2), (3, o3), (0, o0)):
            to = lax.rem(here["x"] + d, 4)
            lhs = gs[to // 2]
            for z in range(4):
                col = pl.multiple_of(z * 2 * BW + lax.rem(to, 2) * BW, BW)
                o[:, z * BW : (z + 1) * BW] = jnp.dot(
                    lhs, xs[:, pl.ds(col, BW)], preferred_element_type=F32
                ).astype(o.dtype)

    return call(
        body,
        [jax.ShapeDtypeStruct((384, 4 * BW), F32 if d == 0 else BF16) for d in range(4)],
        [
            pltpu.VMEM((1024, 8 * BW), BF16),
            pltpu.VMEM((2, 384, 1024), BF16),
            pltpu.SemaphoreType.DMA((16,)),
        ],
        3 * 10**9 // NJ,
        8 * 10**6 // NJ,
        [ANY] * 13,
        [VMEM] * 4,
    )(*gt, *kvt, *inputs)


def add_a(own, got):
    def body(o, r1, r2, r3, m0, m1, m2, m3, tot):
        x = place()["x"]
        tot[...] = o[...] + r1[...].astype(F32) + r2[...].astype(F32) + r3[...].astype(F32)
        for d, m in ((1, m1), (2, m2), (3, m3), (0, m0)):
            to = lax.rem(x + d, 4)
            m[...] = tot[
                pl.ds(mult(to // 2, 384), 384), pl.ds(mult(lax.rem(to, 2), BW), BW)
            ].astype(m.dtype)

    return call(
        body,
        [jax.ShapeDtypeStruct((384, BW), F32 if d == 0 else BF16) for d in range(4)],
        [pltpu.VMEM((768, 2 * BW), F32)],
        10**6,
        6 * 10**6 // NJ,
        [VMEM] * 4,
        [VMEM] * 4,
    )(own, *got)


def add_b(own, got):
    def body(o, r1, r2, r3, m0, m1, m2, m3, tot):
        z = place()["z"]
        tot[...] = o[...] + r1[...].astype(F32) + r2[...].astype(F32) + r3[...].astype(F32)
        for d, m in ((1, m1), (2, m2), (3, m3), (0, m0)):
            m[...] = tot[:, pl.ds(mult(lax.rem(z + d, 4), BW), BW)].astype(m.dtype)

    return call(
        body,
        [jax.ShapeDtypeStruct((384, BW), F32 if d == 0 else BF16) for d in range(4)],
        [pltpu.VMEM((384, 4 * BW), F32)],
        10**6,
        6 * 10**6 // NJ,
        [VMEM] * 4,
        [VMEM] * 4,
    )(own, *got)


def finish(parts):
    def body(*refs):
        ins, (qo, ko, vo) = refs[: 8 * NJ], refs[8 * NJ :]
        for j in range(NJ):
            a0, a1, a2, a3, b0, b1, b2, b3 = ins[j * 8 : (j + 1) * 8]
            rows = slice(j * BW, (j + 1) * BW)

            def total(r0, r1, r2, r3):
                t = r0[...] + r1[...].astype(F32) + r2[...].astype(F32) + r3[...].astype(F32)
                return (t * FACTOR).T

            a = total(a0, a1, a2, a3)
            b = total(b0, b1, b2, b3)
            qo[rows, 0:384] = a
            qo[rows, 384:512] = b[:, 0:128]
            ko[rows, :] = b[:, 128:256]
            vo[rows, :] = b[:, 256:384]

    return call(
        body,
        [
            jax.ShapeDtypeStruct((256, 512), F32),
            jax.ShapeDtypeStruct((256, 128), F32),
            jax.ShapeDtypeStruct((256, 128), F32),
        ],
        [],
        10**6,
        3 * 10**6,
        [VMEM] * (8 * NJ),
        [VMEM] * 3,
    )(*parts)


def per_device(hidden_in, queries, key_heads, saved_value_heads, out_grads, doc_ids):
    ids = jnp.broadcast_to(doc_ids.reshape(128, 1).astype(BF16), (128, 128))
    own, pieces, before = [], [], []
    for h in range(2):
        *msgs, kv = pack_heads(h, queries, key_heads, saved_value_heads, out_grads, ids)
        pieces.append([send(m, dy=d + 1) for d, m in enumerate(msgs)])
        own.append(kv)
    packed = pack_inputs(hidden_in)
    gathered = []
    for j in range(NJ):
        mine = jnp.concatenate([packed[j], send(packed[NJ + j], dc=1)], axis=0)
        r1 = send(mine, dy=1)
        r3 = send(mine, dy=-1)
        r2a = send(r1[0:128], dy=1)
        r2b = send(r3[128:256], dy=-1)
        gathered.append((mine, r1, r3, r2a, r2b))
    for h in range(2):
        kv = jnp.concatenate([own[h]] + [p[:, 1024:] for p in pieces[h]], axis=0)
        before.append(send(kv, dx=2, only_half=0))
    gt, kvt = [], []
    for h in range(2):
        dq, dkv, dprev = attention(
            h, queries, out_grads, own[h], pieces[h], before[h], own[0], pieces[0], before[0]
        )
        gt += [dq, send(dq, dc=1)]
        low = (dkv + send(dprev, dx=2, only_half=1).astype(F32)).astype(BF16)
        kvt += [low, send(low, dc=1)]
    parts = []
    for j in range(NJ):
        pa = weights_a(gt, gathered[j])
        got_a = [send(pa[d], dz=d) for d in (1, 2, 3)]
        pb = weights_b(gt, kvt, gathered[j])
        got_b = [send(pb[d], dx=d) for d in (1, 2, 3)]
        ma = add_a(pa[0], got_a)
        fa = [send(ma[d], dx=d) for d in (1, 2, 3)]
        mb = add_b(pb[0], got_b)
        fb = [send(mb[d], dz=d) for d in (1, 2, 3)]
        parts += [ma[0], *fa, mb[0], *fb]
    return finish(parts)


def solution(mesh):
    return jax.shard_map(
        per_device,
        mesh=mesh,
        in_specs=(
            P("grp", "sp", None),
            P("grp", "sp", None),
            P("grp", "sp", None),
            P("grp", "sp", None),
            P("grp", "sp", None),
            P("grp", "sp"),
        ),
        out_specs=(P("grp", "sp"), P("grp", "sp"), P("grp", "sp")),
        check_vma=False,
    )
```

profile of v0, /device:TPU:24, one launch (start us, length us, event | category | flops | bytes accessed | tf_op | source)
XLA Modules:
  0.0 180.0 jit_solution(15920864078721173788)
XLA Ops:
  0.6 0.7 convert_bitcast_fusion
  1.3 0.7 broadcast_in_dim.2.i
  2.0 2.5 %shard_map.85 = (bf16[128,1408]{1,0:T(8,128)(2,1)}, bf16[128,1408]{1,0:T(8,128)(2,1)}, bf16[128,1408]{1,0:T(8,128)(2,1)}, bf16[128,384]{1,0:T(8,128)(2,1)}) custom-call(bf16[1,128,4096]{2,1,0:T(8,128)(2,1)} %q.7, bf16[1,128,1024]{2,1,0:T(8,128)(2,1)} %k.3, bf16[1,128,1024]{2,1,0:T(8,128)(2,1)} %v.3, bf16[1,128,4096]{2,1,0:T(8,128)(2,1)} %g.7, ...), custom_call_target="tpu_custom_call" | custom-call | bytes 4000000 | tf_op jit(solution)/shard_map/pallas_call | solution.py:104
  4.5 0.2 collective-permute-start
  4.7 2.7 %collective-permute-start.1 = (bf16[128,1408]{1,0:T(8,128)(2,1)}, bf16[128,1408]{1,0:T(8,128)(2,1)S(1)}, u32[]{:S(2)}, u32[]{:S(2)}) collective-permute-start(bf16[128,1408]{1,0:T(8,128)(2,1)} %get-tuple-element.37), channel_id=1, source_target_pairs={{0,2},{8,10},{1,3},{9,11},{2,0},{10,8},{3,1},{11,9},{16,18},{24,26... | collective-permute-start | bytes 1081352 | tf_op jit(solution)/shard_map/ppermute | solution.py:53
  7.4 2.4 %shard_map.89 = (bf16[128,2048]{1,0:T(8,128)(2,1)}, bf16[128,2048]{1,0:T(8,128)(2,1)}) custom-call(bf16[1,128,4096]{2,1,0:T(8,128)(2,1)} %x.1), custom_call_target="tpu_custom_call" | custom-call | bytes 4000000 | tf_op jit(solution)/shard_map/pallas_call | solution.py:128
  9.7 0.0 copy-start.19
  9.8 0.0 copy-start.6
  9.8 0.1 collective-permute-start.10
  9.9 2.5 %shard_map.87 = (bf16[128,1280]{1,0:T(8,128)(2,1)}, bf16[128,1280]{1,0:T(8,128)(2,1)}, bf16[128,1280]{1,0:T(8,128)(2,1)}, bf16[128,256]{1,0:T(8,128)(2,1)}) custom-call(bf16[1,128,4096]{2,1,0:T(8,128)(2,1)} %q.7, bf16[1,128,1024]{2,1,0:T(8,128)(2,1)} %k.3, bf16[1,128,1024]{2,1,0:T(8,128)(2,1)} %v.3, bf16[1,128,4096]{2,1,0:T(8,128)(2,1)} %g.7, ...), custom_call_target="tpu_custom_call" | custom-call | bytes 4000000 | tf_op jit(solution)/shard_map/pallas_call | solution.py:104
  12.3 0.0 copy-start.20
  12.4 3.3 %collective-permute-start.5 = (bf16[128,1280]{1,0:T(8,128)(2,1)}, bf16[128,1280]{1,0:T(8,128)(2,1)S(1)}, u32[]{:S(2)}, u32[]{:S(2)}) collective-permute-start(bf16[128,1280]{1,0:T(8,128)(2,1)} %get-tuple-element.41), channel_id=1, source_target_pairs={{0,1},{8,9},{1,2},{9,10},{2,3},{10,11},{3,0},{11,8},{16,17},{24,25... | collective-permute-start | bytes 983048 | tf_op jit(solution)/shard_map/ppermute | solution.py:53
  15.7 0.4 collective-permute-done.p1.i1
  16.1 1.2 collective-permute-start.6
  17.3 0.4 collective-permute-done.1.p2.i2
  17.8 6.7 %collective-permute-start.7 = (bf16[128,1280]{1,0:T(8,128)(2,1)}, bf16[128,1280]{1,0:T(8,128)(2,1)S(1)}, u32[]{:S(2)}, u32[]{:S(2)}) collective-permute-start(bf16[128,1280]{1,0:T(8,128)(2,1)} %get-tuple-element.43), channel_id=1, source_target_pairs={{0,3},{8,11},{1,0},{9,8},{2,1},{10,9},{3,2},{11,10},{16,19},{24,27... | collective-permute-start | bytes 983048 | tf_op jit(solution)/shard_map/ppermute | solution.py:53
  24.5 0.9 collective-permute-done.2.p3.i3
  25.5 5.8 %collective-permute-start.3 = (bf16[512,384]{1,0:T(8,128)(2,1)S(1)}, bf16[512,384]{1,0:T(8,128)(2,1)}, u32[]{:S(2)}, u32[]{:S(2)}) collective-permute-start(bf16[512,384]{1,0:T(8,128)(2,1)S(1)} %pad_maximum_fusion), channel_id=1, source_target_pairs={{0,4},{8,12},{1,5},{9,13},{2,6},{10,14},{3,7},{11,15},{16,20},{24,... | collective-permute-start | bytes 1179656 | tf_op jit(solution)/shard_map/ppermute | solution.py:53
  31.3 0.0 copy-start.24
  31.3 1.2 collective-permute-done.6.p2
  32.6 5.7 %collective-permute-done.7.p3 = bf16[128,1280]{1,0:T(8,128)(2,1)S(1)} collective-permute-done((bf16[128,1280]{1,0:T(8,128)(2,1)}, bf16[128,1280]{1,0:T(8,128)(2,1)S(1)}, u32[]{:S(2)}, u32[]{:S(2)}) %collective-permute-start.7) | collective-permute-done | bytes 327712 | tf_op jit(solution)/shard_map/ppermute | solution.py:53
  38.4 4.9 %collective-permute-start.8 = (bf16[512,256]{1,0:T(8,128)(2,1)S(1)}, bf16[512,256]{1,0:T(8,128)(2,1)S(1)}, u32[]{:S(2)}, u32[]{:S(2)}) collective-permute-start(bf16[512,256]{1,0:T(8,128)(2,1)S(1)} %pad_maximum_fusion.1), channel_id=1, source_target_pairs={{0,4},{8,12},{1,5},{9,13},{2,6},{10,14},{3,7},{11,15},{16,20},{24,... | collective-permute-start | bytes 786440 | tf_op jit(solution)/shard_map/ppermute | solution.py:53
  43.4 1.2 collective-permute-start.11
  44.6 0.9 collective-permute-start.12
  45.5 3.5 %collective-permute-done.8.pv = bf16[512,256]{1,0:T(8,128)(2,1)S(1)} collective-permute-done((bf16[512,256]{1,0:T(8,128)(2,1)S(1)}, bf16[512,256]{1,0:T(8,128)(2,1)S(1)}, u32[]{:S(2)}, u32[]{:S(2)}) %collective-permute-start.8) | collective-permute-done | bytes 262176 | tf_op jit(solution)/shard_map/ppermute | solution.py:53
  49.0 0.7 copy-done.31
  49.7 11.7 %shard_map.88 = (bf16[512,512]{1,0:T(8,128)(2,1)}, f32[256,512]{1,0:T(8,128)}, bf16[256,512]{1,0:T(8,128)(2,1)}) custom-call(bf16[1,128,4096]{2,1,0:T(8,128)(2,1)} %q.7, bf16[1,128,4096]{2,1,0:T(8,128)(2,1)} %g.7, bf16[128,256]{1,0:T(8,128)(2,1)} %get-tuple-element.40.kv, bf16[128,1280]{1,0:T(8,128)(2,1)} %copy-done.24, bf16[128,1280]{1,0:T(8,128)(2,1)} %copy-done.25, ...), custom_call_target="tpu_custom_call" | custom-call | flops 4000000000 | bytes 4000000 | tf_op jit(solution)/shard_map/pallas_call | solution.py:221
  61.5 1.4 collective-permute-start.23
  62.9 11.8 %shard_map.86 = (bf16[512,512]{1,0:T(8,128)(2,1)}, f32[256,512]{1,0:T(8,128)}, bf16[256,512]{1,0:T(8,128)(2,1)}) custom-call(bf16[1,128,4096]{2,1,0:T(8,128)(2,1)} %q.7, bf16[1,128,4096]{2,1,0:T(8,128)(2,1)} %g.7, bf16[128,384]{1,0:T(8,128)(2,1)} %get-tuple-element.35.kv.kv0, bf16[128,1408]{1,0:T(8,128)(2,1)} %copy-done.21, bf16[128,1408]{1,0:T(8,128)(2,1)} %copy-done.22, ...), custom_call_target="tpu_custom_call" | custom-call | flops 4000000000 | bytes 4000000 | tf_op jit(solution)/shard_map/pallas_call | solution.py:221
  74.7 1.3 collective-permute-start.21
  76.0 0.1 collective-permute-start.9
  76.1 0.5 collective-permute-start.4
  76.6 0.1 add_convert_fusion.k1
  76.7 0.2 collective-permute-start.24
  76.9 0.2 collective-permute-start.13
  77.2 8.6 %collective-permute-done.21 = bf16[256,512]{1,0:T(8,128)(2,1)S(1)} collective-permute-done((bf16[256,512]{1,0:T(8,128)(2,1)}, bf16[256,512]{1,0:T(8,128)(2,1)S(1)}, u32[]{:S(2)}, u32[]{:S(2)}) %collective-permute-start.21) | collective-permute-done | bytes 262176 | tf_op jit(solution)/shard_map/ppermute | solution.py:53
  85.8 0.1 add_convert_fusion.1.k0
  85.9 0.3 collective-permute-start.22
  86.2 1.5 collective-permute-done.22.l0
  87.7 3.5 %collective-permute-done.13.i3 = bf16[128,2048]{1,0:T(8,128)(2,1)S(1)} collective-permute-done((bf16[128,2048]{1,0:T(8,128)(2,1)S(1)}, bf16[128,2048]{1,0:T(8,128)(2,1)S(1)}, u32[]{:S(2)}, u32[]{:S(2)}) %collective-permute-start.13) | collective-permute-done | bytes 524320 | tf_op jit(solution)/shard_map/ppermute | solution.py:53
  91.2 8.0 %collective-permute-done.14.i4 = bf16[128,2048]{1,0:T(8,128)(2,1)} collective-permute-done((bf16[128,2048]{1,0:T(8,128)(2,1)S(1)}, bf16[128,2048]{1,0:T(8,128)(2,1)}, u32[]{:S(2)}, u32[]{:S(2)}) %collective-permute-start.14) | collective-permute-done | bytes 524320 | tf_op jit(solution)/shard_map/ppermute | solution.py:53
  99.2 7.4 %shard_map.92 = (f32[384,1024]{1,0:T(8,128)}, bf16[384,1024]{1,0:T(8,128)(2,1)}, bf16[384,1024]{1,0:T(8,128)(2,1)}, bf16[384,1024]{1,0:T(8,128)(2,1)}) custom-call(bf16[512,512]{1,0:T(8,128)(2,1)} %get-tuple-element.39.a0, bf16[512,512]{1,0:T(8,128)(2,1)} %copy-done.28, bf16[512,512]{1,0:T(8,128)(2,1)} %get-tuple-element.44.a1, bf16[512,512]{1,0:T(8,128)(2,1)} %copy-done.27, ...), custom_call_target="tpu_custom_call" | custom-call | flops 3000000000 | bytes 8000000 | tf_op jit(solution)/shard_map/pallas_call | solution.py:310
  106.7 1.0 collective-permute-start.25
  107.7 0.3 collective-permute-start.26
  107.9 2.5 %collective-permute-start.27 = (bf16[384,1024]{1,0:T(8,128)(2,1)}, bf16[384,1024]{1,0:T(8,128)(2,1)}, u32[]{:S(2)}, u32[]{:S(2)}) collective-permute-start(bf16[384,1024]{1,0:T(8,128)(2,1)} %get-tuple-element.62), channel_id=1, source_target_pairs={{0,20},{8,28},{1,21},{9,29},{2,22},{10,30},{3,23},{11,31},{16,0},{... | collective-permute-start | bytes 2359304 | tf_op jit(solution)/shard_map/ppermute | solution.py:53
  110.4 7.3 %shard_map.90 = (f32[768,512]{1,0:T(8,128)}, bf16[768,512]{1,0:T(8,128)(2,1)}, bf16[768,512]{1,0:T(8,128)(2,1)}, bf16[768,512]{1,0:T(8,128)(2,1)}) custom-call(bf16[512,512]{1,0:T(8,128)(2,1)} %get-tuple-element.39.a0, bf16[512,512]{1,0:T(8,128)(2,1)} %copy-done.28, bf16[512,512]{1,0:T(8,128)(2,1)} %get-tuple-element.44.a1, bf16[512,512]{1,0:T(8,128)(2,1)} %copy-done.27, ...), custom_call_target="tpu_custom_call" | custom-call | flops 3000000000 | bytes 8000000 | tf_op jit(solution)/shard_map/pallas_call | solution.py:274
  117.8 2.0 %collective-permute-start.15 = (bf16[768,512]{1,0:T(8,128)(2,1)}, bf16[768,512]{1,0:T(8,128)(2,1)S(1)}, u32[]{:S(2)}, u32[]{:S(2)}) collective-permute-start(bf16[768,512]{1,0:T(8,128)(2,1)} %get-tuple-element.48), channel_id=1, source_target_pairs={{0,32},{8,40},{1,33},{9,41},{2,34},{10,42},{3,35},{11,43},{16,48},... | collective-permute-start | bytes 2359304 | tf_op jit(solution)/shard_map/ppermute | solution.py:53
  119.8 3.6 %collective-permute-start.16 = (bf16[768,512]{1,0:T(8,128)(2,1)}, bf16[768,512]{1,0:T(8,128)(2,1)S(1)}, u32[]{:S(2)}, u32[]{:S(2)}) collective-permute-start(bf16[768,512]{1,0:T(8,128)(2,1)} %get-tuple-element.49), channel_id=1, source_target_pairs={{0,64},{8,72},{1,65},{9,73},{2,66},{10,74},{3,67},{11,75},{16,80},... | collective-permute-start | bytes 2359304 | tf_op jit(solution)/shard_map/ppermute | solution.py:53
  123.3 18.5 %collective-permute-done.25.r1 = bf16[384,1024]{1,0:T(8,128)(2,1)S(1)} collective-permute-done((bf16[384,1024]{1,0:T(8,128)(2,1)}, bf16[384,1024]{1,0:T(8,128)(2,1)S(1)}, u32[]{:S(2)}, u32[]{:S(2)}) %collective-permute-start.25) | collective-permute-done | bytes 786464 | tf_op jit(solution)/shard_map/ppermute | solution.py:53
  141.9 4.0 %collective-permute-start.17 = (bf16[768,512]{1,0:T(8,128)(2,1)}, bf16[768,512]{1,0:T(8,128)(2,1)S(1)}, u32[]{:S(2)}, u32[]{:S(2)}) collective-permute-start(bf16[768,512]{1,0:T(8,128)(2,1)} %get-tuple-element.50), channel_id=1, source_target_pairs={{0,96},{8,104},{1,97},{9,105},{2,98},{10,106},{3,99},{11,107},{16,... | collective-permute-start | bytes 2359304 | tf_op jit(solution)/shard_map/ppermute | solution.py:53
  145.9 0.9 copy-done.4
  146.8 3.6 %shard_map.93 = (f32[384,256]{1,0:T(8,128)}, bf16[384,256]{1,0:T(8,128)(2,1)}, bf16[384,256]{1,0:T(8,128)(2,1)}, bf16[384,256]{1,0:T(8,128)(2,1)}) custom-call(f32[384,1024]{1,0:T(8,128)} %get-tuple-element.59.o, bf16[384,1024]{1,0:T(8,128)(2,1)} %copy-done.2, bf16[384,1024]{1,0:T(8,128)(2,1)} %copy-done.4, bf16[384,1024]{1,0:T(8,128)(2,1)} %collective-permute-done.27.r3), custom_call_target="tpu_custom_call" | custom-call | flops 1000000 | bytes 6000000 | tf_op jit(solution)/shard_map/pallas_call | solution.py:353
  150.4 1.9 %collective-permute-start.29 = (bf16[384,256]{1,0:T(8,128)(2,1)}, bf16[384,256]{1,0:T(8,128)(2,1)S(1)}, u32[]{:S(2)}, u32[]{:S(2)}) collective-permute-start(bf16[384,256]{1,0:T(8,128)(2,1)} %get-tuple-element.65), channel_id=1, source_target_pairs={{0,64},{8,72},{1,65},{9,73},{2,66},{10,74},{3,67},{11,75},{16,80},... | collective-permute-start | bytes 589832 | tf_op jit(solution)/shard_map/ppermute | solution.py:53
  152.3 1.4 collective-permute-start.30
  153.7 4.4 %collective-permute-done.16.r2 = bf16[768,512]{1,0:T(8,128)(2,1)S(1)} collective-permute-done((bf16[768,512]{1,0:T(8,128)(2,1)}, bf16[768,512]{1,0:T(8,128)(2,1)S(1)}, u32[]{:S(2)}, u32[]{:S(2)}) %collective-permute-start.16) | collective-permute-done | bytes 786464 | tf_op jit(solution)/shard_map/ppermute | solution.py:53
  158.1 3.9 %collective-permute-done.17.r3 = bf16[768,512]{1,0:T(8,128)(2,1)S(1)} collective-permute-done((bf16[768,512]{1,0:T(8,128)(2,1)}, bf16[768,512]{1,0:T(8,128)(2,1)S(1)}, u32[]{:S(2)}, u32[]{:S(2)}) %collective-permute-start.17) | collective-permute-done | bytes 786464 | tf_op jit(solution)/shard_map/ppermute | solution.py:53
  162.0 0.9 copy-done.3
  162.9 3.6 %shard_map.91 = (f32[384,256]{1,0:T(8,128)}, bf16[384,256]{1,0:T(8,128)(2,1)}, bf16[384,256]{1,0:T(8,128)(2,1)}, bf16[384,256]{1,0:T(8,128)(2,1)}) custom-call(f32[768,512]{1,0:T(8,128)} %get-tuple-element.47.o, bf16[768,512]{1,0:T(8,128)(2,1)} %copy-done, bf16[768,512]{1,0:T(8,128)(2,1)} %copy-done.1, bf16[768,512]{1,0:T(8,128)(2,1)} %copy-done.3), custom_call_target="tpu_custom_call" | custom-call | flops 1000000 | bytes 6000000 | tf_op jit(solution)/shard_map/pallas_call | solution.py:335
  166.5 0.1 collective-permute-start.19
  166.6 3.2 %collective-permute-start.20 = (bf16[384,256]{1,0:T(8,128)(2,1)}, bf16[384,256]{1,0:T(8,128)(2,1)S(1)}, u32[]{:S(2)}, u32[]{:S(2)}) collective-permute-start(bf16[384,256]{1,0:T(8,128)(2,1)} %get-tuple-element.54), channel_id=1, source_target_pairs={{0,20},{8,28},{1,21},{9,29},{2,22},{10,30},{3,23},{11,31},{16,0},{... | collective-permute-start | bytes 589832 | tf_op jit(solution)/shard_map/ppermute | solution.py:53
  169.9 5.9 %collective-permute-done.18.refs_1_ = bf16[384,256]{1,0:T(8,128)(2,1)S(1)} collective-permute-done((bf16[384,256]{1,0:T(8,128)(2,1)}, bf16[384,256]{1,0:T(8,128)(2,1)S(1)}, u32[]{:S(2)}, u32[]{:S(2)}) %collective-permute-start.18) | collective-permute-done | bytes 196640 | tf_op jit(solution)/shard_map/ppermute | solution.py:53
  175.7 0.9 collective-permute-done.20.refs_3_
  176.7 0.7 copy-done.18
  177.3 2.7 %shard_map.94 = (f32[256,512]{1,0:T(8,128)}, f32[256,128]{1,0:T(8,128)}, f32[256,128]{1,0:T(8,128)}) custom-call(f32[384,256]{1,0:T(8,128)} %get-tuple-element.51.refs_0_, bf16[384,256]{1,0:T(8,128)(2,1)} %copy-done.16, bf16[384,256]{1,0:T(8,128)(2,1)} %copy-done.17, bf16[384,256]{1,0:T(8,128)(2,1)} %copy-done.18, f32[384,256]{1,0:T(8,128)} %get-tuple-element.63.refs_4_, ...), custom_call_target="tpu_custom_call" | custom-call | flops 1000000 | bytes 3000000 | tf_op jit(solution)/shard_map/pallas_call | solution.py:382
  (90 shorter events, 0.4 us)
Async XLA Ops:
  4.5 11.6 %collective-permute-start = (bf16[128,1408]{1,0:T(8,128)(2,1)}, bf16[128,1408]{1,0:T(8,128)(2,1)S(1)}, u32[]{:S(2)}, u32[]{:S(2)}) collective-permute-start(bf16[128,1408]{1,0:T(8,128)(2,1)} %get-tuple-element.36), channel_id=1, source_target_pairs={{0,1},{8,9},{1,2},{9,10},{2,3},{10,11},{3,0},{11,8},{16,17},{24,25... | collective-permute-start | bytes 1081352 | tf_op jit(solution)/shard_map/ppermute | solution.py:53
  4.7 13.1 %collective-permute-start.1 = (bf16[128,1408]{1,0:T(8,128)(2,1)}, bf16[128,1408]{1,0:T(8,128)(2,1)S(1)}, u32[]{:S(2)}, u32[]{:S(2)}) collective-permute-start(bf16[128,1408]{1,0:T(8,128)(2,1)} %get-tuple-element.37), channel_id=1, source_target_pairs={{0,2},{8,10},{1,3},{9,11},{2,0},{10,8},{3,1},{11,9},{16,18},{24,26... | collective-permute-start | bytes 1081352 | tf_op jit(solution)/shard_map/ppermute | solution.py:53
  7.4 18.0 %collective-permute-start.2 = (bf16[128,1408]{1,0:T(8,128)(2,1)}, bf16[128,1408]{1,0:T(8,128)(2,1)S(1)}, u32[]{:S(2)}, u32[]{:S(2)}) collective-permute-start(bf16[128,1408]{1,0:T(8,128)(2,1)} %get-tuple-element.38), channel_id=1, source_target_pairs={{0,3},{8,11},{1,0},{9,8},{2,1},{10,9},{3,2},{11,10},{16,19},{24,27... | collective-permute-start | bytes 1081352 | tf_op jit(solution)/shard_map/ppermute | solution.py:53
  9.7 15.7 %copy-start.19 = (bf16[128,384]{1,0:T(8,128)(2,1)S(1)}, bf16[128,384]{1,0:T(8,128)(2,1)}, u32[]{:S(2)}) copy-start(bf16[128,384]{1,0:T(8,128)(2,1)} %get-tuple-element.35.kv.kv0) | copy-start | bytes 294916
  9.8 21.5 %copy-start.6 = (bf16[128,2048]{1,0:T(8,128)(2,1)S(1)}, bf16[128,2048]{1,0:T(8,128)(2,1)}, u32[]{:S(2)}) copy-start(bf16[128,2048]{1,0:T(8,128)(2,1)} %get-tuple-element.45) | copy-start | bytes 1572868
  9.8 33.5 %collective-permute-start.10 = (bf16[128,2048]{1,0:T(8,128)(2,1)}, bf16[128,2048]{1,0:T(8,128)(2,1)S(1)}, u32[]{:S(2)}, u32[]{:S(2)}) collective-permute-start(bf16[128,2048]{1,0:T(8,128)(2,1)} %get-tuple-element.46), channel_id=1, source_target_pairs={{0,8},{8,0},{1,9},{9,1},{2,10},{10,2},{3,11},{11,3},{16,24},{24,16... | collective-permute-start | bytes 1572872 | tf_op jit(solution)/shard_map/ppermute | solution.py:53
  12.3 25.9 %copy-start.20 = (bf16[128,256]{1,0:T(8,128)(2,1)S(1)}, bf16[128,256]{1,0:T(8,128)(2,1)}, u32[]{:S(2)}) copy-start(bf16[128,256]{1,0:T(8,128)(2,1)} %get-tuple-element.40.kv) | copy-start | bytes 196612
  12.4 19.0 %collective-permute-start.5 = (bf16[128,1280]{1,0:T(8,128)(2,1)}, bf16[128,1280]{1,0:T(8,128)(2,1)S(1)}, u32[]{:S(2)}, u32[]{:S(2)}) collective-permute-start(bf16[128,1280]{1,0:T(8,128)(2,1)} %get-tuple-element.41), channel_id=1, source_target_pairs={{0,1},{8,9},{1,2},{9,10},{2,3},{10,11},{3,0},{11,8},{16,17},{24,25... | collective-permute-start | bytes 983048 | tf_op jit(solution)/shard_map/ppermute | solution.py:53
  16.1 22.3 %copy-start.21 = (bf16[128,1408]{1,0:T(8,128)(2,1)}, bf16[128,1408]{1,0:T(8,128)(2,1)S(1)}, u32[]{:S(2)}) copy-start(bf16[128,1408]{1,0:T(8,128)(2,1)S(1)} %collective-permute-done.p1.i1) | copy-start | bytes 1081348
  16.1 16.5 %collective-permute-start.6 = (bf16[128,1280]{1,0:T(8,128)(2,1)}, bf16[128,1280]{1,0:T(8,128)(2,1)S(1)}, u32[]{:S(2)}, u32[]{:S(2)}) collective-permute-start(bf16[128,1280]{1,0:T(8,128)(2,1)} %get-tuple-element.42), channel_id=1, source_target_pairs={{0,2},{8,10},{1,3},{9,11},{2,0},{10,8},{3,1},{11,9},{16,18},{24,26... | collective-permute-start | bytes 983048 | tf_op jit(solution)/shard_map/ppermute | solution.py:53
  17.8 20.6 %copy-start.22 = (bf16[128,1408]{1,0:T(8,128)(2,1)}, bf16[128,1408]{1,0:T(8,128)(2,1)S(1)}, u32[]{:S(2)}) copy-start(bf16[128,1408]{1,0:T(8,128)(2,1)S(1)} %collective-permute-done.1.p2.i2) | copy-start | bytes 1081348
  17.8 20.5 %collective-permute-start.7 = (bf16[128,1280]{1,0:T(8,128)(2,1)}, bf16[128,1280]{1,0:T(8,128)(2,1)S(1)}, u32[]{:S(2)}, u32[]{:S(2)}) collective-permute-start(bf16[128,1280]{1,0:T(8,128)(2,1)} %get-tuple-element.43), channel_id=1, source_target_pairs={{0,3},{8,11},{1,0},{9,8},{2,1},{10,9},{3,2},{11,10},{16,19},{24,27... | collective-permute-start | bytes 983048 | tf_op jit(solution)/shard_map/ppermute | solution.py:53
  25.4 5.9 %copy-start.23 = (bf16[128,1408]{1,0:T(8,128)(2,1)}, bf16[128,1408]{1,0:T(8,128)(2,1)S(1)}, u32[]{:S(2)}) copy-start(bf16[128,1408]{1,0:T(8,128)(2,1)S(1)} %collective-permute-done.2.p3.i3) | copy-start | bytes 1081348
  25.5 24.2 %collective-permute-start.3 = (bf16[512,384]{1,0:T(8,128)(2,1)S(1)}, bf16[512,384]{1,0:T(8,128)(2,1)}, u32[]{:S(2)}, u32[]{:S(2)}) collective-permute-start(bf16[512,384]{1,0:T(8,128)(2,1)S(1)} %pad_maximum_fusion), channel_id=1, source_target_pairs={{0,4},{8,12},{1,5},{9,13},{2,6},{10,14},{3,7},{11,15},{16,20},{24,... | collective-permute-start | bytes 1179656 | tf_op jit(solution)/shard_map/ppermute | solution.py:53
  31.3 12.0 %copy-start.24 = (bf16[128,1280]{1,0:T(8,128)(2,1)}, bf16[128,1280]{1,0:T(8,128)(2,1)S(1)}, u32[]{:S(2)}) copy-start(bf16[128,1280]{1,0:T(8,128)(2,1)S(1)} %collective-permute-done.5.p1) | copy-start | bytes 983044
  32.5 10.8 %copy-start.25 = (bf16[128,1280]{1,0:T(8,128)(2,1)}, bf16[128,1280]{1,0:T(8,128)(2,1)S(1)}, u32[]{:S(2)}) copy-start(bf16[128,1280]{1,0:T(8,128)(2,1)S(1)} %collective-permute-done.6.p2) | copy-start | bytes 983044
  38.3 5.1 %copy-start.26 = (bf16[128,1280]{1,0:T(8,128)(2,1)}, bf16[128,1280]{1,0:T(8,128)(2,1)S(1)}, u32[]{:S(2)}) copy-start(bf16[128,1280]{1,0:T(8,128)(2,1)S(1)} %collective-permute-done.7.p3) | copy-start | bytes 983044
  38.4 10.6 %collective-permute-start.8 = (bf16[512,256]{1,0:T(8,128)(2,1)S(1)}, bf16[512,256]{1,0:T(8,128)(2,1)S(1)}, u32[]{:S(2)}, u32[]{:S(2)}) collective-permute-start(bf16[512,256]{1,0:T(8,128)(2,1)S(1)} %pad_maximum_fusion.1), channel_id=1, source_target_pairs={{0,4},{8,12},{1,5},{9,13},{2,6},{10,14},{3,7},{11,15},{16,20},{24,... | collective-permute-start | bytes 786440 | tf_op jit(solution)/shard_map/ppermute | solution.py:53
  43.4 18.0 %copy-start.10 = (bf16[256,2048]{1,0:T(8,128)(2,1)}, bf16[256,2048]{1,0:T(8,128)(2,1)S(1)}, u32[]{:S(2)}) copy-start(bf16[256,2048]{1,0:T(8,128)(2,1)S(1)} %constant_dynamic-update-slice_fusion.i0) | copy-start | bytes 3145732
  43.4 33.3 %collective-permute-start.11 = (bf16[256,2048]{1,0:T(8,128)(2,1)S(1)}, bf16[256,2048]{1,0:T(8,128)(2,1)S(1)}, u32[]{:S(2)}, u32[]{:S(2)}) collective-permute-start(bf16[256,2048]{1,0:T(8,128)(2,1)S(1)} %constant_dynamic-update-slice_fusion.i0), channel_id=1, source_target_pairs={{0,1},{8,9},{1,2},{9,10},{2,3},{10,11},{3,0},{11,8},{16,17},{24,25... | collective-permute-start | bytes 3145736 | tf_op jit(solution)/shard_map/ppermute | solution.py:53
  44.6 32.3 %collective-permute-start.12 = (bf16[256,2048]{1,0:T(8,128)(2,1)S(1)}, bf16[256,2048]{1,0:T(8,128)(2,1)S(1)}, u32[]{:S(2)}, u32[]{:S(2)}) collective-permute-start(bf16[256,2048]{1,0:T(8,128)(2,1)S(1)} %constant_dynamic-update-slice_fusion.i0), channel_id=1, source_target_pairs={{0,3},{8,11},{1,0},{9,8},{2,1},{10,9},{3,2},{11,10},{16,19},{24,27... | collective-permute-start | bytes 3145736 | tf_op jit(solution)/shard_map/ppermute | solution.py:53
  49.0 0.7 copy-start.31
  61.4 15.1 %copy-start.7 = (f32[256,512]{1,0:T(8,128)S(1)}, f32[256,512]{1,0:T(8,128)}, u32[]{:S(2)}) copy-start(f32[256,512]{1,0:T(8,128)} %get-tuple-element.57) | copy-start | bytes 1572868
  61.5 14.6 %collective-permute-start.23 = (bf16[256,512]{1,0:T(8,128)(2,1)}, bf16[256,512]{1,0:T(8,128)(2,1)S(1)}, u32[]{:S(2)}, u32[]{:S(2)}) collective-permute-start(bf16[256,512]{1,0:T(8,128)(2,1)} %get-tuple-element.58), channel_id=1, source_target_pairs={{4,0},{12,8},{5,1},{13,9},{6,2},{14,10},{7,3},{15,11},{20,16},{28,... | collective-permute-start | bytes 786440 | tf_op jit(solution)/shard_map/ppermute | solution.py:53
  74.7 11.1 %collective-permute-start.21 = (bf16[256,512]{1,0:T(8,128)(2,1)}, bf16[256,512]{1,0:T(8,128)(2,1)S(1)}, u32[]{:S(2)}, u32[]{:S(2)}) collective-permute-start(bf16[256,512]{1,0:T(8,128)(2,1)} %get-tuple-element.56), channel_id=1, source_target_pairs={{4,0},{12,8},{5,1},{13,9},{6,2},{14,10},{7,3},{15,11},{20,16},{28,... | collective-permute-start | bytes 786440 | tf_op jit(solution)/shard_map/ppermute | solution.py:53
  76.0 11.7 %collective-permute-start.9 = (bf16[512,512]{1,0:T(8,128)(2,1)}, bf16[512,512]{1,0:T(8,128)(2,1)S(1)}, u32[]{:S(2)}, u32[]{:S(2)}) collective-permute-start(bf16[512,512]{1,0:T(8,128)(2,1)} %get-tuple-element.44.a1), channel_id=1, source_target_pairs={{0,8},{8,0},{1,9},{9,1},{2,10},{10,2},{3,11},{11,3},{16,24},{24,16... | collective-permute-start | bytes 1572872 | tf_op jit(solution)/shard_map/ppermute | solution.py:53
  76.1 11.6 %collective-permute-start.4 = (bf16[512,512]{1,0:T(8,128)(2,1)}, bf16[512,512]{1,0:T(8,128)(2,1)S(1)}, u32[]{:S(2)}, u32[]{:S(2)}) collective-permute-start(bf16[512,512]{1,0:T(8,128)(2,1)} %get-tuple-element.39.a0), channel_id=1, source_target_pairs={{0,8},{8,0},{1,9},{9,1},{2,10},{10,2},{3,11},{11,3},{16,24},{24,16... | collective-permute-start | bytes 1572872 | tf_op jit(solution)/shard_map/ppermute | solution.py:53
  76.6 9.2 %copy-start.5 = (f32[256,512]{1,0:T(8,128)S(1)}, f32[256,512]{1,0:T(8,128)}, u32[]{:S(2)}) copy-start(f32[256,512]{1,0:T(8,128)} %get-tuple-element.55) | copy-start | bytes 1572868
  76.6 9.2 %copy-start.11 = (bf16[256,512]{1,0:T(8,128)(2,1)}, bf16[256,512]{1,0:T(8,128)(2,1)S(1)}, u32[]{:S(2)}) copy-start(bf16[256,512]{1,0:T(8,128)(2,1)S(1)} %add_convert_fusion.k1) | copy-start | bytes 786436
  76.7 9.2 %copy-start.8 = (bf16[256,2048]{1,0:T(8,128)(2,1)}, bf16[256,2048]{1,0:T(8,128)(2,1)S(1)}, u32[]{:S(2)}) copy-start(bf16[256,2048]{1,0:T(8,128)(2,1)S(1)} %collective-permute-done.11.i1) | copy-start | bytes 3145732
  76.7 9.2 %collective-permute-start.24 = (bf16[256,512]{1,0:T(8,128)(2,1)S(1)}, bf16[256,512]{1,0:T(8,128)(2,1)S(1)}, u32[]{:S(2)}, u32[]{:S(2)}) collective-permute-start(bf16[256,512]{1,0:T(8,128)(2,1)S(1)} %add_convert_fusion.k1), channel_id=1, source_target_pairs={{0,8},{8,0},{1,9},{9,1},{2,10},{10,2},{3,11},{11,3},{16,24},{24,16... | collective-permute-start | bytes 786440 | tf_op jit(solution)/shard_map/ppermute | solution.py:53
  76.9 22.3 %copy-start.9 = (bf16[256,2048]{1,0:T(8,128)(2,1)}, bf16[256,2048]{1,0:T(8,128)(2,1)S(1)}, u32[]{:S(2)}) copy-start(bf16[256,2048]{1,0:T(8,128)(2,1)S(1)} %collective-permute-done.12.i2) | copy-start | bytes 3145732
  76.9 14.3 %collective-permute-start.13 = (bf16[128,2048]{1,0:T(8,128)(2,1)S(1)}, bf16[128,2048]{1,0:T(8,128)(2,1)S(1)}, u32[]{:S(2)}, u32[]{:S(2)}) collective-permute-start(bf16[128,2048]{1,0:T(8,128)(2,1)S(1)} %slice.38), channel_id=1, source_target_pairs={{0,1},{8,9},{1,2},{9,10},{2,3},{10,11},{3,0},{11,8},{16,17},{24,25... | collective-permute-start | bytes 1572872 | tf_op jit(solution)/shard_map/ppermute | solution.py:53
  85.7 13.5 %collective-permute-start.14 = (bf16[128,2048]{1,0:T(8,128)(2,1)S(1)}, bf16[128,2048]{1,0:T(8,128)(2,1)}, u32[]{:S(2)}, u32[]{:S(2)}) collective-permute-start(bf16[128,2048]{1,0:T(8,128)(2,1)S(1)} %slice.39), channel_id=1, source_target_pairs={{0,3},{8,11},{1,0},{9,8},{2,1},{10,9},{3,2},{11,10},{16,19},{24,27... | collective-permute-start | bytes 1572872 | tf_op jit(solution)/shard_map/ppermute | solution.py:53
  85.9 13.4 %copy-start.12 = (bf16[256,512]{1,0:T(8,128)(2,1)}, bf16[256,512]{1,0:T(8,128)(2,1)S(1)}, u32[]{:S(2)}) copy-start(bf16[256,512]{1,0:T(8,128)(2,1)S(1)} %add_convert_fusion.1.k0) | copy-start | bytes 786436
  85.9 13.4 %copy-start.30 = (bf16[256,512]{1,0:T(8,128)(2,1)}, bf16[256,512]{1,0:T(8,128)(2,1)S(1)}, u32[]{:S(2)}) copy-start(bf16[256,512]{1,0:T(8,128)(2,1)S(1)} %collective-permute-done.24.l1) | copy-start | bytes 786436
  85.9 1.8 collective-permute-start.22
  87.7 11.6 %copy-start.32 = (bf16[256,512]{1,0:T(8,128)(2,1)}, bf16[256,512]{1,0:T(8,128)(2,1)S(1)}, u32[]{:S(2)}) copy-start(bf16[256,512]{1,0:T(8,128)(2,1)S(1)} %collective-permute-done.22.l0) | copy-start | bytes 786436
  87.7 3.6 %copy-start.27 = (bf16[512,512]{1,0:T(8,128)(2,1)}, bf16[512,512]{1,0:T(8,128)(2,1)S(1)}, u32[]{:S(2)}) copy-start(bf16[512,512]{1,0:T(8,128)(2,1)S(1)} %collective-permute-done.9.b1) | copy-start | bytes 1572868
  87.7 3.6 %copy-start.28 = (bf16[512,512]{1,0:T(8,128)(2,1)}, bf16[512,512]{1,0:T(8,128)(2,1)S(1)}, u32[]{:S(2)}) copy-start(bf16[512,512]{1,0:T(8,128)(2,1)S(1)} %collective-permute-done.4.b0) | copy-start | bytes 1572868
  91.2 8.0 %copy-start.29 = (bf16[128,2048]{1,0:T(8,128)(2,1)}, bf16[128,2048]{1,0:T(8,128)(2,1)S(1)}, u32[]{:S(2)}) copy-start(bf16[128,2048]{1,0:T(8,128)(2,1)S(1)} %collective-permute-done.13.i3) | copy-start | bytes 1572868
  106.7 35.2 %collective-permute-start.25 = (bf16[384,1024]{1,0:T(8,128)(2,1)}, bf16[384,1024]{1,0:T(8,128)(2,1)S(1)}, u32[]{:S(2)}, u32[]{:S(2)}) collective-permute-start(bf16[384,1024]{1,0:T(8,128)(2,1)} %get-tuple-element.60), channel_id=1, source_target_pairs={{0,16},{8,24},{1,17},{9,25},{2,18},{10,26},{3,19},{11,27},{16,4},{... | collective-permute-start | bytes 2359304 | tf_op jit(solution)/shard_map/ppermute | solution.py:53
  107.7 38.2 %collective-permute-start.26 = (bf16[384,1024]{1,0:T(8,128)(2,1)}, bf16[384,1024]{1,0:T(8,128)(2,1)S(1)}, u32[]{:S(2)}, u32[]{:S(2)}) collective-permute-start(bf16[384,1024]{1,0:T(8,128)(2,1)} %get-tuple-element.61), channel_id=1, source_target_pairs={{0,4},{8,12},{1,5},{9,13},{2,6},{10,14},{3,7},{11,15},{16,20},{24,... | collective-permute-start | bytes 2359304 | tf_op jit(solution)/shard_map/ppermute | solution.py:53
  107.9 37.9 %collective-permute-start.27 = (bf16[384,1024]{1,0:T(8,128)(2,1)}, bf16[384,1024]{1,0:T(8,128)(2,1)}, u32[]{:S(2)}, u32[]{:S(2)}) collective-permute-start(bf16[384,1024]{1,0:T(8,128)(2,1)} %get-tuple-element.62), channel_id=1, source_target_pairs={{0,20},{8,28},{1,21},{9,29},{2,22},{10,30},{3,23},{11,31},{16,0},{... | collective-permute-start | bytes 2359304 | tf_op jit(solution)/shard_map/ppermute | solution.py:53
  117.8 34.5 %collective-permute-start.15 = (bf16[768,512]{1,0:T(8,128)(2,1)}, bf16[768,512]{1,0:T(8,128)(2,1)S(1)}, u32[]{:S(2)}, u32[]{:S(2)}) collective-permute-start(bf16[768,512]{1,0:T(8,128)(2,1)} %get-tuple-element.48), channel_id=1, source_target_pairs={{0,32},{8,40},{1,33},{9,41},{2,34},{10,42},{3,35},{11,43},{16,48},... | collective-permute-start | bytes 2359304 | tf_op jit(solution)/shard_map/ppermute | solution.py:53
  119.8 38.4 %collective-permute-start.16 = (bf16[768,512]{1,0:T(8,128)(2,1)}, bf16[768,512]{1,0:T(8,128)(2,1)S(1)}, u32[]{:S(2)}, u32[]{:S(2)}) collective-permute-start(bf16[768,512]{1,0:T(8,128)(2,1)} %get-tuple-element.49), channel_id=1, source_target_pairs={{0,64},{8,72},{1,65},{9,73},{2,66},{10,74},{3,67},{11,75},{16,80},... | collective-permute-start | bytes 2359304 | tf_op jit(solution)/shard_map/ppermute | solution.py:53
  141.9 4.0 %copy-start.2 = (bf16[384,1024]{1,0:T(8,128)(2,1)}, bf16[384,1024]{1,0:T(8,128)(2,1)S(1)}, u32[]{:S(2)}) copy-start(bf16[384,1024]{1,0:T(8,128)(2,1)S(1)} %collective-permute-done.25.r1) | copy-start | bytes 2359300
  141.9 20.2 %collective-permute-start.17 = (bf16[768,512]{1,0:T(8,128)(2,1)}, bf16[768,512]{1,0:T(8,128)(2,1)S(1)}, u32[]{:S(2)}, u32[]{:S(2)}) collective-permute-start(bf16[768,512]{1,0:T(8,128)(2,1)} %get-tuple-element.50), channel_id=1, source_target_pairs={{0,96},{8,104},{1,97},{9,105},{2,98},{10,106},{3,99},{11,107},{16,... | collective-permute-start | bytes 2359304 | tf_op jit(solution)/shard_map/ppermute | solution.py:53
  145.9 0.9 copy-start.4
  150.4 16.2 %collective-permute-start.28 = (bf16[384,256]{1,0:T(8,128)(2,1)}, bf16[384,256]{1,0:T(8,128)(2,1)S(1)}, u32[]{:S(2)}, u32[]{:S(2)}) collective-permute-start(bf16[384,256]{1,0:T(8,128)(2,1)} %get-tuple-element.64), channel_id=1, source_target_pairs={{0,32},{8,40},{1,33},{9,41},{2,34},{10,42},{3,35},{11,43},{16,48},... | collective-permute-start | bytes 589832 | tf_op jit(solution)/shard_map/ppermute | solution.py:53
  150.4 19.4 %collective-permute-start.29 = (bf16[384,256]{1,0:T(8,128)(2,1)}, bf16[384,256]{1,0:T(8,128)(2,1)S(1)}, u32[]{:S(2)}, u32[]{:S(2)}) collective-permute-start(bf16[384,256]{1,0:T(8,128)(2,1)} %get-tuple-element.65), channel_id=1, source_target_pairs={{0,64},{8,72},{1,65},{9,73},{2,66},{10,74},{3,67},{11,75},{16,80},... | collective-permute-start | bytes 589832 | tf_op jit(solution)/shard_map/ppermute | solution.py:53
  152.3 9.7 %copy-start = (bf16[768,512]{1,0:T(8,128)(2,1)}, bf16[768,512]{1,0:T(8,128)(2,1)S(1)}, u32[]{:S(2)}) copy-start(bf16[768,512]{1,0:T(8,128)(2,1)S(1)} %collective-permute-done.15.r1) | copy-start | bytes 2359300
  152.3 17.6 %collective-permute-start.30 = (bf16[384,256]{1,0:T(8,128)(2,1)}, bf16[384,256]{1,0:T(8,128)(2,1)S(1)}, u32[]{:S(2)}, u32[]{:S(2)}) collective-permute-start(bf16[384,256]{1,0:T(8,128)(2,1)} %get-tuple-element.66), channel_id=1, source_target_pairs={{0,96},{8,104},{1,97},{9,105},{2,98},{10,106},{3,99},{11,107},{16,... | collective-permute-start | bytes 589832 | tf_op jit(solution)/shard_map/ppermute | solution.py:53
  158.1 3.9 %copy-start.1 = (bf16[768,512]{1,0:T(8,128)(2,1)}, bf16[768,512]{1,0:T(8,128)(2,1)S(1)}, u32[]{:S(2)}) copy-start(bf16[768,512]{1,0:T(8,128)(2,1)S(1)} %collective-permute-done.16.r2) | copy-start | bytes 2359300
  162.0 0.9 copy-start.3
  166.5 9.2 %collective-permute-start.18 = (bf16[384,256]{1,0:T(8,128)(2,1)}, bf16[384,256]{1,0:T(8,128)(2,1)S(1)}, u32[]{:S(2)}, u32[]{:S(2)}) collective-permute-start(bf16[384,256]{1,0:T(8,128)(2,1)} %get-tuple-element.52), channel_id=1, source_target_pairs={{0,16},{8,24},{1,17},{9,25},{2,18},{10,26},{3,19},{11,27},{16,4},{... | collective-permute-start | bytes 589832 | tf_op jit(solution)/shard_map/ppermute | solution.py:53
  166.5 9.2 %collective-permute-start.19 = (bf16[384,256]{1,0:T(8,128)(2,1)}, bf16[384,256]{1,0:T(8,128)(2,1)S(1)}, u32[]{:S(2)}, u32[]{:S(2)}) collective-permute-start(bf16[384,256]{1,0:T(8,128)(2,1)} %get-tuple-element.53), channel_id=1, source_target_pairs={{0,4},{8,12},{1,5},{9,13},{2,6},{10,14},{3,7},{11,15},{16,20},{24,... | collective-permute-start | bytes 589832 | tf_op jit(solution)/shard_map/ppermute | solution.py:53
  166.6 10.0 %copy-start.13 = (bf16[384,256]{1,0:T(8,128)(2,1)}, bf16[384,256]{1,0:T(8,128)(2,1)S(1)}, u32[]{:S(2)}) copy-start(bf16[384,256]{1,0:T(8,128)(2,1)S(1)} %collective-permute-done.28.refs_5_) | copy-start | bytes 589828
  166.6 10.0 %collective-permute-start.20 = (bf16[384,256]{1,0:T(8,128)(2,1)}, bf16[384,256]{1,0:T(8,128)(2,1)S(1)}, u32[]{:S(2)}, u32[]{:S(2)}) collective-permute-start(bf16[384,256]{1,0:T(8,128)(2,1)} %get-tuple-element.54), channel_id=1, source_target_pairs={{0,20},{8,28},{1,21},{9,29},{2,22},{10,30},{3,23},{11,31},{16,0},{... | collective-permute-start | bytes 589832 | tf_op jit(solution)/shard_map/ppermute | solution.py:53
  169.8 6.8 %copy-start.14 = (bf16[384,256]{1,0:T(8,128)(2,1)}, bf16[384,256]{1,0:T(8,128)(2,1)S(1)}, u32[]{:S(2)}) copy-start(bf16[384,256]{1,0:T(8,128)(2,1)S(1)} %collective-permute-done.29.refs_6_) | copy-start | bytes 589828
  169.8 6.8 %copy-start.15 = (bf16[384,256]{1,0:T(8,128)(2,1)}, bf16[384,256]{1,0:T(8,128)(2,1)S(1)}, u32[]{:S(2)}) copy-start(bf16[384,256]{1,0:T(8,128)(2,1)S(1)} %collective-permute-done.30.refs_7_) | copy-start | bytes 589828
  175.7 0.9 copy-start.16
  175.7 0.9 copy-start.17
  176.6 0.7 copy-start.18
where the time goes:
time: 180 us
  waiting for transfers between devices  67.3 us (37%)
  Pallas kernels  55.5 us (31%)
  starting transfers between devices  50.9 us (28%)
  local copies, waits for them, and re-layouts  4.17 us (2%)
    ppermute x31, waiting for transfers between devices, send(): return lax.ppermute(a, ('grp', 'sp'), pairs(**k))  67.3 us
    ppermute x31, starting transfers between devices, send(): return lax.ppermute(a, ('grp', 'sp'), pairs(**k))  50.9 us
    pallas_call x2, Pallas kernels, attention(): call(body, [jax.ShapeDtypeStruct((512, 512), BF16), jax.ShapeDtypeStruct(...  23.5 us
    pallas_call x1, Pallas kernels, weights_b(): call(body, [jax.ShapeDtypeStruct((384, 4 * BW), F32 if d == 0 else BF16)...  7.41 us
    pallas_call x1, Pallas kernels, weights_a(): call(body, [jax.ShapeDtypeStruct((768, 2 * BW), F32 if d == 0 else BF16)...  7.33 us
    pallas_call x2, Pallas kernels, pack_heads(): call(body, [shape] * 3 + [jax.ShapeDtypeStruct((128, 256 + extra), BF16)]...  4.96 us
    pallas_call x1, Pallas kernels, add_b(): call(body, [jax.ShapeDtypeStruct((384, BW), F32 if d == 0 else BF16) for...  3.63 us
    pallas_call x1, Pallas kernels, add_a(): call(body, [jax.ShapeDtypeStruct((384, BW), F32 if d == 0 else BF16) for...  3.62 us
  transfers between devices with their start and end apart: 31, of which 15 were waited for; matrix products, arithmetic and copies ran while one was open for 0% of the time, Pallas kernels for 24%

commit v1 on v0

v1 whole, which is shorter than its diff:
```python
import math

import jax
import jax.numpy as jnp
from jax import lax
from jax.experimental import pallas as pl
from jax.experimental.pallas import tpu as pltpu
from jax.sharding import PartitionSpec as P

HEAD = 128
NEG = -1e30
SCALE = 1.0 / math.sqrt(HEAD)
FACTOR = 16384 ** -0.5
BW = 256
VM = 32 * 1024 * 1024
BIG = 60 * 1024 * 1024
F32 = jnp.float32
BF16 = jnp.bfloat16
ANY = pl.BlockSpec(memory_space=pl.ANY)
VMEM = pl.BlockSpec(memory_space=pltpu.VMEM)


def place():
    g = lax.axis_index("grp")
    s = lax.axis_index("sp")
    return dict(
        z=g // 4, x=(s // 4) * 2 + (g // 2) % 2, c=lax.rem(g, 2), y=lax.rem(s, 4), xh=s // 4
    )


def pairs(dx=0, dy=0, dz=0, dc=0, only_half=None):
    out = []
    for z in range(4):
        for x in range(4):
            for y in range(4):
                for c in range(2):
                    if only_half is not None and x // 2 != only_half:
                        continue

                    def flat(z, x, y, c):
                        return (z * 4 + (x % 2) * 2 + c) * 8 + (x // 2) * 4 + y

                    out.append(
                        (
                            flat(z, x, y, c),
                            flat((z + dz) % 4, (x + dx) % 4, (y + dy) % 4, (c + dc) % 2),
                        )
                    )
    return out


def send(label, a, **k):
    with jax.named_scope(label):
        return lax.ppermute(a, ("grp", "sp"), pairs(**k))


def call(body, outs, scratch, flops, nbytes, in_specs, out_specs, vm=VM):
    return pl.pallas_call(
        body,
        name=body.__name__,
        out_shape=outs,
        in_specs=in_specs,
        out_specs=out_specs,
        scratch_shapes=scratch,
        compiler_params=pltpu.CompilerParams(vmem_limit_bytes=vm),
        cost_estimate=pl.CostEstimate(flops=flops, bytes_accessed=nbytes, transcendentals=0),
    )


def run_copies(todo, sems):
    made = [pltpu.make_async_copy(a, b, sems.at[i]) for i, (a, b) in enumerate(todo)]
    for m in made:
        m.start()
    for m in made:
        m.wait()


def mult(i, n):
    return pl.multiple_of(i * n, n)


def pack_heads(queries, keys, values, grads, ids):
    def pack_heads_body(q, k, v, g, i, k1, k2, k3, k0, q1, q2, q3, sems):
        y = place()["y"]
        todo = []
        for d, ko, qo in ((1, k1, q1), (3, k3, q3), (2, k2, q2), (0, k0, None)):
            for h in range(2):
                s = h * 4 + lax.rem(y + d, 4)
                cols = pl.ds(mult(s, 128), 128)
                todo += [
                    (k.at[0, :, cols], ko.at[:, h * 256 : h * 256 + 128]),
                    (v.at[0, :, cols], ko.at[:, h * 256 + 128 : h * 256 + 256]),
                ]
                if d:
                    cols = pl.ds(mult(s, 512), 512)
                    todo += [
                        (q.at[0, :, cols], qo.at[:, h * 1024 : h * 1024 + 512]),
                        (g.at[0, :, cols], qo.at[:, h * 1024 + 512 : h * 1024 + 1024]),
                    ]
        spread = jnp.broadcast_to(i[...].astype(F32), (128, 128)).T.astype(BF16)
        for o in (k1, k2, k3, k0):
            o[:, 512:640] = spread
        run_copies(todo, sems)

    return call(
        pack_heads_body,
        [jax.ShapeDtypeStruct((128, 640), BF16)] * 4 + [jax.ShapeDtypeStruct((128, 2048), BF16)] * 3,
        [pltpu.SemaphoreType.DMA((28,))],
        10**8,
        10**6,
        [ANY] * 4 + [VMEM],
        [VMEM] * 7,
        BIG,
    )(queries, keys, values, grads, ids)


def pack_inputs(hidden):
    def pack_inputs_body(x, keep, give, sems):
        c = place()["c"]
        todo = []
        for b in range(8):
            at = (b % 2) * 4 + b // 2
            for o, cc in ((keep, c), (give, 1 - c)):
                cols = pl.ds(mult(b * 2 + cc, BW), BW)
                todo.append((x.at[0, :, cols], o.at[:, at * BW : (at + 1) * BW]))
        run_copies(todo, sems)

    shape = jax.ShapeDtypeStruct((128, 8 * BW), BF16)
    return call(
        pack_inputs_body,
        [shape] * 2,
        [pltpu.SemaphoreType.DMA((16,))],
        10**9,
        10**6,
        [ANY],
        [VMEM] * 2,
        BIG,
    )(hidden)


def attention(h, queries, grads, own, msgs, keys, before):
    def attention_body(q, g, kv, q1, q2, q3, k1, k2, k3, pv, pi, dq, dkv, dprev, qs, gs, ks, vs, ids, bias, acck, accv, sems):
        here = place()
        y, xh = here["y"], here["xh"]
        s = h * 4 + y
        row = mult(y, 128)
        todo = [
            (q.at[0, :, pl.ds(mult(s, 512), 512)], qs.at[pl.ds(row, 128), :]),
            (g.at[0, :, pl.ds(mult(s, 512), 512)], gs.at[pl.ds(row, 128), :]),
        ]
        for d, m, k in ((0, None, kv), (1, q1, k1), (2, q2, k2), (3, q3, k3)):
            r = mult(lax.rem(y - d + 4, 4), 128)
            if d:
                todo += [
                    (m.at[:, h * 1024 : h * 1024 + 512], qs.at[pl.ds(r, 128), :]),
                    (m.at[:, h * 1024 + 512 : h * 1024 + 1024], gs.at[pl.ds(r, 128), :]),
                ]
            todo += [
                (k.at[:, h * 256 : h * 256 + 128], ks.at[pl.ds(r + 512, 128), :]),
                (k.at[:, h * 256 + 128 : h * 256 + 256], vs.at[pl.ds(r + 512, 128), :]),
                (k.at[:, 512:640], ids.at[pl.ds(r + 512, 128), :]),
            ]
            rows = pl.ds(d * 128, 128)
            todo += [
                (pv.at[rows, 0:128], ks.at[pl.ds(r, 128), :]),
                (pv.at[rows, 128:256], vs.at[pl.ds(r, 128), :]),
                (pi.at[rows, 256:384], ids.at[pl.ds(r, 128), :]),
            ]
        run_copies(todo, sems)

        low = xh * 512
        own_ids = ids[512:1024, :].astype(F32)
        prev_ids = ids[0:512, :].astype(F32)
        second = xh.astype(F32)

        def count(top):
            a = jnp.sum(jnp.where(own_ids <= top, 1.0, 0.0), axis=0, keepdims=True)
            b = jnp.sum(jnp.where(prev_ids <= top, 1.0, 0.0), axis=0, keepdims=True)
            return (a + second * b)[:, 0:1].astype(jnp.int32)

        first, both = count(0.5), count(1.5)
        acck[...] = jnp.zeros_like(acck)
        accv[...] = jnp.zeros_like(accv)
        for blk in range(2):
            lo = blk * 256
            t = lax.broadcasted_iota(jnp.int32, (1, 256), 1) + lo
            ta = t + low
            start = jnp.where(ta < first, 0, jnp.where(ta < both, first, both)) - low
            u = lax.broadcasted_iota(jnp.int32, (768, 256), 0) + (lo - 512)
            bias[blk] = jnp.where((u <= t) & (u >= start), 0.0, NEG)

        def head(hq, _):
            cols = pl.ds(mult(hq, 128), 128)
            for blk in range(2):
                lo = blk * 256
                keys = ks[lo : lo + 768, :]
                vals = vs[lo : lo + 768, :]
                qq = qs[lo : lo + 256, cols]
                gg = gs[lo : lo + 256, cols]
                nt = (((1,), (1,)), ((), ()))
                sc = lax.dot_general(keys, qq, nt, preferred_element_type=F32) * SCALE + bias[blk]
                e = jnp.exp(sc - jnp.max(sc, axis=0, keepdims=True))
                p = e * (1.0 / jnp.sum(e, axis=0, keepdims=True))
                p_low = p.astype(BF16)
                dp = lax.dot_general(vals, gg, nt, preferred_element_type=F32)
                delta = jnp.sum(p_low.astype(F32) * dp, axis=0, keepdims=True)
                ds = (p * (dp - delta) * SCALE).astype(BF16)
                tn = (((0,), (0,)), ((), ()))
                dqt = lax.dot_general(keys, ds, tn, preferred_element_type=F32)
                dq[cols, lo : lo + 256] = dqt.astype(BF16)
                acck[lo : lo + 768, :] += jnp.dot(ds, qq, preferred_element_type=F32)
                accv[lo : lo + 768, :] += jnp.dot(p_low, gg, preferred_element_type=F32)
            return 0

        lax.fori_loop(0, 4, head, 0)
        dkv[0:128, :] = acck[512:1024, :].T
        dkv[128:256, :] = accv[512:1024, :].T
        dprev[0:128, :] = acck[0:512, :].astype(BF16).T
        dprev[128:256, :] = accv[0:512, :].astype(BF16).T

    return call(
        attention_body,
        [
            jax.ShapeDtypeStruct((512, 512), BF16),
            jax.ShapeDtypeStruct((256, 512), F32),
            jax.ShapeDtypeStruct((256, 512), BF16),
        ],
        [
            pltpu.VMEM((512, 512), BF16),
            pltpu.VMEM((512, 512), BF16),
            pltpu.VMEM((1024, 128), BF16),
            pltpu.VMEM((1024, 128), BF16),
            pltpu.VMEM((1024, 128), BF16),
            pltpu.VMEM((2, 768, 256), F32),
            pltpu.VMEM((1024, 128), F32),
            pltpu.VMEM((1024, 128), F32),
            pltpu.SemaphoreType.DMA((32,)),
        ],
        10**9,
        10**6,
        [ANY] * 11,
        [VMEM] * 3,
    )(queries, grads, own, *msgs, *keys, before[1 - h], before[0])


def gather_a(gt):
    def gather_a_body(a0, b0, a1, b1, ga, sems):
        todo = []
        for h, pair in enumerate(((a0, b0), (a1, b1))):
            for i, src in enumerate(pair):
                to = ga.at[h * 384 : (h + 1) * 384, i * 512 : (i + 1) * 512]
                todo.append((src.at[0:384, :], to))
        run_copies(todo, sems)

    return call(
        gather_a_body,
        jax.ShapeDtypeStruct((768, 1024), BF16),
        [pltpu.SemaphoreType.DMA((4,))],
        10**8,
        10**6,
        [ANY] * 4,
        VMEM,
    )(*gt)


def gather_b(gt, kv):
    def gather_b_body(a0, b0, a1, b1, k, l, gb, sems):
        todo = []
        for h, pair in enumerate(((a0, b0), (a1, b1))):
            for i, (src, low) in enumerate(zip(pair, (k, l))):
                cols = slice(i * 512, (i + 1) * 512)
                todo += [
                    (src.at[384:512, :], gb.at[h * 384 : h * 384 + 128, cols]),
                    (low.at[h * 256 : (h + 1) * 256, :], gb.at[h * 384 + 128 : (h + 1) * 384, cols]),
                ]
        run_copies(todo, sems)

    return call(
        gather_b_body,
        jax.ShapeDtypeStruct((768, 1024), BF16),
        [pltpu.SemaphoreType.DMA((8,))],
        10**8,
        10**6,
        [ANY] * 6,
        VMEM,
    )(*gt, *kv)


def product(a, b):
    return jnp.dot(a, b, preferred_element_type=F32)


def z_cols(xs, z):
    return jnp.concatenate(
        [xs[:, pl.ds(mult(z, BW), BW)], xs[:, pl.ds(mult(z + 4, BW), BW)]], axis=1
    )


def far_a(ga, inputs):
    def far_a_body(g, own, r1, r3, r2a, r2b, xs, up, down, sems):
        here = place()
        y = here["y"]

        def at(d, half):
            row = lax.rem(y - d + 4, 4) * 128 + half * 512
            return xs.at[pl.ds(pl.multiple_of(row, 128), 128), :]

        todo = []
        for d, r in ((0, own), (1, r1), (3, r3)):
            todo += [(r.at[0:128, :], at(d, 0)), (r.at[128:256, :], at(d, 1))]
        run_copies(todo + [(r2a, at(2, 0)), (r2b, at(2, 1))], sems)
        p = product(g[...], z_cols(xs, lax.rem(here["z"] + 2, 4)))
        up[...] = p[:, 0:BW].astype(BF16)
        down[...] = p[:, BW:].astype(BF16)

    return call(
        far_a_body,
        [jax.ShapeDtypeStruct((1024, 8 * BW), BF16)] + [jax.ShapeDtypeStruct((768, BW), BF16)] * 2,
        [pltpu.SemaphoreType.DMA((8,))],
        10**9,
        10**6,
        [VMEM] + [ANY] * 5,
        [VMEM] * 3,
    )(ga, *inputs)


def x_product(g, xs, to, lo, size):
    cols = xs[:, pl.ds(mult(lax.rem(to, 2) * 4 + lo, BW), size * BW)]
    return product(g[pl.ds(mult(to // 2, 384), 384), :], cols)


def far_b(gb, xs):
    def far_b_body(g, x, up, down):
        to = lax.rem(place()["x"] + 2, 4)
        for o, lo in ((up, 0), (down, 2)):
            o[...] = x_product(g, x, to, lo, 2).astype(BF16)

    return call(
        far_b_body,
        [jax.ShapeDtypeStruct((384, 2 * BW), BF16)] * 2,
        [],
        10**9,
        10**6,
        [VMEM] * 2,
        [VMEM] * 2,
    )(gb, xs)


def near_a(ga, xs):
    def near_a_body(g, x, up, down, own):
        z = place()["z"]
        for o, d in ((up, 1), (down, 3), (own, 0)):
            o[...] = product(g[...], z_cols(x, lax.rem(z + d, 4)))

    return call(
        near_a_body,
        [jax.ShapeDtypeStruct((768, 2 * BW), F32)] * 3,
        [],
        10**9,
        10**6,
        [VMEM] * 2,
        [VMEM] * 3,
    )(ga, xs)


def near_b(gb, xs):
    def near_b_body(g, x, up, down, own):
        for o, d in ((up, 1), (down, 3), (own, 0)):
            o[...] = x_product(g, x, lax.rem(place()["x"] + d, 4), 0, 4)

    return call(
        near_b_body,
        [jax.ShapeDtypeStruct((384, 4 * BW), F32)] * 3,
        [],
        10**9,
        10**6,
        [VMEM] * 2,
        [VMEM] * 3,
    )(gb, xs)


def add_near(up, down, got_up, got_down):
    rows, cols = up.shape
    half = cols // 2

    def add_near_body(u, d, gu, gd, ou, od):
        ou[:, 0:half] = (u[:, 0:half] + gu[...].astype(F32)).astype(BF16)
        ou[:, half:] = u[:, half:].astype(BF16)
        od[:, 0:half] = d[:, 0:half].astype(BF16)
        od[:, half:] = (d[:, half:] + gd[...].astype(F32)).astype(BF16)

    return call(
        add_near_body,
        [jax.ShapeDtypeStruct((rows, cols), BF16)] * 2,
        [],
        5 * 10**8,
        10**6,
        [VMEM] * 4,
        [VMEM] * 2,
    )(up, down, got_up, got_down)


def partial_shapes(*shape):
    return [jax.ShapeDtypeStruct(shape, F32 if d == 0 else BF16) for d in range(4)]


def total(refs):
    t = refs[0][...]
    for r in refs[1:]:
        t = t + r[...].astype(F32)
    return t


def add_a(parts):
    def add_a_body(*refs):
        outs, t = refs[3:7], refs[7]
        x = place()["x"]
        t[...] = total(refs[0:3])
        for d in range(4):
            to = lax.rem(x + d, 4)
            rows, cols = pl.ds(mult(to // 2, 384), 384), pl.ds(mult(lax.rem(to, 2), BW), BW)
            outs[d][...] = t[rows, cols].astype(outs[d].dtype)

    return call(
        add_a_body,
        partial_shapes(384, 256),
        [pltpu.VMEM((768, 2 * BW), F32)],
        5 * 10**8,
        10**6,
        [VMEM] * 3,
        [VMEM] * 4,
    )(*parts)


def add_b(parts):
    def add_b_body(*refs):
        outs, t = refs[3:7], refs[7]
        z = place()["z"]
        t[...] = total(refs[0:3])
        for d in range(4):
            o = outs[d]
            o[...] = t[:, pl.ds(mult(lax.rem(z + d, 4), BW), BW)].astype(o.dtype)

    return call(
        add_b_body,
        partial_shapes(384, 256),
        [pltpu.VMEM((384, 4 * BW), F32)],
        5 * 10**8,
        10**6,
        [VMEM] * 3,
        [VMEM] * 4,
    )(*parts)


def finish(parts):
    def finish_body(*refs):
        qo, ko, vo = refs[8:]
        a = (total(refs[0:4]) * FACTOR).T
        b = (total(refs[4:8]) * FACTOR).T
        qo[:, 0:384] = a
        qo[:, 384:512] = b[:, 0:128]
        ko[...] = b[:, 128:256]
        vo[...] = b[:, 256:384]

    return call(
        finish_body,
        [
            jax.ShapeDtypeStruct((256, 512), F32),
            jax.ShapeDtypeStruct((256, 128), F32),
            jax.ShapeDtypeStruct((256, 128), F32),
        ],
        [],
        0,
        0,
        [VMEM] * 8,
        [VMEM] * 3,
    )(*parts)


def after(x, *deps):
    return lax.optimization_barrier((x, *deps))[0]


def ring(label, far, up, down, **axis):
    step = {k: -v for k, v in axis.items()}
    got_up = send(label + "_far_up", far[0], **axis)
    got_down = send(label + "_far_down", far[1], **step)
    ou, od = add_near(up, down, got_up, got_down)
    return send(label + "_up", ou, **axis), send(label + "_down", od, **step)


def per_device(hidden_in, queries, key_heads, saved_value_heads, out_grads, doc_ids):
    *kmsg, own, q1, q2, q3 = pack_heads(queries, key_heads, saved_value_heads, out_grads, doc_ids)
    keys = [send("keys_y%d" % (d + 1), m, dy=d + 1) for d, m in enumerate(kmsg)]
    keep, give = pack_inputs(after(hidden_in, own))
    got = send("swap_inputs", give, dc=1)
    m1 = send("queries_y1", after(q1, keys[0]), dy=1)
    m3 = send("queries_y3", after(q3, keys[0], keys[2]), dy=3)
    m2 = send("queries_y2", after(q2, keys[0], keys[2], got), dy=2)
    msgs = [m1, m2, m3]
    all_keys = jnp.concatenate([own] + keys, axis=0)
    before = [
        send("half0", all_keys[:, 256:640], dx=2, only_half=0),
        send("half1", all_keys[:, 0:256], dx=2, only_half=0),
    ]
    mine = jnp.concatenate([keep, got], axis=0)
    sent = after(mine, m1, m3)
    up = send("inputs_up", sent, dy=1)
    down = send("inputs_down", sent, dy=-1)

    dq0, dkv0, back0 = attention(0, queries, out_grads, own, msgs, keys, before)
    swap0 = send("swap_dq0", dq0, dc=1)
    dq1, dkv1, back1 = attention(1, after(queries, dq0, swap0), out_grads, own, msgs, keys, before)
    fwd = send("inputs_up2", after(up[0:128], dq1), dy=1)
    rev = send("inputs_down2", after(down[128:256], dq1), dy=-1)
    swap1 = send("swap_dq1", dq1, dc=1)
    ret = send("back", jnp.concatenate([back0, back1], axis=0), dx=2, only_half=1)
    ret = after(ret, fwd, rev, swap1).astype(F32)
    low = (jnp.concatenate([dkv0, dkv1], axis=0) + ret).astype(BF16)
    kv = (low, send("swap_dkv", low, dc=1))
    inputs = (mine, up, down, fwd, rev)
    gt = (dq0, swap0, dq1, swap1)

    ga = gather_a(gt)
    xs, *fa = far_a(ga, inputs)
    gb = gather_b(gt, kv)
    fb = far_b(after(gb, fa[0]), xs)
    ua, da, oa = near_a(after(ga, fb[0]), xs)
    ub, db, ob = near_b(after(gb, oa), xs)
    ra = ring("reduce_a", fa, ua, da, dz=1)
    rb = ring("reduce_b", fb, ub, db, dx=1)
    ma = add_a([oa, *ra])
    sa = [send("second_a_x%d" % d, ma[d], dx=d) for d in (1, 3, 2)]
    mb = add_b([ob, *rb])
    sb = [send("second_b_z%d" % d, mb[d], dz=d) for d in (1, 3, 2)]
    return finish([ma[0], *sa, mb[0], *sb])


def solution(mesh):
    return jax.shard_map(
        per_device,
        mesh=mesh,
        in_specs=(
            P("grp", "sp", None),
            P("grp", "sp", None),
            P("grp", "sp", None),
            P("grp", "sp", None),
            P("grp", "sp", None),
            P("grp", "sp"),
        ),
        out_specs=(P("grp", "sp"), P("grp", "sp"), P("grp", "sp")),
        check_vma=False,
    )
```

time: 180 us -> 141 us (0.78)
  Pallas kernels: 55.5 us -> 36.7 us
  waiting for transfers between devices: 67.3 us -> 55.4 us
  starting transfers between devices: 50.9 us -> 45.8 us
  local copies, waits for them, and re-layouts: 4.17 us -> 1.38 us
    pallas_call x10 -> x15, Pallas kernels: 55.5 us -> 36.7 us  [the longest x2 19.8 us: attention(): call(attention_body, [jax.ShapeDtypeStruct((512, 512), BF16), jax.ShapeDt...]
    ppermute x31, waiting for transfers between devices: 67.3 us -> 55.4 us  [send(): return lax.ppermute(a, ('grp', 'sp'), pairs(**k))]
    ppermute x31, starting transfers between devices: 50.9 us -> 45.8 us  [send(): return lax.ppermute(a, ('grp', 'sp'), pairs(**k))]
    unnamed x67 -> x18, local copies, waits for them, and re-layouts: 3.31 us -> 1.17 us
  transfers between devices with their start and end apart: 31 -> 31, of which waited for: 15 -> 12; matrix products, arithmetic and copies ran while one was open for 0% -> 1% of each run, Pallas kernels for 24% -> 23%
where the time goes in v1:
time: 141 us
  waiting for transfers between devices  55.4 us (39%)
  starting transfers between devices  45.8 us (32%)
  Pallas kernels  36.7 us (26%)
    ppermute x31, waiting for transfers between devices, send(): return lax.ppermute(a, ('grp', 'sp'), pairs(**k))  55.4 us
    ppermute x31, starting transfers between devices, send(): return lax.ppermute(a, ('grp', 'sp'), pairs(**k))  45.8 us
    pallas_call x2, Pallas kernels, attention(): call(attention_body, [jax.ShapeDtypeStruct((512, 512), BF16), jax.ShapeDt...  19.8 us
    pallas_call x1, Pallas kernels, pack_heads(): call(pack_heads_body, [jax.ShapeDtypeStruct((128, 640), BF16)] * 4 + [jax...  3.98 us
  transfers between devices with their start and end apart: 31, of which 12 were waited for; matrix products, arithmetic and copies ran while one was open for 1% of the time, Pallas kernels for 23%

profile of v1, /device:TPU:24, one launch (start us, length us, event | category | flops | bytes accessed | tf_op | source)
XLA Modules:
  0.0 140.5 jit_solution(17930337559564075162)
XLA Ops:
  0.6 4.0 %pack_heads_body.1 = (bf16[128,640]{1,0:T(8,128)(2,1)}, bf16[128,640]{1,0:T(8,128)(2,1)}, bf16[128,640]{1,0:T(8,128)(2,1)}, bf16[128,640]{1,0:T(8,128)(2,1)}, bf...) custom-call(bf16[1,128,4096]{2,1,0:T(8,128)(2,1)} %q.4, bf16[1,128,1024]{2,1,0:T(8,128)(2,1)} %k.1, ...), custom_call_target="tpu_custom_call" | custom-call | flops 100000000 | bytes 1000000 | tf_op jit(solution)/shard_map/pack_heads_body/pallas_call | solution.py:105
  4.6 0.2 collective-permute-start
  4.8 1.9 %collective-permute-start.2 = (bf16[128,640]{1,0:T(8,128)(2,1)}, bf16[128,640]{1,0:T(8,128)(2,1)S(1)}, u32[]{:S(2)}, u32[]{:S(2)}) collective-permute-start(bf16[128,640]{1,0:T(8,128)(2,1)} %get-tuple-element.58), channel_id=1, source_target_pairs={{0,3},{8,11},{1,0},{9,8},{2,1},{10,9},{3,2},{11,10},{16,19},{24,27... | collective-permute-start | bytes 491528 | tf_op jit(solution)/shard_map/keys_y3/ppermute | solution.py:54
  6.7 2.5 %pack_inputs_body.1 = (bf16[128,2048]{1,0:T(8,128)(2,1)}, bf16[128,2048]{1,0:T(8,128)(2,1)}) custom-call(bf16[1,128,4096]{2,1,0:T(8,128)(2,1)} %x), custom_call_target="tpu_custom_call" | custom-call | flops 1000000000 | bytes 1000000 | tf_op jit(solution)/shard_map/pack_inputs_body/pallas_call | solution.py:129
  9.2 0.1 collective-permute-start.3
  9.3 1.3 collective-permute-start.6
  10.6 1.1 constant_dynamic-update-slice_fusion.5
  11.8 2.3 %collective-permute-start.1 = (bf16[128,2048]{1,0:T(8,128)(2,1)S(1)}, bf16[128,2048]{1,0:T(8,128)(2,1)S(1)}, u32[]{:S(2)}, u32[]{:S(2)}) collective-permute-start(bf16[128,2048]{1,0:T(8,128)(2,1)S(1)} %copy-done.5), channel_id=1, source_target_pairs={{0,1},{8,9},{1,2},{9,10},{2,3},{10,11},{3,0},{11,8},{16,17},{24,25... | collective-permute-start | bytes 1572872 | tf_op jit(solution)/shard_map/queries_y1/ppermute | solution.py:54
  14.0 0.0 collective-permute-start.5
  14.1 0.0 copy-start
  14.1 0.0 copy-start.1
  14.1 3.8 %collective-permute-done.6.k2 = bf16[128,640]{1,0:T(8,128)(2,1)S(1)} collective-permute-done((bf16[128,640]{1,0:T(8,128)(2,1)S(1)}, bf16[128,640]{1,0:T(8,128)(2,1)S(1)}, u32[]{:S(2)}, u32[]{:S(2)}) %collective-permute-start.6) | collective-permute-done | bytes 163872 | tf_op jit(solution)/shard_map/keys_y2/ppermute | solution.py:54
  17.9 0.0 collective-permute-done.3
  18.0 1.2 collective-permute-start.4
  19.2 4.9 %collective-permute-start.7 = (bf16[512,256]{1,0:T(8,128)(2,1)S(1)}, bf16[512,256]{1,0:T(8,128)(2,1)S(1)}, u32[]{:S(2)}, u32[]{:S(2)}) collective-permute-start(bf16[512,256]{1,0:T(8,128)(2,1)S(1)} %slice.16), channel_id=1, source_target_pairs={{0,4},{8,12},{1,5},{9,13},{2,6},{10,14},{3,7},{11,15},{16,20},{24,... | collective-permute-start | bytes 786440 | tf_op jit(solution)/shard_map/half1/ppermute | solution.py:54
  24.2 1.3 collective-permute-start.8
  25.5 2.3 %collective-permute-done.1.q1 = bf16[128,2048]{1,0:T(8,128)(2,1)S(1)} collective-permute-done((bf16[128,2048]{1,0:T(8,128)(2,1)S(1)}, bf16[128,2048]{1,0:T(8,128)(2,1)S(1)}, u32[]{:S(2)}, u32[]{:S(2)}) %collective-permute-start.1) | collective-permute-done | bytes 524320 | tf_op jit(solution)/shard_map/queries_y1/ppermute | solution.py:54
  27.8 12.7 %collective-permute-done.5.q3 = bf16[128,2048]{1,0:T(8,128)(2,1)S(1)} collective-permute-done((bf16[128,2048]{1,0:T(8,128)(2,1)S(1)}, bf16[128,2048]{1,0:T(8,128)(2,1)S(1)}, u32[]{:S(2)}, u32[]{:S(2)}) %collective-permute-start.5) | collective-permute-done | bytes 524320 | tf_op jit(solution)/shard_map/queries_y3/ppermute | solution.py:54
  40.5 0.0 collective-permute-start.12
  40.5 2.0 %collective-permute-start.14 = (bf16[256,2048]{1,0:T(8,128)(2,1)S(1)}, bf16[256,2048]{1,0:T(8,128)(2,1)S(1)}, u32[]{:S(2)}, u32[]{:S(2)}) collective-permute-start(bf16[256,2048]{1,0:T(8,128)(2,1)S(1)} %constant_dynamic-update-slice_fusion.4.own), channel_id=1, source_target_pairs={{0,3},{8,11},{1,0},{9,8},{2,1},{10,9},{3,2},{11,10},{16,19},{24,27... | collective-permute-start | bytes 3145736 | tf_op jit(solution)/shard_map/inputs_down/ppermute | solution.py:54
  42.5 0.0 collective-permute-done.7.pv
  42.6 9.9 %attention_body.2 = (bf16[512,512]{1,0:T(8,128)(2,1)S(1)}, f32[256,512]{1,0:T(8,128)S(1)}, bf16[256,512]{1,0:T(8,128)(2,1)S(1)}) custom-call(bf16[1,128,4096]{2,1,0:T(8,128)(2,1)S(1)} %copy-done, bf16[1,128,4096]{2,1,0:T(8,128)(2,1)S(1)} %copy-done.1, bf16[128,640]{1,0:T(8,128)(2,1)S(1)} %copy-done.2, bf16[128,2048]{1,0:T(8,128)(2,1)S(1)} %collective-permute-done.1.q1, ...), custom_call_target="tpu_custom_call" | custom-call | flops 1000000000 | bytes 1000000 | tf_op jit(solution)/shard_map/attention_body/pallas_call | solution.py:221
  52.5 0.1 collective-permute-start.9
  52.6 1.9 %collective-permute-done.9.b0 = bf16[512,512]{1,0:T(8,128)(2,1)S(1)} collective-permute-done((bf16[512,512]{1,0:T(8,128)(2,1)S(1)}, bf16[512,512]{1,0:T(8,128)(2,1)S(1)}, u32[]{:S(2)}, u32[]{:S(2)}) %collective-permute-start.9) | collective-permute-done | bytes 524320 | tf_op jit(solution)/shard_map/swap_dq0/ppermute | solution.py:54
  54.5 9.9 %attention_body.3 = (bf16[512,512]{1,0:T(8,128)(2,1)S(1)}, f32[256,512]{1,0:T(8,128)S(1)}, bf16[256,512]{1,0:T(8,128)(2,1)S(1)}) custom-call(bf16[1,128,4096]{2,1,0:T(8,128)(2,1)S(1)} %copy-done, bf16[1,128,4096]{2,1,0:T(8,128)(2,1)S(1)} %copy-done.1, bf16[128,640]{1,0:T(8,128)(2,1)S(1)} %copy-done.2, bf16[128,2048]{1,0:T(8,128)(2,1)S(1)} %collective-permute-done.1.q1, ...), custom_call_target="tpu_custom_call" | custom-call | flops 1000000000 | bytes 1000000 | tf_op jit(solution)/shard_map/attention_body/pallas_call | solution.py:221
  64.3 0.2 collective-permute-start.10
  64.6 1.3 collective-permute-start.11
  66.0 1.3 collective-permute-start.13
  67.3 0.9 collective-permute-start.15
  68.2 14.0 %collective-permute-done.11 = bf16[512,512]{1,0:T(8,128)(2,1)S(1)} collective-permute-done((bf16[512,512]{1,0:T(8,128)(2,1)S(1)}, bf16[512,512]{1,0:T(8,128)(2,1)S(1)}, u32[]{:S(2)}, u32[]{:S(2)}) %collective-permute-start.11) | collective-permute-done | bytes 524320 | tf_op jit(solution)/shard_map/back/ppermute | solution.py:54
  82.2 0.3 collective-permute-done.15.r2b
  82.5 0.2 fusion.k
  82.6 0.3 collective-permute-start.16
  82.9 0.2 gather_a_body.1.g
  83.1 1.4 %far_a_body.1 = (bf16[1024,2048]{1,0:T(8,128)(2,1)S(1)}, bf16[768,256]{1,0:T(8,128)(2,1)S(1)}, bf16[768,256]{1,0:T(8,128)(2,1)S(1)}) custom-call(bf16[768,1024]{1,0:T(8,128)(2,1)S(1)} %gather_a_body.1.g, bf16[256,2048]{1,0:T(8,128)(2,1)S(1)} %constant_dynamic-update-slice_fusion.4.own, bf16[256,2048]{1,0:T(8,128)(2,1)S(1)} %collective-permute-done.12.r1, ...), custom_call_target="tpu_custom_call" | custom-call | flops 1000000000 | bytes 1000000 | tf_op jit(solution)/shard_map/far_a_body/pallas_call | solution.py:316
  84.5 2.0 %collective-permute-start.17 = (bf16[768,256]{1,0:T(8,128)(2,1)S(1)}, bf16[768,256]{1,0:T(8,128)(2,1)S(1)}, u32[]{:S(2)}, u32[]{:S(2)}) collective-permute-start(bf16[768,256]{1,0:T(8,128)(2,1)S(1)} %get-tuple-element.77), channel_id=1, source_target_pairs={{0,32},{8,40},{1,33},{9,41},{2,34},{10,42},{3,35},{11,43},{16,48},... | collective-permute-start | bytes 1179656 | tf_op jit(solution)/shard_map/reduce_a_far_up/ppermute | solution.py:54
  86.5 2.2 %collective-permute-start.18 = (bf16[768,256]{1,0:T(8,128)(2,1)S(1)}, bf16[768,256]{1,0:T(8,128)(2,1)S(1)}, u32[]{:S(2)}, u32[]{:S(2)}) collective-permute-start(bf16[768,256]{1,0:T(8,128)(2,1)S(1)} %get-tuple-element.85), channel_id=1, source_target_pairs={{0,96},{8,104},{1,97},{9,105},{2,98},{10,106},{3,99},{11,107},{16,... | collective-permute-start | bytes 1179656 | tf_op jit(solution)/shard_map/reduce_a_far_down/ppermute | solution.py:54
  88.7 0.2 gather_b_body.1.g
  89.0 1.0 far_b_body.1
  90.0 1.6 %collective-permute-start.24 = (bf16[384,512]{1,0:T(8,128)(2,1)S(1)}, bf16[384,512]{1,0:T(8,128)(2,1)S(1)}, u32[]{:S(2)}, u32[]{:S(2)}) collective-permute-start(bf16[384,512]{1,0:T(8,128)(2,1)S(1)} %get-tuple-element.80), channel_id=1, source_target_pairs={{0,16},{8,24},{1,17},{9,25},{2,18},{10,26},{3,19},{11,27},{16,4},{... | collective-permute-start | bytes 1179656 | tf_op jit(solution)/shard_map/reduce_b_far_up/ppermute | solution.py:54
  91.5 3.1 %collective-permute-start.25 = (bf16[384,512]{1,0:T(8,128)(2,1)S(1)}, bf16[384,512]{1,0:T(8,128)(2,1)S(1)}, u32[]{:S(2)}, u32[]{:S(2)}) collective-permute-start(bf16[384,512]{1,0:T(8,128)(2,1)S(1)} %get-tuple-element.96), channel_id=1, source_target_pairs={{0,20},{8,28},{1,21},{9,29},{2,22},{10,30},{3,23},{11,31},{16,0},{... | collective-permute-start | bytes 1179656 | tf_op jit(solution)/shard_map/reduce_b_far_down/ppermute | solution.py:54
  94.6 2.6 %near_a_body.1 = (f32[768,512]{1,0:T(8,128)S(1)}, f32[768,512]{1,0:T(8,128)S(1)}, f32[768,512]{1,0:T(8,128)S(1)}) custom-call(bf16[768,1024]{1,0:T(8,128)(2,1)S(1)} %gather_a_body.1.g, bf16[1024,2048]{1,0:T(8,128)(2,1)S(1)} %get-tuple-element.79.x), custom_call_target="tpu_custom_call" | custom-call | flops 1000000000 | bytes 1000000 | tf_op jit(solution)/shard_map/near_a_body/pallas_call | solution.py:355
  97.3 1.1 collective-permute-done.17.gu
  98.4 0.2 add_near_body.2
  98.6 1.3 collective-permute-start.19
  99.9 2.0 %collective-permute-start.20 = (bf16[768,512]{1,0:T(8,128)(2,1)S(1)}, bf16[768,512]{1,0:T(8,128)(2,1)S(1)}, u32[]{:S(2)}, u32[]{:S(2)}) collective-permute-start(bf16[768,512]{1,0:T(8,128)(2,1)S(1)} %get-tuple-element.87), channel_id=1, source_target_pairs={{0,96},{8,104},{1,97},{9,105},{2,98},{10,106},{3,99},{11,107},{16,... | collective-permute-start | bytes 2359304 | tf_op jit(solution)/shard_map/reduce_a_down/ppermute | solution.py:54
  101.9 2.6 %near_b_body.1 = (f32[384,1024]{1,0:T(8,128)S(1)}, f32[384,1024]{1,0:T(8,128)S(1)}, f32[384,1024]{1,0:T(8,128)S(1)}) custom-call(bf16[768,1024]{1,0:T(8,128)(2,1)S(1)} %gather_b_body.1.g, bf16[1024,2048]{1,0:T(8,128)(2,1)S(1)} %get-tuple-element.79.x), custom_call_target="tpu_custom_call" | custom-call | flops 1000000000 | bytes 1000000 | tf_op jit(solution)/shard_map/near_b_body/pallas_call | solution.py:371
  104.6 0.2 add_near_body.3
  104.8 1.5 %collective-permute-start.26 = (bf16[384,1024]{1,0:T(8,128)(2,1)S(1)}, bf16[384,1024]{1,0:T(8,128)(2,1)S(1)}, u32[]{:S(2)}, u32[]{:S(2)}) collective-permute-start(bf16[384,1024]{1,0:T(8,128)(2,1)S(1)} %get-tuple-element.97), channel_id=1, source_target_pairs={{0,16},{8,24},{1,17},{9,25},{2,18},{10,26},{3,19},{11,27},{16,4},{... | collective-permute-start | bytes 2359304 | tf_op jit(solution)/shard_map/reduce_b_up/ppermute | solution.py:54
  106.3 3.1 %collective-permute-start.27 = (bf16[384,1024]{1,0:T(8,128)(2,1)S(1)}, bf16[384,1024]{1,0:T(8,128)(2,1)S(1)}, u32[]{:S(2)}, u32[]{:S(2)}) collective-permute-start(bf16[384,1024]{1,0:T(8,128)(2,1)S(1)} %get-tuple-element.98), channel_id=1, source_target_pairs={{0,20},{8,28},{1,21},{9,29},{2,22},{10,30},{3,23},{11,31},{16,0},{... | collective-permute-start | bytes 2359304 | tf_op jit(solution)/shard_map/reduce_b_down/ppermute | solution.py:54
  109.4 9.8 %collective-permute-done.19.refs_1_ = bf16[768,512]{1,0:T(8,128)(2,1)S(1)} collective-permute-done((bf16[768,512]{1,0:T(8,128)(2,1)S(1)}, bf16[768,512]{1,0:T(8,128)(2,1)S(1)}, u32[]{:S(2)}, u32[]{:S(2)}) %collective-permute-start.19) | collective-permute-done | bytes 786464 | tf_op jit(solution)/shard_map/reduce_a_up/ppermute | solution.py:54
  119.3 0.5 add_a_body.1
  119.7 1.5 %collective-permute-start.21 = (bf16[384,256]{1,0:T(8,128)(2,1)S(1)}, bf16[384,256]{1,0:T(8,128)(2,1)S(1)}, u32[]{:S(2)}, u32[]{:S(2)}) collective-permute-start(bf16[384,256]{1,0:T(8,128)(2,1)S(1)} %get-tuple-element.89), channel_id=1, source_target_pairs={{0,16},{8,24},{1,17},{9,25},{2,18},{10,26},{3,19},{11,27},{16,4},{... | collective-permute-start | bytes 589832 | tf_op jit(solution)/shard_map/second_a_x1/ppermute | solution.py:54
  121.3 3.1 %collective-permute-start.22 = (bf16[384,256]{1,0:T(8,128)(2,1)S(1)}, bf16[384,256]{1,0:T(8,128)(2,1)S(1)}, u32[]{:S(2)}, u32[]{:S(2)}) collective-permute-start(bf16[384,256]{1,0:T(8,128)(2,1)S(1)} %get-tuple-element.90), channel_id=1, source_target_pairs={{0,20},{8,28},{1,21},{9,29},{2,22},{10,30},{3,23},{11,31},{16,0},{... | collective-permute-start | bytes 589832 | tf_op jit(solution)/shard_map/second_a_x3/ppermute | solution.py:54
  124.4 1.4 collective-permute-start.23
  125.8 2.0 %collective-permute-done.26.refs_1_ = bf16[384,1024]{1,0:T(8,128)(2,1)S(1)} collective-permute-done((bf16[384,1024]{1,0:T(8,128)(2,1)S(1)}, bf16[384,1024]{1,0:T(8,128)(2,1)S(1)}, u32[]{:S(2)}, u32[]{:S(2)}) %collective-permute-start.26) | collective-permute-done | bytes 786464 | tf_op jit(solution)/shard_map/reduce_b_up/ppermute | solution.py:54
  127.8 0.5 add_b_body.1
  128.3 0.1 collective-permute-start.28
  128.4 3.2 %collective-permute-start.29 = (bf16[384,256]{1,0:T(8,128)(2,1)S(1)}, bf16[384,256]{1,0:T(8,128)(2,1)S(1)}, u32[]{:S(2)}, u32[]{:S(2)}) collective-permute-start(bf16[384,256]{1,0:T(8,128)(2,1)S(1)} %get-tuple-element.101), channel_id=1, source_target_pairs={{0,96},{8,104},{1,97},{9,105},{2,98},{10,106},{3,99},{11,107},{16,... | collective-permute-start | bytes 589832 | tf_op jit(solution)/shard_map/second_b_z3/ppermute | solution.py:54
  131.6 0.4 collective-permute-start.30
  132.0 2.2 %collective-permute-done.22.refs_2_ = bf16[384,256]{1,0:T(8,128)(2,1)S(1)} collective-permute-done((bf16[384,256]{1,0:T(8,128)(2,1)S(1)}, bf16[384,256]{1,0:T(8,128)(2,1)S(1)}, u32[]{:S(2)}, u32[]{:S(2)}) %collective-permute-start.22) | collective-permute-done | bytes 196640 | tf_op jit(solution)/shard_map/second_a_x3/ppermute | solution.py:54
  134.2 1.8 %collective-permute-done.23.refs_3_ = bf16[384,256]{1,0:T(8,128)(2,1)S(1)} collective-permute-done((bf16[384,256]{1,0:T(8,128)(2,1)S(1)}, bf16[384,256]{1,0:T(8,128)(2,1)S(1)}, u32[]{:S(2)}, u32[]{:S(2)}) %collective-permute-start.23) | collective-permute-done | bytes 196640 | tf_op jit(solution)/shard_map/second_a_x2/ppermute | solution.py:54
  136.0 3.4 %collective-permute-done.28.refs_5_ = bf16[384,256]{1,0:T(8,128)(2,1)S(1)} collective-permute-done((bf16[384,256]{1,0:T(8,128)(2,1)S(1)}, bf16[384,256]{1,0:T(8,128)(2,1)S(1)}, u32[]{:S(2)}, u32[]{:S(2)}) %collective-permute-start.28) | collective-permute-done | bytes 196640 | tf_op jit(solution)/shard_map/second_b_z1/ppermute | solution.py:54
  139.5 1.1 finish_body.1
  (39 shorter events, 0.4 us)
Async XLA Ops:
  4.6 7.1 %collective-permute-start = (bf16[128,640]{1,0:T(8,128)(2,1)}, bf16[128,640]{1,0:T(8,128)(2,1)S(1)}, u32[]{:S(2)}, u32[]{:S(2)}) collective-permute-start(bf16[128,640]{1,0:T(8,128)(2,1)} %get-tuple-element.55), channel_id=1, source_target_pairs={{0,1},{8,9},{1,2},{9,10},{2,3},{10,11},{3,0},{11,8},{16,17},{24,25... | collective-permute-start | bytes 491528 | tf_op jit(solution)/shard_map/keys_y1/ppermute | solution.py:54
  4.8 9.2 %collective-permute-start.2 = (bf16[128,640]{1,0:T(8,128)(2,1)}, bf16[128,640]{1,0:T(8,128)(2,1)S(1)}, u32[]{:S(2)}, u32[]{:S(2)}) collective-permute-start(bf16[128,640]{1,0:T(8,128)(2,1)} %get-tuple-element.58), channel_id=1, source_target_pairs={{0,3},{8,11},{1,0},{9,8},{2,1},{10,9},{3,2},{11,10},{16,19},{24,27... | collective-permute-start | bytes 491528 | tf_op jit(solution)/shard_map/keys_y3/ppermute | solution.py:54
  6.7 2.6 %copy-start.6 = (bf16[128,640]{1,0:T(8,128)(2,1)S(1)}, bf16[128,640]{1,0:T(8,128)(2,1)}, u32[]{:S(2)}) copy-start(bf16[128,640]{1,0:T(8,128)(2,1)} %get-tuple-element.64) | copy-start | bytes 491524
  6.7 5.0 %copy-start.2 = (bf16[128,640]{1,0:T(8,128)(2,1)S(1)}, bf16[128,640]{1,0:T(8,128)(2,1)}, u32[]{:S(2)}) copy-start(bf16[128,640]{1,0:T(8,128)(2,1)} %get-tuple-element.53.kv) | copy-start | bytes 491524
  6.7 5.1 %copy-start.5 = (bf16[128,2048]{1,0:T(8,128)(2,1)S(1)}, bf16[128,2048]{1,0:T(8,128)(2,1)}, u32[]{:S(2)}) copy-start(bf16[128,2048]{1,0:T(8,128)(2,1)} %get-tuple-element.56) | copy-start | bytes 1572868
  6.7 7.3 %copy-start.4 = (bf16[128,2048]{1,0:T(8,128)(2,1)S(1)}, bf16[128,2048]{1,0:T(8,128)(2,1)}, u32[]{:S(2)}) copy-start(bf16[128,2048]{1,0:T(8,128)(2,1)} %get-tuple-element.63) | copy-start | bytes 1572868
  9.2 8.7 %copy-start.3 = (bf16[128,2048]{1,0:T(8,128)(2,1)S(1)}, bf16[128,2048]{1,0:T(8,128)(2,1)}, u32[]{:S(2)}) copy-start(bf16[128,2048]{1,0:T(8,128)(2,1)} %get-tuple-element.61) | copy-start | bytes 1572868
  9.2 8.7 %collective-permute-start.3 = (bf16[128,2048]{1,0:T(8,128)(2,1)}, bf16[128,2048]{1,0:T(8,128)(2,1)S(1)}, u32[]{:S(2)}, u32[]{:S(2)}) collective-permute-start(bf16[128,2048]{1,0:T(8,128)(2,1)} %get-tuple-element.60), channel_id=1, source_target_pairs={{0,8},{8,0},{1,9},{9,1},{2,10},{10,2},{3,11},{11,3},{16,24},{24,16... | collective-permute-start | bytes 1572872 | tf_op jit(solution)/shard_map/swap_inputs/ppermute | solution.py:54
  9.3 8.6 %collective-permute-start.6 = (bf16[128,640]{1,0:T(8,128)(2,1)S(1)}, bf16[128,640]{1,0:T(8,128)(2,1)S(1)}, u32[]{:S(2)}, u32[]{:S(2)}) collective-permute-start(bf16[128,640]{1,0:T(8,128)(2,1)S(1)} %copy-done.6), channel_id=1, source_target_pairs={{0,2},{8,10},{1,3},{9,11},{2,0},{10,8},{3,1},{11,9},{16,18},{24,26... | collective-permute-start | bytes 491528 | tf_op jit(solution)/shard_map/keys_y2/ppermute | solution.py:54
  11.8 16.0 %collective-permute-start.1 = (bf16[128,2048]{1,0:T(8,128)(2,1)S(1)}, bf16[128,2048]{1,0:T(8,128)(2,1)S(1)}, u32[]{:S(2)}, u32[]{:S(2)}) collective-permute-start(bf16[128,2048]{1,0:T(8,128)(2,1)S(1)} %copy-done.5), channel_id=1, source_target_pairs={{0,1},{8,9},{1,2},{9,10},{2,3},{10,11},{3,0},{11,8},{16,17},{24,25... | collective-permute-start | bytes 1572872 | tf_op jit(solution)/shard_map/queries_y1/ppermute | solution.py:54
  14.0 26.5 %collective-permute-start.5 = (bf16[128,2048]{1,0:T(8,128)(2,1)S(1)}, bf16[128,2048]{1,0:T(8,128)(2,1)S(1)}, u32[]{:S(2)}, u32[]{:S(2)}) collective-permute-start(bf16[128,2048]{1,0:T(8,128)(2,1)S(1)} %copy-done.4), channel_id=1, source_target_pairs={{0,3},{8,11},{1,0},{9,8},{2,1},{10,9},{3,2},{11,10},{16,19},{24,27... | collective-permute-start | bytes 1572872 | tf_op jit(solution)/shard_map/queries_y3/ppermute | solution.py:54
  14.1 28.5 %copy-start = (bf16[1,128,4096]{2,1,0:T(8,128)(2,1)S(1)}, bf16[1,128,4096]{2,1,0:T(8,128)(2,1)}, u32[]{:S(2)}) copy-start(bf16[1,128,4096]{2,1,0:T(8,128)(2,1)} %q.4) | copy-start | bytes 3145732
  14.1 28.5 %copy-start.1 = (bf16[1,128,4096]{2,1,0:T(8,128)(2,1)S(1)}, bf16[1,128,4096]{2,1,0:T(8,128)(2,1)}, u32[]{:S(2)}) copy-start(bf16[1,128,4096]{2,1,0:T(8,128)(2,1)} %g.5) | copy-start | bytes 3145732
  18.0 24.6 %collective-permute-start.4 = (bf16[128,2048]{1,0:T(8,128)(2,1)S(1)}, bf16[128,2048]{1,0:T(8,128)(2,1)S(1)}, u32[]{:S(2)}, u32[]{:S(2)}) collective-permute-start(bf16[128,2048]{1,0:T(8,128)(2,1)S(1)} %copy-done.3), channel_id=1, source_target_pairs={{0,2},{8,10},{1,3},{9,11},{2,0},{10,8},{3,1},{11,9},{16,18},{24,26... | collective-permute-start | bytes 1572872 | tf_op jit(solution)/shard_map/queries_y2/ppermute | solution.py:54
  19.2 23.3 %collective-permute-start.7 = (bf16[512,256]{1,0:T(8,128)(2,1)S(1)}, bf16[512,256]{1,0:T(8,128)(2,1)S(1)}, u32[]{:S(2)}, u32[]{:S(2)}) collective-permute-start(bf16[512,256]{1,0:T(8,128)(2,1)S(1)} %slice.16), channel_id=1, source_target_pairs={{0,4},{8,12},{1,5},{9,13},{2,6},{10,14},{3,7},{11,15},{16,20},{24,... | collective-permute-start | bytes 786440 | tf_op jit(solution)/shard_map/half1/ppermute | solution.py:54
  24.2 18.4 %collective-permute-start.8 = (bf16[512,384]{1,0:T(8,128)(2,1)S(1)}, bf16[512,384]{1,0:T(8,128)(2,1)S(1)}, u32[]{:S(2)}, u32[]{:S(2)}) collective-permute-start(bf16[512,384]{1,0:T(8,128)(2,1)S(1)} %slice.17), channel_id=1, source_target_pairs={{0,4},{8,12},{1,5},{9,13},{2,6},{10,14},{3,7},{11,15},{16,20},{24,... | collective-permute-start | bytes 1179656 | tf_op jit(solution)/shard_map/half0/ppermute | solution.py:54
  40.5 25.4 %collective-permute-start.12 = (bf16[256,2048]{1,0:T(8,128)(2,1)S(1)}, bf16[256,2048]{1,0:T(8,128)(2,1)S(1)}, u32[]{:S(2)}, u32[]{:S(2)}) collective-permute-start(bf16[256,2048]{1,0:T(8,128)(2,1)S(1)} %constant_dynamic-update-slice_fusion.4.own), channel_id=1, source_target_pairs={{0,1},{8,9},{1,2},{9,10},{2,3},{10,11},{3,0},{11,8},{16,17},{24,25... | collective-permute-start | bytes 3145736 | tf_op jit(solution)/shard_map/inputs_up/ppermute | solution.py:54
  40.5 26.8 %collective-permute-start.14 = (bf16[256,2048]{1,0:T(8,128)(2,1)S(1)}, bf16[256,2048]{1,0:T(8,128)(2,1)S(1)}, u32[]{:S(2)}, u32[]{:S(2)}) collective-permute-start(bf16[256,2048]{1,0:T(8,128)(2,1)S(1)} %constant_dynamic-update-slice_fusion.4.own), channel_id=1, source_target_pairs={{0,3},{8,11},{1,0},{9,8},{2,1},{10,9},{3,2},{11,10},{16,19},{24,27... | collective-permute-start | bytes 3145736 | tf_op jit(solution)/shard_map/inputs_down/ppermute | solution.py:54
  52.5 2.0 %collective-permute-start.9 = (bf16[512,512]{1,0:T(8,128)(2,1)S(1)}, bf16[512,512]{1,0:T(8,128)(2,1)S(1)}, u32[]{:S(2)}, u32[]{:S(2)}) collective-permute-start(bf16[512,512]{1,0:T(8,128)(2,1)S(1)} %get-tuple-element.65.a0), channel_id=1, source_target_pairs={{0,8},{8,0},{1,9},{9,1},{2,10},{10,2},{3,11},{11,3},{16,24},{24,16... | collective-permute-start | bytes 1572872 | tf_op jit(solution)/shard_map/swap_dq0/ppermute | solution.py:54
  64.3 3.9 %collective-permute-start.10 = (bf16[512,512]{1,0:T(8,128)(2,1)S(1)}, bf16[512,512]{1,0:T(8,128)(2,1)S(1)}, u32[]{:S(2)}, u32[]{:S(2)}) collective-permute-start(bf16[512,512]{1,0:T(8,128)(2,1)S(1)} %get-tuple-element.67.a1), channel_id=1, source_target_pairs={{0,8},{8,0},{1,9},{9,1},{2,10},{10,2},{3,11},{11,3},{16,24},{24,16... | collective-permute-start | bytes 1572872 | tf_op jit(solution)/shard_map/swap_dq1/ppermute | solution.py:54
  64.6 17.6 %collective-permute-start.11 = (bf16[512,512]{1,0:T(8,128)(2,1)S(1)}, bf16[512,512]{1,0:T(8,128)(2,1)S(1)}, u32[]{:S(2)}, u32[]{:S(2)}) collective-permute-start(bf16[512,512]{1,0:T(8,128)(2,1)S(1)} %pad_maximum_fusion), channel_id=1, source_target_pairs={{4,0},{12,8},{5,1},{13,9},{6,2},{14,10},{7,3},{15,11},{20,16},{28,... | collective-permute-start | bytes 1572872 | tf_op jit(solution)/shard_map/back/ppermute | solution.py:54
  66.0 16.2 %collective-permute-start.13 = (bf16[128,2048]{1,0:T(8,128)(2,1)S(1)}, bf16[128,2048]{1,0:T(8,128)(2,1)S(1)}, u32[]{:S(2)}, u32[]{:S(2)}) collective-permute-start(bf16[128,2048]{1,0:T(8,128)(2,1)S(1)} %slice.18), channel_id=1, source_target_pairs={{0,1},{8,9},{1,2},{9,10},{2,3},{10,11},{3,0},{11,8},{16,17},{24,25... | collective-permute-start | bytes 1572872 | tf_op jit(solution)/shard_map/inputs_up2/ppermute | solution.py:54
  67.3 15.2 %collective-permute-start.15 = (bf16[128,2048]{1,0:T(8,128)(2,1)S(1)}, bf16[128,2048]{1,0:T(8,128)(2,1)S(1)}, u32[]{:S(2)}, u32[]{:S(2)}) collective-permute-start(bf16[128,2048]{1,0:T(8,128)(2,1)S(1)} %slice.19), channel_id=1, source_target_pairs={{0,3},{8,11},{1,0},{9,8},{2,1},{10,9},{3,2},{11,10},{16,19},{24,27... | collective-permute-start | bytes 1572872 | tf_op jit(solution)/shard_map/inputs_down2/ppermute | solution.py:54
  82.6 6.1 %collective-permute-start.16 = (bf16[512,512]{1,0:T(8,128)(2,1)S(1)}, bf16[512,512]{1,0:T(8,128)(2,1)S(1)}, u32[]{:S(2)}, u32[]{:S(2)}) collective-permute-start(bf16[512,512]{1,0:T(8,128)(2,1)S(1)} %fusion.k), channel_id=1, source_target_pairs={{0,8},{8,0},{1,9},{9,1},{2,10},{10,2},{3,11},{11,3},{16,24},{24,16... | collective-permute-start | bytes 1572872 | tf_op jit(solution)/shard_map/swap_dkv/ppermute | solution.py:54
  84.5 13.9 %collective-permute-start.17 = (bf16[768,256]{1,0:T(8,128)(2,1)S(1)}, bf16[768,256]{1,0:T(8,128)(2,1)S(1)}, u32[]{:S(2)}, u32[]{:S(2)}) collective-permute-start(bf16[768,256]{1,0:T(8,128)(2,1)S(1)} %get-tuple-element.77), channel_id=1, source_target_pairs={{0,32},{8,40},{1,33},{9,41},{2,34},{10,42},{3,35},{11,43},{16,48},... | collective-permute-start | bytes 1179656 | tf_op jit(solution)/shard_map/reduce_a_far_up/ppermute | solution.py:54
  86.5 11.9 %collective-permute-start.18 = (bf16[768,256]{1,0:T(8,128)(2,1)S(1)}, bf16[768,256]{1,0:T(8,128)(2,1)S(1)}, u32[]{:S(2)}, u32[]{:S(2)}) collective-permute-start(bf16[768,256]{1,0:T(8,128)(2,1)S(1)} %get-tuple-element.85), channel_id=1, source_target_pairs={{0,96},{8,104},{1,97},{9,105},{2,98},{10,106},{3,99},{11,107},{16,... | collective-permute-start | bytes 1179656 | tf_op jit(solution)/shard_map/reduce_a_far_down/ppermute | solution.py:54
  90.0 14.6 %collective-permute-start.24 = (bf16[384,512]{1,0:T(8,128)(2,1)S(1)}, bf16[384,512]{1,0:T(8,128)(2,1)S(1)}, u32[]{:S(2)}, u32[]{:S(2)}) collective-permute-start(bf16[384,512]{1,0:T(8,128)(2,1)S(1)} %get-tuple-element.80), channel_id=1, source_target_pairs={{0,16},{8,24},{1,17},{9,25},{2,18},{10,26},{3,19},{11,27},{16,4},{... | collective-permute-start | bytes 1179656 | tf_op jit(solution)/shard_map/reduce_b_far_up/ppermute | solution.py:54
  91.5 13.0 %collective-permute-start.25 = (bf16[384,512]{1,0:T(8,128)(2,1)S(1)}, bf16[384,512]{1,0:T(8,128)(2,1)S(1)}, u32[]{:S(2)}, u32[]{:S(2)}) collective-permute-start(bf16[384,512]{1,0:T(8,128)(2,1)S(1)} %get-tuple-element.96), channel_id=1, source_target_pairs={{0,20},{8,28},{1,21},{9,29},{2,22},{10,30},{3,23},{11,31},{16,0},{... | collective-permute-start | bytes 1179656 | tf_op jit(solution)/shard_map/reduce_b_far_down/ppermute | solution.py:54
  98.6 20.6 %collective-permute-start.19 = (bf16[768,512]{1,0:T(8,128)(2,1)S(1)}, bf16[768,512]{1,0:T(8,128)(2,1)S(1)}, u32[]{:S(2)}, u32[]{:S(2)}) collective-permute-start(bf16[768,512]{1,0:T(8,128)(2,1)S(1)} %get-tuple-element.86), channel_id=1, source_target_pairs={{0,32},{8,40},{1,33},{9,41},{2,34},{10,42},{3,35},{11,43},{16,48},... | collective-permute-start | bytes 2359304 | tf_op jit(solution)/shard_map/reduce_a_up/ppermute | solution.py:54
  99.9 19.3 %collective-permute-start.20 = (bf16[768,512]{1,0:T(8,128)(2,1)S(1)}, bf16[768,512]{1,0:T(8,128)(2,1)S(1)}, u32[]{:S(2)}, u32[]{:S(2)}) collective-permute-start(bf16[768,512]{1,0:T(8,128)(2,1)S(1)} %get-tuple-element.87), channel_id=1, source_target_pairs={{0,96},{8,104},{1,97},{9,105},{2,98},{10,106},{3,99},{11,107},{16,... | collective-permute-start | bytes 2359304 | tf_op jit(solution)/shard_map/reduce_a_down/ppermute | solution.py:54
  104.8 23.0 %collective-permute-start.26 = (bf16[384,1024]{1,0:T(8,128)(2,1)S(1)}, bf16[384,1024]{1,0:T(8,128)(2,1)S(1)}, u32[]{:S(2)}, u32[]{:S(2)}) collective-permute-start(bf16[384,1024]{1,0:T(8,128)(2,1)S(1)} %get-tuple-element.97), channel_id=1, source_target_pairs={{0,16},{8,24},{1,17},{9,25},{2,18},{10,26},{3,19},{11,27},{16,4},{... | collective-permute-start | bytes 2359304 | tf_op jit(solution)/shard_map/reduce_b_up/ppermute | solution.py:54
  106.3 21.5 %collective-permute-start.27 = (bf16[384,1024]{1,0:T(8,128)(2,1)S(1)}, bf16[384,1024]{1,0:T(8,128)(2,1)S(1)}, u32[]{:S(2)}, u32[]{:S(2)}) collective-permute-start(bf16[384,1024]{1,0:T(8,128)(2,1)S(1)} %get-tuple-element.98), channel_id=1, source_target_pairs={{0,20},{8,28},{1,21},{9,29},{2,22},{10,30},{3,23},{11,31},{16,0},{... | collective-permute-start | bytes 2359304 | tf_op jit(solution)/shard_map/reduce_b_down/ppermute | solution.py:54
  119.7 11.9 %collective-permute-start.21 = (bf16[384,256]{1,0:T(8,128)(2,1)S(1)}, bf16[384,256]{1,0:T(8,128)(2,1)S(1)}, u32[]{:S(2)}, u32[]{:S(2)}) collective-permute-start(bf16[384,256]{1,0:T(8,128)(2,1)S(1)} %get-tuple-element.89), channel_id=1, source_target_pairs={{0,16},{8,24},{1,17},{9,25},{2,18},{10,26},{3,19},{11,27},{16,4},{... | collective-permute-start | bytes 589832 | tf_op jit(solution)/shard_map/second_a_x1/ppermute | solution.py:54
  121.3 12.9 %collective-permute-start.22 = (bf16[384,256]{1,0:T(8,128)(2,1)S(1)}, bf16[384,256]{1,0:T(8,128)(2,1)S(1)}, u32[]{:S(2)}, u32[]{:S(2)}) collective-permute-start(bf16[384,256]{1,0:T(8,128)(2,1)S(1)} %get-tuple-element.90), channel_id=1, source_target_pairs={{0,20},{8,28},{1,21},{9,29},{2,22},{10,30},{3,23},{11,31},{16,0},{... | collective-permute-start | bytes 589832 | tf_op jit(solution)/shard_map/second_a_x3/ppermute | solution.py:54
  124.4 11.6 %collective-permute-start.23 = (bf16[384,256]{1,0:T(8,128)(2,1)S(1)}, bf16[384,256]{1,0:T(8,128)(2,1)S(1)}, u32[]{:S(2)}, u32[]{:S(2)}) collective-permute-start(bf16[384,256]{1,0:T(8,128)(2,1)S(1)} %get-tuple-element.91), channel_id=1, source_target_pairs={{0,4},{8,12},{1,5},{9,13},{2,6},{10,14},{3,7},{11,15},{16,20},{24,... | collective-permute-start | bytes 589832 | tf_op jit(solution)/shard_map/second_a_x2/ppermute | solution.py:54
  128.3 11.2 %collective-permute-start.28 = (bf16[384,256]{1,0:T(8,128)(2,1)S(1)}, bf16[384,256]{1,0:T(8,128)(2,1)S(1)}, u32[]{:S(2)}, u32[]{:S(2)}) collective-permute-start(bf16[384,256]{1,0:T(8,128)(2,1)S(1)} %get-tuple-element.100), channel_id=1, source_target_pairs={{0,32},{8,40},{1,33},{9,41},{2,34},{10,42},{3,35},{11,43},{16,48},... | collective-permute-start | bytes 589832 | tf_op jit(solution)/shard_map/second_b_z1/ppermute | solution.py:54
  128.4 11.1 %collective-permute-start.29 = (bf16[384,256]{1,0:T(8,128)(2,1)S(1)}, bf16[384,256]{1,0:T(8,128)(2,1)S(1)}, u32[]{:S(2)}, u32[]{:S(2)}) collective-permute-start(bf16[384,256]{1,0:T(8,128)(2,1)S(1)} %get-tuple-element.101), channel_id=1, source_target_pairs={{0,96},{8,104},{1,97},{9,105},{2,98},{10,106},{3,99},{11,107},{16,... | collective-permute-start | bytes 589832 | tf_op jit(solution)/shard_map/second_b_z3/ppermute | solution.py:54
  131.6 7.9 %collective-permute-start.30 = (bf16[384,256]{1,0:T(8,128)(2,1)S(1)}, bf16[384,256]{1,0:T(8,128)(2,1)S(1)}, u32[]{:S(2)}, u32[]{:S(2)}) collective-permute-start(bf16[384,256]{1,0:T(8,128)(2,1)S(1)} %get-tuple-element.102), channel_id=1, source_target_pairs={{0,64},{8,72},{1,65},{9,73},{2,66},{10,74},{3,67},{11,75},{16,80},... | collective-permute-start | bytes 589832 | tf_op jit(solution)/shard_map/second_b_z2/ppermute | solution.py:54

commit v2 on v1

--- a/solution.py
+++ b/solution.py
@@ -80,23 +80,22 @@
 
 
 def pack_heads(queries, keys, values, grads, ids):
-    def pack_heads_body(q, k, v, g, i, k1, k2, k3, k0, q1, q2, q3, sems):
+    def pack_heads_body(q, k, v, g, i, k1, k2, k3, k0, *refs):
+        qs, sems = refs[:6], refs[6]
         y = place()["y"]
         todo = []
-        for d, ko, qo in ((1, k1, q1), (3, k3, q3), (2, k2, q2), (0, k0, None)):
+        for d, o in ((1, k1), (3, k3), (2, k2), (0, k0)):
             for h in range(2):
-                s = h * 4 + lax.rem(y + d, 4)
-                cols = pl.ds(mult(s, 128), 128)
+                cols = pl.ds(mult(h * 4 + lax.rem(y + d, 4), 128), 128)
                 todo += [
-                    (k.at[0, :, cols], ko.at[:, h * 256 : h * 256 + 128]),
-                    (v.at[0, :, cols], ko.at[:, h * 256 + 128 : h * 256 + 256]),
+                    (k.at[0, :, cols], o.at[:, h * 256 : h * 256 + 128]),
+                    (v.at[0, :, cols], o.at[:, h * 256 + 128 : h * 256 + 256]),
                 ]
-                if d:
-                    cols = pl.ds(mult(s, 512), 512)
-                    todo += [
-                        (q.at[0, :, cols], qo.at[:, h * 1024 : h * 1024 + 512]),
-                        (g.at[0, :, cols], qo.at[:, h * 1024 + 512 : h * 1024 + 1024]),
-                    ]
+        for h in range(2):
+            for d in (1, 2, 3):
+                o = qs[h * 3 + d - 1]
+                cols = pl.ds(mult(h * 4 + lax.rem(y + d, 4), 512), 512)
+                todo += [(q.at[0, :, cols], o.at[:, 0:512]), (g.at[0, :, cols], o.at[:, 512:1024])]
         spread = jnp.broadcast_to(i[...].astype(F32), (128, 128)).T.astype(BF16)
         for o in (k1, k2, k3, k0):
             o[:, 512:640] = spread
@@ -104,12 +103,12 @@
 
     return call(
         pack_heads_body,
-        [jax.ShapeDtypeStruct((128, 640), BF16)] * 4 + [jax.ShapeDtypeStruct((128, 2048), BF16)] * 3,
+        [jax.ShapeDtypeStruct((128, 640), BF16)] * 4 + [jax.ShapeDtypeStruct((128, 1024), BF16)] * 6,
         [pltpu.SemaphoreType.DMA((28,))],
         10**8,
         10**6,
         [ANY] * 4 + [VMEM],
-        [VMEM] * 7,
+        [VMEM] * 10,
         BIG,
     )(queries, keys, values, grads, ids)
 
@@ -138,23 +137,34 @@
     )(hidden)
 
 
-def attention(h, queries, grads, own, msgs, keys, before):
-    def attention_body(q, g, kv, q1, q2, q3, k1, k2, k3, pv, pi, dq, dkv, dprev, qs, gs, ks, vs, ids, bias, acck, accv, sems):
+def arrange(h, queries, grads, msgs):
+    def arrange_body(q, g, q1, q2, q3, qs, gs, sems):
+        y = place()["y"]
+        cols, row = pl.ds(mult(h * 4 + y, 512), 512), pl.ds(mult(y, 128), 128)
+        todo = [(q.at[0, :, cols], qs.at[row, :]), (g.at[0, :, cols], gs.at[row, :])]
+        for d, m in ((1, q1), (2, q2), (3, q3)):
+            row = pl.ds(mult(lax.rem(y - d + 4, 4), 128), 128)
+            todo += [(m.at[:, 0:512], qs.at[row, :]), (m.at[:, 512:1024], gs.at[row, :])]
+        run_copies(todo, sems)
+
+    return call(
+        arrange_body,
+        [jax.ShapeDtypeStruct((512, 512), BF16)] * 2,
+        [pltpu.SemaphoreType.DMA((8,))],
+        6 * 10**9,
+        10**6,
+        [ANY] * 5,
+        [VMEM] * 2,
+    )(queries, grads, *msgs)
+
+
+def attention(h, queries, grads, own, keys, before):
+    def attention_body(qs, gs, kv, k1, k2, k3, pv, dq, dkv, dprev, ks, vs, ids, bias, acck, accv, sems):
         here = place()
         y, xh = here["y"], here["xh"]
-        s = h * 4 + y
-        row = mult(y, 128)
-        todo = [
-            (q.at[0, :, pl.ds(mult(s, 512), 512)], qs.at[pl.ds(row, 128), :]),
-            (g.at[0, :, pl.ds(mult(s, 512), 512)], gs.at[pl.ds(row, 128), :]),
-        ]
-        for d, m, k in ((0, None, kv), (1, q1, k1), (2, q2, k2), (3, q3, k3)):
+        todo = []
+        for d, k in ((0, kv), (1, k1), (2, k2), (3, k3)):
             r = mult(lax.rem(y - d + 4, 4), 128)
-            if d:
-                todo += [
-                    (m.at[:, h * 1024 : h * 1024 + 512], qs.at[pl.ds(r, 128), :]),
-                    (m.at[:, h * 1024 + 512 : h * 1024 + 1024], gs.at[pl.ds(r, 128), :]),
-                ]
             todo += [
                 (k.at[:, h * 256 : h * 256 + 128], ks.at[pl.ds(r + 512, 128), :]),
                 (k.at[:, h * 256 + 128 : h * 256 + 256], vs.at[pl.ds(r + 512, 128), :]),
@@ -162,9 +172,9 @@
             ]
             rows = pl.ds(d * 128, 128)
             todo += [
-                (pv.at[rows, 0:128], ks.at[pl.ds(r, 128), :]),
-                (pv.at[rows, 128:256], vs.at[pl.ds(r, 128), :]),
-                (pi.at[rows, 256:384], ids.at[pl.ds(r, 128), :]),
+                (pv.at[rows, h * 256 : h * 256 + 128], ks.at[pl.ds(r, 128), :]),
+                (pv.at[rows, h * 256 + 128 : h * 256 + 256], vs.at[pl.ds(r, 128), :]),
+                (pv.at[rows, 512:640], ids.at[pl.ds(r, 128), :]),
             ]
         run_copies(todo, sems)
 
@@ -212,7 +222,7 @@
                 accv[lo : lo + 768, :] += jnp.dot(p_low, gg, preferred_element_type=F32)
             return 0
 
-        lax.fori_loop(0, 4, head, 0)
+        lax.fori_loop(0, 4, head, 0, unroll=4)
         dkv[0:128, :] = acck[512:1024, :].T
         dkv[128:256, :] = accv[512:1024, :].T
         dprev[0:128, :] = acck[0:512, :].astype(BF16).T
@@ -226,8 +236,6 @@
             jax.ShapeDtypeStruct((256, 512), BF16),
         ],
         [
-            pltpu.VMEM((512, 512), BF16),
-            pltpu.VMEM((512, 512), BF16),
             pltpu.VMEM((1024, 128), BF16),
             pltpu.VMEM((1024, 128), BF16),
             pltpu.VMEM((1024, 128), BF16),
@@ -236,11 +244,11 @@
             pltpu.VMEM((1024, 128), F32),
             pltpu.SemaphoreType.DMA((32,)),
         ],
-        10**9,
-        10**6,
-        [ANY] * 11,
-        [VMEM] * 3,
-    )(queries, grads, own, *msgs, *keys, before[1 - h], before[0])
+        12 * 10**9,
+        10**6,
+        [VMEM] * 2 + [ANY] * 5,
+        [VMEM] * 3,
+    )(queries, grads, own, *keys, before)
 
 
 def gather_a(gt):
@@ -490,35 +498,38 @@
 
 
 def per_device(hidden_in, queries, key_heads, saved_value_heads, out_grads, doc_ids):
-    *kmsg, own, q1, q2, q3 = pack_heads(queries, key_heads, saved_value_heads, out_grads, doc_ids)
+    *kmsg, own, q01, q02, q03, q11, q12, q13 = pack_heads(
+        queries, key_heads, saved_value_heads, out_grads, doc_ids
+    )
     keys = [send("keys_y%d" % (d + 1), m, dy=d + 1) for d, m in enumerate(kmsg)]
     keep, give = pack_inputs(after(hidden_in, own))
     got = send("swap_inputs", give, dc=1)
-    m1 = send("queries_y1", after(q1, keys[0]), dy=1)
-    m3 = send("queries_y3", after(q3, keys[0], keys[2]), dy=3)
-    m2 = send("queries_y2", after(q2, keys[0], keys[2], got), dy=2)
-    msgs = [m1, m2, m3]
-    all_keys = jnp.concatenate([own] + keys, axis=0)
-    before = [
-        send("half0", all_keys[:, 256:640], dx=2, only_half=0),
-        send("half1", all_keys[:, 0:256], dx=2, only_half=0),
-    ]
-    mine = jnp.concatenate([keep, got], axis=0)
-    sent = after(mine, m1, m3)
+    a1 = send("queries0_y1", after(q01, keys[0]), dy=1)
+    a3 = send("queries0_y3", after(q03, keys[0], keys[2]), dy=3)
+    a2 = send("queries0_y2", after(q02, keys[0], keys[2]), dy=2)
+    before = send("half", jnp.concatenate([own] + keys, axis=0), dx=2)
+    b1 = send("queries1_y1", after(q11, a1), dy=1)
+    b3 = send("queries1_y3", after(q13, a1), dy=3)
+    b2 = send("queries1_y2", after(q12, a1, a3), dy=2)
+    sent = after(jnp.concatenate([keep, got], axis=0), a1, a2, a3)
     up = send("inputs_up", sent, dy=1)
     down = send("inputs_down", sent, dy=-1)
 
-    dq0, dkv0, back0 = attention(0, queries, out_grads, own, msgs, keys, before)
+    def attend(h, dep, msgs):
+        qs, gs = arrange(h, after(queries, *dep), out_grads, msgs)
+        return attention(h, qs, gs, own, keys, before)
+
+    dq0, dkv0, back0 = attend(0, (), (a1, a2, a3))
     swap0 = send("swap_dq0", dq0, dc=1)
-    dq1, dkv1, back1 = attention(1, after(queries, dq0, swap0), out_grads, own, msgs, keys, before)
+    dq1, dkv1, back1 = attend(1, (dq0,), (b1, b2, b3))
     fwd = send("inputs_up2", after(up[0:128], dq1), dy=1)
     rev = send("inputs_down2", after(down[128:256], dq1), dy=-1)
     swap1 = send("swap_dq1", dq1, dc=1)
-    ret = send("back", jnp.concatenate([back0, back1], axis=0), dx=2, only_half=1)
+    ret = send("back", jnp.concatenate([back0, back1], axis=0), dx=2)
     ret = after(ret, fwd, rev, swap1).astype(F32)
     low = (jnp.concatenate([dkv0, dkv1], axis=0) + ret).astype(BF16)
     kv = (low, send("swap_dkv", low, dc=1))
-    inputs = (mine, up, down, fwd, rev)
+    inputs = (sent, up, down, fwd, rev)
     gt = (dq0, swap0, dq1, swap1)
 
     ga = gather_a(gt)

time: 141 us -> 136 us (0.965)
  waiting for transfers between devices: 55.4 us -> 50.2 us
  starting transfers between devices: 45.8 us -> 49.3 us
  Pallas kernels: 36.7 us -> 33.8 us
    ppermute x31 -> x33, waiting for transfers between devices: 55.4 us -> 50.2 us  [send(): return lax.ppermute(a, ('grp', 'sp'), pairs(**k))]
    pallas_call x2, Pallas kernels: 19.8 us -> 16.1 us  [attention(): call(attention_body, [jax.ShapeDtypeStruct((512, 512), BF16), jax.ShapeDt...]
    ppermute x31 -> x33, starting transfers between devices: 45.8 us -> 49.3 us  [send(): return lax.ppermute(a, ('grp', 'sp'), pairs(**k))]
  transfers between devices with their start and end apart: 31 -> 33, of which waited for: 12 -> 15; matrix products, arithmetic and copies ran while one was open for 1% -> 0% of each run, Pallas kernels for 23% -> 21%
where the time goes in v2:
time: 136 us; the launch traced here: 135 us
  waiting for transfers between devices  50.2 us (37%)
  starting transfers between devices  49.3 us (36%)
  Pallas kernels  33.8 us (25%)
    ppermute x33, waiting for transfers between devices, send(): return lax.ppermute(a, ('grp', 'sp'), pairs(**k))  50.2 us
    ppermute x33, starting transfers between devices, send(): return lax.ppermute(a, ('grp', 'sp'), pairs(**k))  49.3 us
    pallas_call x2, Pallas kernels, attention(): call(attention_body, [jax.ShapeDtypeStruct((512, 512), BF16), jax.ShapeDt...  16.1 us
    pallas_call x1, Pallas kernels, pack_heads(): call(pack_heads_body, [jax.ShapeDtypeStruct((128, 640), BF16)] * 4 + [jax...  4 us
  transfers between devices with their start and end apart: 33, of which 15 were waited for; matrix products, arithmetic and copies ran while one was open for 0% of the time, Pallas kernels for 21%

profile of v2, /device:TPU:24, one launch (start us, length us, event | category | flops | bytes accessed | tf_op | source)
XLA Modules:
  0.0 134.8 jit_solution(14707866346244282739)
XLA Ops:
  0.6 4.0 %pack_heads_body.1 = (bf16[128,640]{1,0:T(8,128)(2,1)}, bf16[128,640]{1,0:T(8,128)(2,1)}, bf16[128,640]{1,0:T(8,128)(2,1)}, bf16[128,640]{1,0:T(8,128)(2,1)}, bf...) custom-call(bf16[1,128,4096]{2,1,0:T(8,128)(2,1)} %q.3, ...), custom_call_target="tpu_custom_call" | custom-call | flops 100000000 | bytes 1000000 | tf_op jit(solution)/shard_map/pack_heads_body/pallas_call | solution.py:104
  4.6 0.2 collective-permute-start
  4.9 1.9 %collective-permute-start.2 = (bf16[128,640]{1,0:T(8,128)(2,1)}, bf16[128,640]{1,0:T(8,128)(2,1)S(1)}, u32[]{:S(2)}, u32[]{:S(2)}) collective-permute-start(bf16[128,640]{1,0:T(8,128)(2,1)} %get-tuple-element.67), channel_id=1, source_target_pairs={{0,3},{8,11},{1,0},{9,8},{2,1},{10,9},{3,2},{11,10},{16,19},{24,27... | collective-permute-start | bytes 491528 | tf_op jit(solution)/shard_map/keys_y3/ppermute | solution.py:54
  6.7 1.2 collective-permute-start.5
  8.0 4.0 %collective-permute-done.k1 = bf16[128,640]{1,0:T(8,128)(2,1)S(1)} collective-permute-done((bf16[128,640]{1,0:T(8,128)(2,1)}, bf16[128,640]{1,0:T(8,128)(2,1)S(1)}, u32[]{:S(2)}, u32[]{:S(2)}) %collective-permute-start) | collective-permute-done | bytes 163872 | tf_op jit(solution)/shard_map/keys_y1/ppermute | solution.py:54
  12.0 0.3 collective-permute-start.1
  12.4 2.2 %collective-permute-done.2.k3 = bf16[128,640]{1,0:T(8,128)(2,1)S(1)} collective-permute-done((bf16[128,640]{1,0:T(8,128)(2,1)}, bf16[128,640]{1,0:T(8,128)(2,1)S(1)}, u32[]{:S(2)}, u32[]{:S(2)}) %collective-permute-start.2) | collective-permute-done | bytes 163872 | tf_op jit(solution)/shard_map/keys_y3/ppermute | solution.py:54
  14.5 1.4 %collective-permute-start.3 = (bf16[128,1024]{1,0:T(8,128)(2,1)}, bf16[128,1024]{1,0:T(8,128)(2,1)S(1)}, u32[]{:S(2)}, u32[]{:S(2)}) collective-permute-start(bf16[128,1024]{1,0:T(8,128)(2,1)} %get-tuple-element.68), channel_id=1, source_target_pairs={{0,2},{8,10},{1,3},{9,11},{2,0},{10,8},{3,1},{11,9},{16,18},{24,26... | collective-permute-start | bytes 786440 | tf_op jit(solution)/shard_map/queries0_y2/ppermute | solution.py:54
  15.9 2.5 %pack_inputs_body.1 = (bf16[128,2048]{1,0:T(8,128)(2,1)}, bf16[128,2048]{1,0:T(8,128)(2,1)}) custom-call(bf16[1,128,4096]{2,1,0:T(8,128)(2,1)} %x), custom_call_target="tpu_custom_call" | custom-call | flops 1000000000 | bytes 1000000 | tf_op jit(solution)/shard_map/pack_inputs_body/pallas_call | solution.py:128
  18.5 0.1 collective-permute-start.13
  18.6 3.1 %collective-permute-start.6 = (bf16[512,640]{1,0:T(8,128)(2,1)S(1)}, bf16[512,640]{1,0:T(8,128)(2,1)S(1)}, u32[]{:S(2)}, u32[]{:S(2)}) collective-permute-start(bf16[512,640]{1,0:T(8,128)(2,1)S(1)} %pad_maximum_fusion.1), channel_id=1, source_target_pairs={{0,4},{8,12},{1,5},{9,13},{2,6},{10,14},{3,7},{11,15},{16,20},{24,... | collective-permute-start | bytes 1966088 | tf_op jit(solution)/shard_map/half/ppermute | solution.py:54
  21.7 2.6 %collective-permute-start.8 = (bf16[128,1024]{1,0:T(8,128)(2,1)}, bf16[128,1024]{1,0:T(8,128)(2,1)S(1)}, u32[]{:S(2)}, u32[]{:S(2)}) collective-permute-start(bf16[128,1024]{1,0:T(8,128)(2,1)} %get-tuple-element.78), channel_id=1, source_target_pairs={{0,1},{8,9},{1,2},{9,10},{2,3},{10,11},{3,0},{11,8},{16,17},{24,25... | collective-permute-start | bytes 786440 | tf_op jit(solution)/shard_map/queries1_y1/ppermute | solution.py:54
  24.4 3.1 %collective-permute-done.4.q3 = bf16[128,1024]{1,0:T(8,128)(2,1)S(1)} collective-permute-done((bf16[128,1024]{1,0:T(8,128)(2,1)}, bf16[128,1024]{1,0:T(8,128)(2,1)S(1)}, u32[]{:S(2)}, u32[]{:S(2)}) %collective-permute-start.4) | collective-permute-done | bytes 262176 | tf_op jit(solution)/shard_map/queries0_y3/ppermute | solution.py:54
  27.5 0.6 collective-permute-start.10
  28.1 0.2 arrange_body.2
  28.3 0.2 copy-done.3
  28.5 0.1 pad_maximum_fusion.own
  28.6 2.6 %collective-permute-start.14 = (bf16[256,2048]{1,0:T(8,128)(2,1)S(1)}, bf16[256,2048]{1,0:T(8,128)(2,1)S(1)}, u32[]{:S(2)}, u32[]{:S(2)}) collective-permute-start(bf16[256,2048]{1,0:T(8,128)(2,1)S(1)} %pad_maximum_fusion.own), channel_id=1, source_target_pairs={{0,1},{8,9},{1,2},{9,10},{2,3},{10,11},{3,0},{11,8},{16,17},{24,25... | collective-permute-start | bytes 3145736 | tf_op jit(solution)/shard_map/inputs_up/ppermute | solution.py:54
  31.2 6.1 %collective-permute-done.6.pv = bf16[512,640]{1,0:T(8,128)(2,1)S(1)} collective-permute-done((bf16[512,640]{1,0:T(8,128)(2,1)S(1)}, bf16[512,640]{1,0:T(8,128)(2,1)S(1)}, u32[]{:S(2)}, u32[]{:S(2)}) %collective-permute-start.6) | collective-permute-done | bytes 655392 | tf_op jit(solution)/shard_map/half/ppermute | solution.py:54
  37.3 2.7 %collective-permute-start.16 = (bf16[256,2048]{1,0:T(8,128)(2,1)S(1)}, bf16[256,2048]{1,0:T(8,128)(2,1)S(1)}, u32[]{:S(2)}, u32[]{:S(2)}) collective-permute-start(bf16[256,2048]{1,0:T(8,128)(2,1)S(1)} %pad_maximum_fusion.own), channel_id=1, source_target_pairs={{0,3},{8,11},{1,0},{9,8},{2,1},{10,9},{3,2},{11,10},{16,19},{24,27... | collective-permute-start | bytes 3145736 | tf_op jit(solution)/shard_map/inputs_down/ppermute | solution.py:54
  40.0 8.0 %attention_body.2 = (bf16[512,512]{1,0:T(8,128)(2,1)S(1)}, f32[256,512]{1,0:T(8,128)S(1)}, bf16[256,512]{1,0:T(8,128)(2,1)S(1)}) custom-call(bf16[512,512]{1,0:T(8,128)(2,1)S(1)} %get-tuple-element.71.qs, bf16[512,512]{1,0:T(8,128)(2,1)S(1)} %get-tuple-element.72.gs, bf16[128,640]{1,0:T(8,128)(2,1)S(1)} %copy-done.2, ...), custom_call_target="tpu_custom_call" | custom-call | flops 12000000000 | bytes 1000000 | tf_op jit(solution)/shard_map/attention_body/pallas_call | solution.py:231
  48.1 0.5 arrange_body.3
  48.6 8.0 %attention_body.3 = (bf16[512,512]{1,0:T(8,128)(2,1)S(1)}, f32[256,512]{1,0:T(8,128)S(1)}, bf16[256,512]{1,0:T(8,128)(2,1)S(1)}) custom-call(bf16[512,512]{1,0:T(8,128)(2,1)S(1)} %get-tuple-element.83.qs, bf16[512,512]{1,0:T(8,128)(2,1)S(1)} %get-tuple-element.84.gs, bf16[128,640]{1,0:T(8,128)(2,1)S(1)} %copy-done.2, ...), custom_call_target="tpu_custom_call" | custom-call | flops 12000000000 | bytes 1000000 | tf_op jit(solution)/shard_map/attention_body/pallas_call | solution.py:231
  56.6 0.1 collective-permute-start.11
  56.8 3.1 %collective-permute-start.12 = (bf16[512,512]{1,0:T(8,128)(2,1)S(1)}, bf16[512,512]{1,0:T(8,128)(2,1)S(1)}, u32[]{:S(2)}, u32[]{:S(2)}) collective-permute-start(bf16[512,512]{1,0:T(8,128)(2,1)S(1)} %pad_maximum_fusion.2), channel_id=1, source_target_pairs={{0,4},{8,12},{1,5},{9,13},{2,6},{10,14},{3,7},{11,15},{16,20},{24,... | collective-permute-start | bytes 1572872 | tf_op jit(solution)/shard_map/back/ppermute | solution.py:54
  59.9 2.5 %collective-permute-start.15 = (bf16[128,2048]{1,0:T(8,128)(2,1)S(1)}, bf16[128,2048]{1,0:T(8,128)(2,1)S(1)}, u32[]{:S(2)}, u32[]{:S(2)}) collective-permute-start(bf16[128,2048]{1,0:T(8,128)(2,1)S(1)} %slice.8), channel_id=1, source_target_pairs={{0,1},{8,9},{1,2},{9,10},{2,3},{10,11},{3,0},{11,8},{16,17},{24,25... | collective-permute-start | bytes 1572872 | tf_op jit(solution)/shard_map/inputs_up2/ppermute | solution.py:54
  62.4 0.9 collective-permute-done.16.r3
  63.3 1.6 %collective-permute-start.17 = (bf16[128,2048]{1,0:T(8,128)(2,1)S(1)}, bf16[128,2048]{1,0:T(8,128)(2,1)S(1)}, u32[]{:S(2)}, u32[]{:S(2)}) collective-permute-start(bf16[128,2048]{1,0:T(8,128)(2,1)S(1)} %slice.9), channel_id=1, source_target_pairs={{0,3},{8,11},{1,0},{9,8},{2,1},{10,9},{3,2},{11,10},{16,19},{24,27... | collective-permute-start | bytes 1572872 | tf_op jit(solution)/shard_map/inputs_down2/ppermute | solution.py:54
  64.9 7.8 %collective-permute-done.12 = bf16[512,512]{1,0:T(8,128)(2,1)S(1)} collective-permute-done((bf16[512,512]{1,0:T(8,128)(2,1)S(1)}, bf16[512,512]{1,0:T(8,128)(2,1)S(1)}, u32[]{:S(2)}, u32[]{:S(2)}) %collective-permute-start.12) | collective-permute-done | bytes 524320 | tf_op jit(solution)/shard_map/back/ppermute | solution.py:54
  72.7 1.4 %collective-permute-done.15.r2a = bf16[128,2048]{1,0:T(8,128)(2,1)S(1)} collective-permute-done((bf16[128,2048]{1,0:T(8,128)(2,1)S(1)}, bf16[128,2048]{1,0:T(8,128)(2,1)S(1)}, u32[]{:S(2)}, u32[]{:S(2)}) %collective-permute-start.15) | collective-permute-done | bytes 524320 | tf_op jit(solution)/shard_map/inputs_up2/ppermute | solution.py:54
  74.0 3.2 %collective-permute-done.17.r2b = bf16[128,2048]{1,0:T(8,128)(2,1)S(1)} collective-permute-done((bf16[128,2048]{1,0:T(8,128)(2,1)S(1)}, bf16[128,2048]{1,0:T(8,128)(2,1)S(1)}, u32[]{:S(2)}, u32[]{:S(2)}) %collective-permute-start.17) | collective-permute-done | bytes 524320 | tf_op jit(solution)/shard_map/inputs_down2/ppermute | solution.py:54
  77.3 0.2 fusion.k
  77.4 0.1 collective-permute-start.18
  77.5 0.2 gather_a_body.1.g
  77.7 1.4 %far_a_body.1 = (bf16[1024,2048]{1,0:T(8,128)(2,1)S(1)}, bf16[768,256]{1,0:T(8,128)(2,1)S(1)}, bf16[768,256]{1,0:T(8,128)(2,1)S(1)}) custom-call(bf16[768,1024]{1,0:T(8,128)(2,1)S(1)} %gather_a_body.1.g, bf16[256,2048]{1,0:T(8,128)(2,1)S(1)} %pad_maximum_fusion.own, bf16[256,2048]{1,0:T(8,128)(2,1)S(1)} %collective-permute-done.14.r1, ...), custom_call_target="tpu_custom_call" | custom-call | flops 1000000000 | bytes 1000000 | tf_op jit(solution)/shard_map/far_a_body/pallas_call | solution.py:324
  79.1 2.0 %collective-permute-start.19 = (bf16[768,256]{1,0:T(8,128)(2,1)S(1)}, bf16[768,256]{1,0:T(8,128)(2,1)S(1)}, u32[]{:S(2)}, u32[]{:S(2)}) collective-permute-start(bf16[768,256]{1,0:T(8,128)(2,1)S(1)} %get-tuple-element.97), channel_id=1, source_target_pairs={{0,32},{8,40},{1,33},{9,41},{2,34},{10,42},{3,35},{11,43},{16,48},... | collective-permute-start | bytes 1179656 | tf_op jit(solution)/shard_map/reduce_a_far_up/ppermute | solution.py:54
  81.1 2.2 %collective-permute-start.20 = (bf16[768,256]{1,0:T(8,128)(2,1)S(1)}, bf16[768,256]{1,0:T(8,128)(2,1)S(1)}, u32[]{:S(2)}, u32[]{:S(2)}) collective-permute-start(bf16[768,256]{1,0:T(8,128)(2,1)S(1)} %get-tuple-element.105), channel_id=1, source_target_pairs={{0,96},{8,104},{1,97},{9,105},{2,98},{10,106},{3,99},{11,107},{16,... | collective-permute-start | bytes 1179656 | tf_op jit(solution)/shard_map/reduce_a_far_down/ppermute | solution.py:54
  83.3 0.2 gather_b_body.1.g
  83.5 1.0 far_b_body.1
  84.6 1.6 %collective-permute-start.26 = (bf16[384,512]{1,0:T(8,128)(2,1)S(1)}, bf16[384,512]{1,0:T(8,128)(2,1)S(1)}, u32[]{:S(2)}, u32[]{:S(2)}) collective-permute-start(bf16[384,512]{1,0:T(8,128)(2,1)S(1)} %get-tuple-element.100), channel_id=1, source_target_pairs={{0,16},{8,24},{1,17},{9,25},{2,18},{10,26},{3,19},{11,27},{16,4},{... | collective-permute-start | bytes 1179656 | tf_op jit(solution)/shard_map/reduce_b_far_up/ppermute | solution.py:54
  86.1 2.3 %collective-permute-start.27 = (bf16[384,512]{1,0:T(8,128)(2,1)S(1)}, bf16[384,512]{1,0:T(8,128)(2,1)S(1)}, u32[]{:S(2)}, u32[]{:S(2)}) collective-permute-start(bf16[384,512]{1,0:T(8,128)(2,1)S(1)} %get-tuple-element.116), channel_id=1, source_target_pairs={{0,20},{8,28},{1,21},{9,29},{2,22},{10,30},{3,23},{11,31},{16,0},{... | collective-permute-start | bytes 1179656 | tf_op jit(solution)/shard_map/reduce_b_far_down/ppermute | solution.py:54
  88.5 2.6 %near_a_body.1 = (f32[768,512]{1,0:T(8,128)S(1)}, f32[768,512]{1,0:T(8,128)S(1)}, f32[768,512]{1,0:T(8,128)S(1)}) custom-call(bf16[768,1024]{1,0:T(8,128)(2,1)S(1)} %gather_a_body.1.g, bf16[1024,2048]{1,0:T(8,128)(2,1)S(1)} %get-tuple-element.99.x), custom_call_target="tpu_custom_call" | custom-call | flops 1000000000 | bytes 1000000 | tf_op jit(solution)/shard_map/near_a_body/pallas_call | solution.py:363
  91.1 1.9 %collective-permute-done.19.gu = bf16[768,256]{1,0:T(8,128)(2,1)S(1)} collective-permute-done((bf16[768,256]{1,0:T(8,128)(2,1)S(1)}, bf16[768,256]{1,0:T(8,128)(2,1)S(1)}, u32[]{:S(2)}, u32[]{:S(2)}) %collective-permute-start.19) | collective-permute-done | bytes 393248 | tf_op jit(solution)/shard_map/reduce_a_far_up/ppermute | solution.py:54
  93.0 0.2 add_near_body.2
  93.2 1.3 collective-permute-start.21
  94.5 2.0 %collective-permute-start.22 = (bf16[768,512]{1,0:T(8,128)(2,1)S(1)}, bf16[768,512]{1,0:T(8,128)(2,1)S(1)}, u32[]{:S(2)}, u32[]{:S(2)}) collective-permute-start(bf16[768,512]{1,0:T(8,128)(2,1)S(1)} %get-tuple-element.107), channel_id=1, source_target_pairs={{0,96},{8,104},{1,97},{9,105},{2,98},{10,106},{3,99},{11,107},{16,... | collective-permute-start | bytes 2359304 | tf_op jit(solution)/shard_map/reduce_a_down/ppermute | solution.py:54
  96.5 2.6 %near_b_body.1 = (f32[384,1024]{1,0:T(8,128)S(1)}, f32[384,1024]{1,0:T(8,128)S(1)}, f32[384,1024]{1,0:T(8,128)S(1)}) custom-call(bf16[768,1024]{1,0:T(8,128)(2,1)S(1)} %gather_b_body.1.g, bf16[1024,2048]{1,0:T(8,128)(2,1)S(1)} %get-tuple-element.99.x), custom_call_target="tpu_custom_call" | custom-call | flops 1000000000 | bytes 1000000 | tf_op jit(solution)/shard_map/near_b_body/pallas_call | solution.py:379
  99.1 0.2 add_near_body.3
  99.4 1.6 %collective-permute-start.28 = (bf16[384,1024]{1,0:T(8,128)(2,1)S(1)}, bf16[384,1024]{1,0:T(8,128)(2,1)S(1)}, u32[]{:S(2)}, u32[]{:S(2)}) collective-permute-start(bf16[384,1024]{1,0:T(8,128)(2,1)S(1)} %get-tuple-element.117), channel_id=1, source_target_pairs={{0,16},{8,24},{1,17},{9,25},{2,18},{10,26},{3,19},{11,27},{16,4},{... | collective-permute-start | bytes 2359304 | tf_op jit(solution)/shard_map/reduce_b_up/ppermute | solution.py:54
  100.9 2.3 %collective-permute-start.29 = (bf16[384,1024]{1,0:T(8,128)(2,1)S(1)}, bf16[384,1024]{1,0:T(8,128)(2,1)S(1)}, u32[]{:S(2)}, u32[]{:S(2)}) collective-permute-start(bf16[384,1024]{1,0:T(8,128)(2,1)S(1)} %get-tuple-element.118), channel_id=1, source_target_pairs={{0,20},{8,28},{1,21},{9,29},{2,22},{10,30},{3,23},{11,31},{16,0},{... | collective-permute-start | bytes 2359304 | tf_op jit(solution)/shard_map/reduce_b_down/ppermute | solution.py:54
  103.3 10.6 %collective-permute-done.21.refs_1_ = bf16[768,512]{1,0:T(8,128)(2,1)S(1)} collective-permute-done((bf16[768,512]{1,0:T(8,128)(2,1)S(1)}, bf16[768,512]{1,0:T(8,128)(2,1)S(1)}, u32[]{:S(2)}, u32[]{:S(2)}) %collective-permute-start.21) | collective-permute-done | bytes 786464 | tf_op jit(solution)/shard_map/reduce_a_up/ppermute | solution.py:54
  113.9 0.5 add_a_body.1
  114.3 1.6 %collective-permute-start.23 = (bf16[384,256]{1,0:T(8,128)(2,1)S(1)}, bf16[384,256]{1,0:T(8,128)(2,1)S(1)}, u32[]{:S(2)}, u32[]{:S(2)}) collective-permute-start(bf16[384,256]{1,0:T(8,128)(2,1)S(1)} %get-tuple-element.109), channel_id=1, source_target_pairs={{0,16},{8,24},{1,17},{9,25},{2,18},{10,26},{3,19},{11,27},{16,4},{... | collective-permute-start | bytes 589832 | tf_op jit(solution)/shard_map/second_a_x1/ppermute | solution.py:54
  115.9 2.3 %collective-permute-start.24 = (bf16[384,256]{1,0:T(8,128)(2,1)S(1)}, bf16[384,256]{1,0:T(8,128)(2,1)S(1)}, u32[]{:S(2)}, u32[]{:S(2)}) collective-permute-start(bf16[384,256]{1,0:T(8,128)(2,1)S(1)} %get-tuple-element.110), channel_id=1, source_target_pairs={{0,20},{8,28},{1,21},{9,29},{2,22},{10,30},{3,23},{11,31},{16,0},{... | collective-permute-start | bytes 589832 | tf_op jit(solution)/shard_map/second_a_x3/ppermute | solution.py:54
  118.2 2.5 %collective-permute-start.25 = (bf16[384,256]{1,0:T(8,128)(2,1)S(1)}, bf16[384,256]{1,0:T(8,128)(2,1)S(1)}, u32[]{:S(2)}, u32[]{:S(2)}) collective-permute-start(bf16[384,256]{1,0:T(8,128)(2,1)S(1)} %get-tuple-element.111), channel_id=1, source_target_pairs={{0,4},{8,12},{1,5},{9,13},{2,6},{10,14},{3,7},{11,15},{16,20},{24,... | collective-permute-start | bytes 589832 | tf_op jit(solution)/shard_map/second_a_x2/ppermute | solution.py:54
  120.7 0.9 collective-permute-done.28.refs_1_
  121.6 0.6 collective-permute-done.29.refs_2_
  122.2 0.5 add_b_body.1
  122.8 3.2 %collective-permute-start.31 = (bf16[384,256]{1,0:T(8,128)(2,1)S(1)}, bf16[384,256]{1,0:T(8,128)(2,1)S(1)}, u32[]{:S(2)}, u32[]{:S(2)}) collective-permute-start(bf16[384,256]{1,0:T(8,128)(2,1)S(1)} %get-tuple-element.121), channel_id=1, source_target_pairs={{0,96},{8,104},{1,97},{9,105},{2,98},{10,106},{3,99},{11,107},{16,... | collective-permute-start | bytes 589832 | tf_op jit(solution)/shard_map/second_b_z3/ppermute | solution.py:54
  126.0 0.1 collective-permute-start.32
  126.1 0.3 collective-permute-done.24.refs_2_
  126.4 3.4 %collective-permute-done.25.refs_3_ = bf16[384,256]{1,0:T(8,128)(2,1)S(1)} collective-permute-done((bf16[384,256]{1,0:T(8,128)(2,1)S(1)}, bf16[384,256]{1,0:T(8,128)(2,1)S(1)}, u32[]{:S(2)}, u32[]{:S(2)}) %collective-permute-start.25) | collective-permute-done | bytes 196640 | tf_op jit(solution)/shard_map/second_a_x2/ppermute | solution.py:54
  129.8 3.9 %collective-permute-done.30.refs_5_ = bf16[384,256]{1,0:T(8,128)(2,1)S(1)} collective-permute-done((bf16[384,256]{1,0:T(8,128)(2,1)S(1)}, bf16[384,256]{1,0:T(8,128)(2,1)S(1)}, u32[]{:S(2)}, u32[]{:S(2)}) %collective-permute-start.30) | collective-permute-done | bytes 196640 | tf_op jit(solution)/shard_map/second_b_z1/ppermute | solution.py:54
  133.7 1.1 finish_body.1
  (37 shorter events, 0.3 us)
Async XLA Ops:
  4.6 7.4 %collective-permute-start = (bf16[128,640]{1,0:T(8,128)(2,1)}, bf16[128,640]{1,0:T(8,128)(2,1)S(1)}, u32[]{:S(2)}, u32[]{:S(2)}) collective-permute-start(bf16[128,640]{1,0:T(8,128)(2,1)} %get-tuple-element.64), channel_id=1, source_target_pairs={{0,1},{8,9},{1,2},{9,10},{2,3},{10,11},{3,0},{11,8},{16,17},{24,25... | collective-permute-start | bytes 491528 | tf_op jit(solution)/shard_map/keys_y1/ppermute | solution.py:54
  4.9 9.7 %collective-permute-start.2 = (bf16[128,640]{1,0:T(8,128)(2,1)}, bf16[128,640]{1,0:T(8,128)(2,1)S(1)}, u32[]{:S(2)}, u32[]{:S(2)}) collective-permute-start(bf16[128,640]{1,0:T(8,128)(2,1)} %get-tuple-element.67), channel_id=1, source_target_pairs={{0,3},{8,11},{1,0},{9,8},{2,1},{10,9},{3,2},{11,10},{16,19},{24,27... | collective-permute-start | bytes 491528 | tf_op jit(solution)/shard_map/keys_y3/ppermute | solution.py:54
  6.7 11.8 %collective-permute-start.5 = (bf16[128,640]{1,0:T(8,128)(2,1)}, bf16[128,640]{1,0:T(8,128)(2,1)S(1)}, u32[]{:S(2)}, u32[]{:S(2)}) collective-permute-start(bf16[128,640]{1,0:T(8,128)(2,1)} %get-tuple-element.74), channel_id=1, source_target_pairs={{0,2},{8,10},{1,3},{9,11},{2,0},{10,8},{3,1},{11,9},{16,18},{24,26... | collective-permute-start | bytes 491528 | tf_op jit(solution)/shard_map/keys_y2/ppermute | solution.py:54
  12.0 9.7 %collective-permute-start.1 = (bf16[128,1024]{1,0:T(8,128)(2,1)}, bf16[128,1024]{1,0:T(8,128)(2,1)S(1)}, u32[]{:S(2)}, u32[]{:S(2)}) collective-permute-start(bf16[128,1024]{1,0:T(8,128)(2,1)} %get-tuple-element.65), channel_id=1, source_target_pairs={{0,1},{8,9},{1,2},{9,10},{2,3},{10,11},{3,0},{11,8},{16,17},{24,25... | collective-permute-start | bytes 786440 | tf_op jit(solution)/shard_map/queries0_y1/ppermute | solution.py:54
  14.5 12.9 %collective-permute-start.4 = (bf16[128,1024]{1,0:T(8,128)(2,1)}, bf16[128,1024]{1,0:T(8,128)(2,1)S(1)}, u32[]{:S(2)}, u32[]{:S(2)}) collective-permute-start(bf16[128,1024]{1,0:T(8,128)(2,1)} %get-tuple-element.70), channel_id=1, source_target_pairs={{0,3},{8,11},{1,0},{9,8},{2,1},{10,9},{3,2},{11,10},{16,19},{24,27... | collective-permute-start | bytes 786440 | tf_op jit(solution)/shard_map/queries0_y3/ppermute | solution.py:54
  14.5 12.9 %collective-permute-start.3 = (bf16[128,1024]{1,0:T(8,128)(2,1)}, bf16[128,1024]{1,0:T(8,128)(2,1)S(1)}, u32[]{:S(2)}, u32[]{:S(2)}) collective-permute-start(bf16[128,1024]{1,0:T(8,128)(2,1)} %get-tuple-element.68), channel_id=1, source_target_pairs={{0,2},{8,10},{1,3},{9,11},{2,0},{10,8},{3,1},{11,9},{16,18},{24,26... | collective-permute-start | bytes 786440 | tf_op jit(solution)/shard_map/queries0_y2/ppermute | solution.py:54
  15.9 2.7 %copy-start.2 = (bf16[128,640]{1,0:T(8,128)(2,1)S(1)}, bf16[128,640]{1,0:T(8,128)(2,1)}, u32[]{:S(2)}) copy-start(bf16[128,640]{1,0:T(8,128)(2,1)} %get-tuple-element.73.kv) | copy-start | bytes 491524
  15.9 11.6 %copy-start.5 = (bf16[128,1024]{1,0:T(8,128)(2,1)S(1)}, bf16[128,1024]{1,0:T(8,128)(2,1)}, u32[]{:S(2)}) copy-start(bf16[128,1024]{1,0:T(8,128)(2,1)} %get-tuple-element.80) | copy-start | bytes 786436
  15.9 11.6 %copy-start.4 = (bf16[128,1024]{1,0:T(8,128)(2,1)S(1)}, bf16[128,1024]{1,0:T(8,128)(2,1)}, u32[]{:S(2)}) copy-start(bf16[128,1024]{1,0:T(8,128)(2,1)} %get-tuple-element.82) | copy-start | bytes 786436
  15.9 12.2 %copy-start = (bf16[1,128,4096]{2,1,0:T(8,128)(2,1)S(1)}, bf16[1,128,4096]{2,1,0:T(8,128)(2,1)}, u32[]{:S(2)}) copy-start(bf16[1,128,4096]{2,1,0:T(8,128)(2,1)} %q.3) | copy-start | bytes 3145732
  15.9 12.2 %copy-start.1 = (bf16[1,128,4096]{2,1,0:T(8,128)(2,1)S(1)}, bf16[1,128,4096]{2,1,0:T(8,128)(2,1)}, u32[]{:S(2)}) copy-start(bf16[1,128,4096]{2,1,0:T(8,128)(2,1)} %g.5) | copy-start | bytes 3145732
  18.5 9.9 %collective-permute-start.13 = (bf16[128,2048]{1,0:T(8,128)(2,1)}, bf16[128,2048]{1,0:T(8,128)(2,1)S(1)}, u32[]{:S(2)}, u32[]{:S(2)}) collective-permute-start(bf16[128,2048]{1,0:T(8,128)(2,1)} %get-tuple-element.92), channel_id=1, source_target_pairs={{0,8},{8,0},{1,9},{9,1},{2,10},{10,2},{3,11},{11,3},{16,24},{24,16... | collective-permute-start | bytes 1572872 | tf_op jit(solution)/shard_map/swap_inputs/ppermute | solution.py:54
  18.6 18.7 %collective-permute-start.6 = (bf16[512,640]{1,0:T(8,128)(2,1)S(1)}, bf16[512,640]{1,0:T(8,128)(2,1)S(1)}, u32[]{:S(2)}, u32[]{:S(2)}) collective-permute-start(bf16[512,640]{1,0:T(8,128)(2,1)S(1)} %pad_maximum_fusion.1), channel_id=1, source_target_pairs={{0,4},{8,12},{1,5},{9,13},{2,6},{10,14},{3,7},{11,15},{16,20},{24,... | collective-permute-start | bytes 1966088 | tf_op jit(solution)/shard_map/half/ppermute | solution.py:54
  21.7 26.3 %collective-permute-start.8 = (bf16[128,1024]{1,0:T(8,128)(2,1)}, bf16[128,1024]{1,0:T(8,128)(2,1)S(1)}, u32[]{:S(2)}, u32[]{:S(2)}) collective-permute-start(bf16[128,1024]{1,0:T(8,128)(2,1)} %get-tuple-element.78), channel_id=1, source_target_pairs={{0,1},{8,9},{1,2},{9,10},{2,3},{10,11},{3,0},{11,8},{16,17},{24,25... | collective-permute-start | bytes 786440 | tf_op jit(solution)/shard_map/queries1_y1/ppermute | solution.py:54
  27.5 20.6 %collective-permute-start.9 = (bf16[128,1024]{1,0:T(8,128)(2,1)S(1)}, bf16[128,1024]{1,0:T(8,128)(2,1)S(1)}, u32[]{:S(2)}, u32[]{:S(2)}) collective-permute-start(bf16[128,1024]{1,0:T(8,128)(2,1)S(1)} %copy-done.5), channel_id=1, source_target_pairs={{0,2},{8,10},{1,3},{9,11},{2,0},{10,8},{3,1},{11,9},{16,18},{24,26... | collective-permute-start | bytes 786440 | tf_op jit(solution)/shard_map/queries1_y2/ppermute | solution.py:54
  27.5 1.0 copy-start.3
  27.5 20.6 %collective-permute-start.10 = (bf16[128,1024]{1,0:T(8,128)(2,1)S(1)}, bf16[128,1024]{1,0:T(8,128)(2,1)S(1)}, u32[]{:S(2)}, u32[]{:S(2)}) collective-permute-start(bf16[128,1024]{1,0:T(8,128)(2,1)S(1)} %copy-done.4), channel_id=1, source_target_pairs={{0,3},{8,11},{1,0},{9,8},{2,1},{10,9},{3,2},{11,10},{16,19},{24,27... | collective-permute-start | bytes 786440 | tf_op jit(solution)/shard_map/queries1_y3/ppermute | solution.py:54
  28.6 31.3 %collective-permute-start.14 = (bf16[256,2048]{1,0:T(8,128)(2,1)S(1)}, bf16[256,2048]{1,0:T(8,128)(2,1)S(1)}, u32[]{:S(2)}, u32[]{:S(2)}) collective-permute-start(bf16[256,2048]{1,0:T(8,128)(2,1)S(1)} %pad_maximum_fusion.own), channel_id=1, source_target_pairs={{0,1},{8,9},{1,2},{9,10},{2,3},{10,11},{3,0},{11,8},{16,17},{24,25... | collective-permute-start | bytes 3145736 | tf_op jit(solution)/shard_map/inputs_up/ppermute | solution.py:54
  37.3 26.0 %collective-permute-start.16 = (bf16[256,2048]{1,0:T(8,128)(2,1)S(1)}, bf16[256,2048]{1,0:T(8,128)(2,1)S(1)}, u32[]{:S(2)}, u32[]{:S(2)}) collective-permute-start(bf16[256,2048]{1,0:T(8,128)(2,1)S(1)} %pad_maximum_fusion.own), channel_id=1, source_target_pairs={{0,3},{8,11},{1,0},{9,8},{2,1},{10,9},{3,2},{11,10},{16,19},{24,27... | collective-permute-start | bytes 3145736 | tf_op jit(solution)/shard_map/inputs_down/ppermute | solution.py:54
  56.6 8.3 %collective-permute-start.11 = (bf16[512,512]{1,0:T(8,128)(2,1)S(1)}, bf16[512,512]{1,0:T(8,128)(2,1)S(1)}, u32[]{:S(2)}, u32[]{:S(2)}) collective-permute-start(bf16[512,512]{1,0:T(8,128)(2,1)S(1)} %get-tuple-element.85.a1), channel_id=1, source_target_pairs={{0,8},{8,0},{1,9},{9,1},{2,10},{10,2},{3,11},{11,3},{16,24},{24,16... | collective-permute-start | bytes 1572872 | tf_op jit(solution)/shard_map/swap_dq1/ppermute | solution.py:54
  56.8 15.9 %collective-permute-start.12 = (bf16[512,512]{1,0:T(8,128)(2,1)S(1)}, bf16[512,512]{1,0:T(8,128)(2,1)S(1)}, u32[]{:S(2)}, u32[]{:S(2)}) collective-permute-start(bf16[512,512]{1,0:T(8,128)(2,1)S(1)} %pad_maximum_fusion.2), channel_id=1, source_target_pairs={{0,4},{8,12},{1,5},{9,13},{2,6},{10,14},{3,7},{11,15},{16,20},{24,... | collective-permute-start | bytes 1572872 | tf_op jit(solution)/shard_map/back/ppermute | solution.py:54
  59.9 14.1 %collective-permute-start.15 = (bf16[128,2048]{1,0:T(8,128)(2,1)S(1)}, bf16[128,2048]{1,0:T(8,128)(2,1)S(1)}, u32[]{:S(2)}, u32[]{:S(2)}) collective-permute-start(bf16[128,2048]{1,0:T(8,128)(2,1)S(1)} %slice.8), channel_id=1, source_target_pairs={{0,1},{8,9},{1,2},{9,10},{2,3},{10,11},{3,0},{11,8},{16,17},{24,25... | collective-permute-start | bytes 1572872 | tf_op jit(solution)/shard_map/inputs_up2/ppermute | solution.py:54
  63.3 13.9 %collective-permute-start.17 = (bf16[128,2048]{1,0:T(8,128)(2,1)S(1)}, bf16[128,2048]{1,0:T(8,128)(2,1)S(1)}, u32[]{:S(2)}, u32[]{:S(2)}) collective-permute-start(bf16[128,2048]{1,0:T(8,128)(2,1)S(1)} %slice.9), channel_id=1, source_target_pairs={{0,3},{8,11},{1,0},{9,8},{2,1},{10,9},{3,2},{11,10},{16,19},{24,27... | collective-permute-start | bytes 1572872 | tf_op jit(solution)/shard_map/inputs_down2/ppermute | solution.py:54
  64.9 12.6 %collective-permute-start.7 = (bf16[512,512]{1,0:T(8,128)(2,1)S(1)}, bf16[512,512]{1,0:T(8,128)(2,1)S(1)}, u32[]{:S(2)}, u32[]{:S(2)}) collective-permute-start(bf16[512,512]{1,0:T(8,128)(2,1)S(1)} %get-tuple-element.75.a0), channel_id=1, source_target_pairs={{0,8},{8,0},{1,9},{9,1},{2,10},{10,2},{3,11},{11,3},{16,24},{24,16... | collective-permute-start | bytes 1572872 | tf_op jit(solution)/shard_map/swap_dq0/ppermute | solution.py:54
  77.4 5.9 %collective-permute-start.18 = (bf16[512,512]{1,0:T(8,128)(2,1)S(1)}, bf16[512,512]{1,0:T(8,128)(2,1)S(1)}, u32[]{:S(2)}, u32[]{:S(2)}) collective-permute-start(bf16[512,512]{1,0:T(8,128)(2,1)S(1)} %fusion.k), channel_id=1, source_target_pairs={{0,8},{8,0},{1,9},{9,1},{2,10},{10,2},{3,11},{11,3},{16,24},{24,16... | collective-permute-start | bytes 1572872 | tf_op jit(solution)/shard_map/swap_dkv/ppermute | solution.py:54
  79.1 13.9 %collective-permute-start.19 = (bf16[768,256]{1,0:T(8,128)(2,1)S(1)}, bf16[768,256]{1,0:T(8,128)(2,1)S(1)}, u32[]{:S(2)}, u32[]{:S(2)}) collective-permute-start(bf16[768,256]{1,0:T(8,128)(2,1)S(1)} %get-tuple-element.97), channel_id=1, source_target_pairs={{0,32},{8,40},{1,33},{9,41},{2,34},{10,42},{3,35},{11,43},{16,48},... | collective-permute-start | bytes 1179656 | tf_op jit(solution)/shard_map/reduce_a_far_up/ppermute | solution.py:54
  81.1 11.9 %collective-permute-start.20 = (bf16[768,256]{1,0:T(8,128)(2,1)S(1)}, bf16[768,256]{1,0:T(8,128)(2,1)S(1)}, u32[]{:S(2)}, u32[]{:S(2)}) collective-permute-start(bf16[768,256]{1,0:T(8,128)(2,1)S(1)} %get-tuple-element.105), channel_id=1, source_target_pairs={{0,96},{8,104},{1,97},{9,105},{2,98},{10,106},{3,99},{11,107},{16,... | collective-permute-start | bytes 1179656 | tf_op jit(solution)/shard_map/reduce_a_far_down/ppermute | solution.py:54
  84.6 14.6 %collective-permute-start.26 = (bf16[384,512]{1,0:T(8,128)(2,1)S(1)}, bf16[384,512]{1,0:T(8,128)(2,1)S(1)}, u32[]{:S(2)}, u32[]{:S(2)}) collective-permute-start(bf16[384,512]{1,0:T(8,128)(2,1)S(1)} %get-tuple-element.100), channel_id=1, source_target_pairs={{0,16},{8,24},{1,17},{9,25},{2,18},{10,26},{3,19},{11,27},{16,4},{... | collective-permute-start | bytes 1179656 | tf_op jit(solution)/shard_map/reduce_b_far_up/ppermute | solution.py:54
  86.1 13.0 %collective-permute-start.27 = (bf16[384,512]{1,0:T(8,128)(2,1)S(1)}, bf16[384,512]{1,0:T(8,128)(2,1)S(1)}, u32[]{:S(2)}, u32[]{:S(2)}) collective-permute-start(bf16[384,512]{1,0:T(8,128)(2,1)S(1)} %get-tuple-element.116), channel_id=1, source_target_pairs={{0,20},{8,28},{1,21},{9,29},{2,22},{10,30},{3,23},{11,31},{16,0},{... | collective-permute-start | bytes 1179656 | tf_op jit(solution)/shard_map/reduce_b_far_down/ppermute | solution.py:54
  93.2 20.6 %collective-permute-start.21 = (bf16[768,512]{1,0:T(8,128)(2,1)S(1)}, bf16[768,512]{1,0:T(8,128)(2,1)S(1)}, u32[]{:S(2)}, u32[]{:S(2)}) collective-permute-start(bf16[768,512]{1,0:T(8,128)(2,1)S(1)} %get-tuple-element.106), channel_id=1, source_target_pairs={{0,32},{8,40},{1,33},{9,41},{2,34},{10,42},{3,35},{11,43},{16,48},... | collective-permute-start | bytes 2359304 | tf_op jit(solution)/shard_map/reduce_a_up/ppermute | solution.py:54
  94.5 19.3 %collective-permute-start.22 = (bf16[768,512]{1,0:T(8,128)(2,1)S(1)}, bf16[768,512]{1,0:T(8,128)(2,1)S(1)}, u32[]{:S(2)}, u32[]{:S(2)}) collective-permute-start(bf16[768,512]{1,0:T(8,128)(2,1)S(1)} %get-tuple-element.107), channel_id=1, source_target_pairs={{0,96},{8,104},{1,97},{9,105},{2,98},{10,106},{3,99},{11,107},{16,... | collective-permute-start | bytes 2359304 | tf_op jit(solution)/shard_map/reduce_a_down/ppermute | solution.py:54
  99.4 22.2 %collective-permute-start.28 = (bf16[384,1024]{1,0:T(8,128)(2,1)S(1)}, bf16[384,1024]{1,0:T(8,128)(2,1)S(1)}, u32[]{:S(2)}, u32[]{:S(2)}) collective-permute-start(bf16[384,1024]{1,0:T(8,128)(2,1)S(1)} %get-tuple-element.117), channel_id=1, source_target_pairs={{0,16},{8,24},{1,17},{9,25},{2,18},{10,26},{3,19},{11,27},{16,4},{... | collective-permute-start | bytes 2359304 | tf_op jit(solution)/shard_map/reduce_b_up/ppermute | solution.py:54
  100.9 21.3 %collective-permute-start.29 = (bf16[384,1024]{1,0:T(8,128)(2,1)S(1)}, bf16[384,1024]{1,0:T(8,128)(2,1)S(1)}, u32[]{:S(2)}, u32[]{:S(2)}) collective-permute-start(bf16[384,1024]{1,0:T(8,128)(2,1)S(1)} %get-tuple-element.118), channel_id=1, source_target_pairs={{0,20},{8,28},{1,21},{9,29},{2,22},{10,30},{3,23},{11,31},{16,0},{... | collective-permute-start | bytes 2359304 | tf_op jit(solution)/shard_map/reduce_b_down/ppermute | solution.py:54
  114.3 11.7 %collective-permute-start.23 = (bf16[384,256]{1,0:T(8,128)(2,1)S(1)}, bf16[384,256]{1,0:T(8,128)(2,1)S(1)}, u32[]{:S(2)}, u32[]{:S(2)}) collective-permute-start(bf16[384,256]{1,0:T(8,128)(2,1)S(1)} %get-tuple-element.109), channel_id=1, source_target_pairs={{0,16},{8,24},{1,17},{9,25},{2,18},{10,26},{3,19},{11,27},{16,4},{... | collective-permute-start | bytes 589832 | tf_op jit(solution)/shard_map/second_a_x1/ppermute | solution.py:54
  115.9 10.5 %collective-permute-start.24 = (bf16[384,256]{1,0:T(8,128)(2,1)S(1)}, bf16[384,256]{1,0:T(8,128)(2,1)S(1)}, u32[]{:S(2)}, u32[]{:S(2)}) collective-permute-start(bf16[384,256]{1,0:T(8,128)(2,1)S(1)} %get-tuple-element.110), channel_id=1, source_target_pairs={{0,20},{8,28},{1,21},{9,29},{2,22},{10,30},{3,23},{11,31},{16,0},{... | collective-permute-start | bytes 589832 | tf_op jit(solution)/shard_map/second_a_x3/ppermute | solution.py:54
  118.2 11.6 %collective-permute-start.25 = (bf16[384,256]{1,0:T(8,128)(2,1)S(1)}, bf16[384,256]{1,0:T(8,128)(2,1)S(1)}, u32[]{:S(2)}, u32[]{:S(2)}) collective-permute-start(bf16[384,256]{1,0:T(8,128)(2,1)S(1)} %get-tuple-element.111), channel_id=1, source_target_pairs={{0,4},{8,12},{1,5},{9,13},{2,6},{10,14},{3,7},{11,15},{16,20},{24,... | collective-permute-start | bytes 589832 | tf_op jit(solution)/shard_map/second_a_x2/ppermute | solution.py:54
  122.7 11.0 %collective-permute-start.30 = (bf16[384,256]{1,0:T(8,128)(2,1)S(1)}, bf16[384,256]{1,0:T(8,128)(2,1)S(1)}, u32[]{:S(2)}, u32[]{:S(2)}) collective-permute-start(bf16[384,256]{1,0:T(8,128)(2,1)S(1)} %get-tuple-element.120), channel_id=1, source_target_pairs={{0,32},{8,40},{1,33},{9,41},{2,34},{10,42},{3,35},{11,43},{16,48},... | collective-permute-start | bytes 589832 | tf_op jit(solution)/shard_map/second_b_z1/ppermute | solution.py:54
  122.8 11.0 %collective-permute-start.31 = (bf16[384,256]{1,0:T(8,128)(2,1)S(1)}, bf16[384,256]{1,0:T(8,128)(2,1)S(1)}, u32[]{:S(2)}, u32[]{:S(2)}) collective-permute-start(bf16[384,256]{1,0:T(8,128)(2,1)S(1)} %get-tuple-element.121), channel_id=1, source_target_pairs={{0,96},{8,104},{1,97},{9,105},{2,98},{10,106},{3,99},{11,107},{16,... | collective-permute-start | bytes 589832 | tf_op jit(solution)/shard_map/second_b_z3/ppermute | solution.py:54
  126.0 7.7 %collective-permute-start.32 = (bf16[384,256]{1,0:T(8,128)(2,1)S(1)}, bf16[384,256]{1,0:T(8,128)(2,1)S(1)}, u32[]{:S(2)}, u32[]{:S(2)}) collective-permute-start(bf16[384,256]{1,0:T(8,128)(2,1)S(1)} %get-tuple-element.122), channel_id=1, source_target_pairs={{0,64},{8,72},{1,65},{9,73},{2,66},{10,74},{3,67},{11,75},{16,80},... | collective-permute-start | bytes 589832 | tf_op jit(solution)/shard_map/second_b_z2/ppermute | solution.py:54

commit v3 on v2

--- a/solution.py
+++ b/solution.py
@@ -504,9 +504,9 @@
     keys = [send("keys_y%d" % (d + 1), m, dy=d + 1) for d, m in enumerate(kmsg)]
     keep, give = pack_inputs(after(hidden_in, own))
     got = send("swap_inputs", give, dc=1)
-    a1 = send("queries0_y1", after(q01, keys[0]), dy=1)
-    a3 = send("queries0_y3", after(q03, keys[0], keys[2]), dy=3)
-    a2 = send("queries0_y2", after(q02, keys[0], keys[2]), dy=2)
+    a1 = send("queries0_y1", q01, dy=1)
+    a3 = send("queries0_y3", q03, dy=3)
+    a2 = send("queries0_y2", q02, dy=2)
     before = send("half", jnp.concatenate([own] + keys, axis=0), dx=2)
     b1 = send("queries1_y1", after(q11, a1), dy=1)
     b3 = send("queries1_y3", after(q13, a1), dy=3)

time: 136 us -> 134 us (0.985)
  no operation moved by 1% of the time
where the time goes in v3:
time: 134 us
  waiting for transfers between devices  49.4 us (37%)
  starting transfers between devices  49.3 us (37%)
  Pallas kernels  33.8 us (25%)
    ppermute x33, waiting for transfers between devices, send(): return lax.ppermute(a, ('grp', 'sp'), pairs(**k))  49.4 us
    ppermute x33, starting transfers between devices, send(): return lax.ppermute(a, ('grp', 'sp'), pairs(**k))  49.3 us
    pallas_call x2, Pallas kernels, attention(): call(attention_body, [jax.ShapeDtypeStruct((512, 512), BF16), jax.ShapeDt...  16 us
    pallas_call x1, Pallas kernels, pack_heads(): call(pack_heads_body, [jax.ShapeDtypeStruct((128, 640), BF16)] * 4 + [jax...  4 us
  transfers between devices with their start and end apart: 33, of which 15 were waited for; matrix products, arithmetic and copies ran while one was open for 0% of the time, Pallas kernels for 21%

profile of v3, /device:TPU:24, one launch (start us, length us, event | category | flops | bytes accessed | tf_op | source)
XLA Modules:
  0.0 134.0 jit_solution(16164845026343484957)
XLA Ops:
  0.6 4.0 %pack_heads_body.1 = (bf16[128,640]{1,0:T(8,128)(2,1)}, bf16[128,640]{1,0:T(8,128)(2,1)}, bf16[128,640]{1,0:T(8,128)(2,1)}, bf16[128,640]{1,0:T(8,128)(2,1)}, bf...) custom-call(bf16[1,128,4096]{2,1,0:T(8,128)(2,1)} %q.3, ...), custom_call_target="tpu_custom_call" | custom-call | flops 100000000 | bytes 1000000 | tf_op jit(solution)/shard_map/pack_heads_body/pallas_call | solution.py:104
  4.6 0.2 collective-permute-start.3
  4.9 2.7 %collective-permute-start.4 = (bf16[128,640]{1,0:T(8,128)(2,1)}, bf16[128,640]{1,0:T(8,128)(2,1)S(1)}, u32[]{:S(2)}, u32[]{:S(2)}) collective-permute-start(bf16[128,640]{1,0:T(8,128)(2,1)} %get-tuple-element.67), channel_id=1, source_target_pairs={{0,2},{8,10},{1,3},{9,11},{2,0},{10,8},{3,1},{11,9},{16,18},{24,26... | collective-permute-start | bytes 491528 | tf_op jit(solution)/shard_map/keys_y2/ppermute | solution.py:54
  7.5 3.2 %collective-permute-start = (bf16[128,1024]{1,0:T(8,128)(2,1)}, bf16[128,1024]{1,0:T(8,128)(2,1)S(1)}, u32[]{:S(2)}, u32[]{:S(2)}) collective-permute-start(bf16[128,1024]{1,0:T(8,128)(2,1)} %get-tuple-element.60), channel_id=1, source_target_pairs={{0,1},{8,9},{1,2},{9,10},{2,3},{10,11},{3,0},{11,8},{16,17},{24,25... | collective-permute-start | bytes 786440 | tf_op jit(solution)/shard_map/queries0_y1/ppermute | solution.py:54
  10.8 1.2 collective-permute-done.3.k1
  12.0 3.1 %collective-permute-start.1 = (bf16[128,1024]{1,0:T(8,128)(2,1)}, bf16[128,1024]{1,0:T(8,128)(2,1)S(1)}, u32[]{:S(2)}, u32[]{:S(2)}) collective-permute-start(bf16[128,1024]{1,0:T(8,128)(2,1)} %get-tuple-element.61), channel_id=1, source_target_pairs={{0,2},{8,10},{1,3},{9,11},{2,0},{10,8},{3,1},{11,9},{16,18},{24,26... | collective-permute-start | bytes 786440 | tf_op jit(solution)/shard_map/queries0_y2/ppermute | solution.py:54
  15.1 2.5 %pack_inputs_body.1 = (bf16[128,2048]{1,0:T(8,128)(2,1)}, bf16[128,2048]{1,0:T(8,128)(2,1)}) custom-call(bf16[1,128,4096]{2,1,0:T(8,128)(2,1)} %x), custom_call_target="tpu_custom_call" | custom-call | flops 1000000000 | bytes 1000000 | tf_op jit(solution)/shard_map/pack_inputs_body/pallas_call | solution.py:128
  17.6 0.1 collective-permute-start.13
  17.7 0.1 pad_maximum_fusion.1
  17.8 3.1 %collective-permute-start.6 = (bf16[512,640]{1,0:T(8,128)(2,1)S(1)}, bf16[512,640]{1,0:T(8,128)(2,1)S(1)}, u32[]{:S(2)}, u32[]{:S(2)}) collective-permute-start(bf16[512,640]{1,0:T(8,128)(2,1)S(1)} %pad_maximum_fusion.1), channel_id=1, source_target_pairs={{0,4},{8,12},{1,5},{9,13},{2,6},{10,14},{3,7},{11,15},{16,20},{24,... | collective-permute-start | bytes 1966088 | tf_op jit(solution)/shard_map/half/ppermute | solution.py:54
  20.9 0.3 collective-permute-done.q1
  21.2 3.2 %collective-permute-start.8 = (bf16[128,1024]{1,0:T(8,128)(2,1)}, bf16[128,1024]{1,0:T(8,128)(2,1)S(1)}, u32[]{:S(2)}, u32[]{:S(2)}) collective-permute-start(bf16[128,1024]{1,0:T(8,128)(2,1)} %get-tuple-element.72), channel_id=1, source_target_pairs={{0,1},{8,9},{1,2},{9,10},{2,3},{10,11},{3,0},{11,8},{16,17},{24,25... | collective-permute-start | bytes 786440 | tf_op jit(solution)/shard_map/queries1_y1/ppermute | solution.py:54
  24.4 2.8 %collective-permute-done.1.q2 = bf16[128,1024]{1,0:T(8,128)(2,1)S(1)} collective-permute-done((bf16[128,1024]{1,0:T(8,128)(2,1)}, bf16[128,1024]{1,0:T(8,128)(2,1)S(1)}, u32[]{:S(2)}, u32[]{:S(2)}) %collective-permute-start.1) | collective-permute-done | bytes 262176 | tf_op jit(solution)/shard_map/queries0_y2/ppermute | solution.py:54
  27.2 0.3 arrange_body.2
  27.5 0.1 pad_maximum_fusion.own
  27.6 3.3 %collective-permute-start.14 = (bf16[256,2048]{1,0:T(8,128)(2,1)S(1)}, bf16[256,2048]{1,0:T(8,128)(2,1)S(1)}, u32[]{:S(2)}, u32[]{:S(2)}) collective-permute-start(bf16[256,2048]{1,0:T(8,128)(2,1)S(1)} %pad_maximum_fusion.own), channel_id=1, source_target_pairs={{0,1},{8,9},{1,2},{9,10},{2,3},{10,11},{3,0},{11,8},{16,17},{24,25... | collective-permute-start | bytes 3145736 | tf_op jit(solution)/shard_map/inputs_up/ppermute | solution.py:54
  30.9 5.6 %collective-permute-done.6.pv = bf16[512,640]{1,0:T(8,128)(2,1)S(1)} collective-permute-done((bf16[512,640]{1,0:T(8,128)(2,1)S(1)}, bf16[512,640]{1,0:T(8,128)(2,1)S(1)}, u32[]{:S(2)}, u32[]{:S(2)}) %collective-permute-start.6) | collective-permute-done | bytes 655392 | tf_op jit(solution)/shard_map/half/ppermute | solution.py:54
  36.5 0.8 collective-permute-start.16
  37.3 8.0 %attention_body.2 = (bf16[512,512]{1,0:T(8,128)(2,1)S(1)}, f32[256,512]{1,0:T(8,128)S(1)}, bf16[256,512]{1,0:T(8,128)(2,1)S(1)}) custom-call(bf16[512,512]{1,0:T(8,128)(2,1)S(1)} %get-tuple-element.63.qs, bf16[512,512]{1,0:T(8,128)(2,1)S(1)} %get-tuple-element.64.gs, bf16[128,640]{1,0:T(8,128)(2,1)S(1)} %copy-done.2, ...), custom_call_target="tpu_custom_call" | custom-call | flops 12000000000 | bytes 1000000 | tf_op jit(solution)/shard_map/attention_body/pallas_call | solution.py:231
  45.4 0.5 arrange_body.3
  45.9 8.0 %attention_body.3 = (bf16[512,512]{1,0:T(8,128)(2,1)S(1)}, f32[256,512]{1,0:T(8,128)S(1)}, bf16[256,512]{1,0:T(8,128)(2,1)S(1)}) custom-call(bf16[512,512]{1,0:T(8,128)(2,1)S(1)} %get-tuple-element.77.qs, bf16[512,512]{1,0:T(8,128)(2,1)S(1)} %get-tuple-element.78.gs, bf16[128,640]{1,0:T(8,128)(2,1)S(1)} %copy-done.2, ...), custom_call_target="tpu_custom_call" | custom-call | flops 12000000000 | bytes 1000000 | tf_op jit(solution)/shard_map/attention_body/pallas_call | solution.py:231
  53.9 0.1 collective-permute-start.11
  54.0 3.1 %collective-permute-start.12 = (bf16[512,512]{1,0:T(8,128)(2,1)S(1)}, bf16[512,512]{1,0:T(8,128)(2,1)S(1)}, u32[]{:S(2)}, u32[]{:S(2)}) collective-permute-start(bf16[512,512]{1,0:T(8,128)(2,1)S(1)} %pad_maximum_fusion.2), channel_id=1, source_target_pairs={{0,4},{8,12},{1,5},{9,13},{2,6},{10,14},{3,7},{11,15},{16,20},{24,... | collective-permute-start | bytes 1572872 | tf_op jit(solution)/shard_map/back/ppermute | solution.py:54
  57.1 2.3 %collective-permute-done.14.r1 = bf16[256,2048]{1,0:T(8,128)(2,1)S(1)} collective-permute-done((bf16[256,2048]{1,0:T(8,128)(2,1)S(1)}, bf16[256,2048]{1,0:T(8,128)(2,1)S(1)}, u32[]{:S(2)}, u32[]{:S(2)}) %collective-permute-start.14) | collective-permute-done | bytes 1048608 | tf_op jit(solution)/shard_map/inputs_up/ppermute | solution.py:54
  59.5 3.4 %collective-permute-start.15 = (bf16[128,2048]{1,0:T(8,128)(2,1)S(1)}, bf16[128,2048]{1,0:T(8,128)(2,1)S(1)}, u32[]{:S(2)}, u32[]{:S(2)}) collective-permute-start(bf16[128,2048]{1,0:T(8,128)(2,1)S(1)} %slice.8), channel_id=1, source_target_pairs={{0,1},{8,9},{1,2},{9,10},{2,3},{10,11},{3,0},{11,8},{16,17},{24,25... | collective-permute-start | bytes 1572872 | tf_op jit(solution)/shard_map/inputs_up2/ppermute | solution.py:54
  62.9 0.1 collective-permute-done.16.r3
  63.0 0.1 collective-permute-start.17
  63.1 0.1 collective-permute-start.7
  63.2 6.7 %collective-permute-done.12 = bf16[512,512]{1,0:T(8,128)(2,1)S(1)} collective-permute-done((bf16[512,512]{1,0:T(8,128)(2,1)S(1)}, bf16[512,512]{1,0:T(8,128)(2,1)S(1)}, u32[]{:S(2)}, u32[]{:S(2)}) %collective-permute-start.12) | collective-permute-done | bytes 524320 | tf_op jit(solution)/shard_map/back/ppermute | solution.py:54
  69.9 4.0 %collective-permute-done.15.r2a = bf16[128,2048]{1,0:T(8,128)(2,1)S(1)} collective-permute-done((bf16[128,2048]{1,0:T(8,128)(2,1)S(1)}, bf16[128,2048]{1,0:T(8,128)(2,1)S(1)}, u32[]{:S(2)}, u32[]{:S(2)}) %collective-permute-start.15) | collective-permute-done | bytes 524320 | tf_op jit(solution)/shard_map/inputs_up2/ppermute | solution.py:54
  74.0 3.5 %collective-permute-done.17.r2b = bf16[128,2048]{1,0:T(8,128)(2,1)S(1)} collective-permute-done((bf16[128,2048]{1,0:T(8,128)(2,1)S(1)}, bf16[128,2048]{1,0:T(8,128)(2,1)S(1)}, u32[]{:S(2)}, u32[]{:S(2)}) %collective-permute-start.17) | collective-permute-done | bytes 524320 | tf_op jit(solution)/shard_map/inputs_down2/ppermute | solution.py:54
  77.5 0.2 fusion.k
  77.7 0.1 collective-permute-start.18
  77.8 0.2 gather_a_body.1.g
  77.9 1.4 %far_a_body.1 = (bf16[1024,2048]{1,0:T(8,128)(2,1)S(1)}, bf16[768,256]{1,0:T(8,128)(2,1)S(1)}, bf16[768,256]{1,0:T(8,128)(2,1)S(1)}) custom-call(bf16[768,1024]{1,0:T(8,128)(2,1)S(1)} %gather_a_body.1.g, bf16[256,2048]{1,0:T(8,128)(2,1)S(1)} %pad_maximum_fusion.own, bf16[256,2048]{1,0:T(8,128)(2,1)S(1)} %collective-permute-done.14.r1, ...), custom_call_target="tpu_custom_call" | custom-call | flops 1000000000 | bytes 1000000 | tf_op jit(solution)/shard_map/far_a_body/pallas_call | solution.py:324
  79.4 2.0 %collective-permute-start.19 = (bf16[768,256]{1,0:T(8,128)(2,1)S(1)}, bf16[768,256]{1,0:T(8,128)(2,1)S(1)}, u32[]{:S(2)}, u32[]{:S(2)}) collective-permute-start(bf16[768,256]{1,0:T(8,128)(2,1)S(1)} %get-tuple-element.91), channel_id=1, source_target_pairs={{0,32},{8,40},{1,33},{9,41},{2,34},{10,42},{3,35},{11,43},{16,48},... | collective-permute-start | bytes 1179656 | tf_op jit(solution)/shard_map/reduce_a_far_up/ppermute | solution.py:54
  81.3 2.2 %collective-permute-start.20 = (bf16[768,256]{1,0:T(8,128)(2,1)S(1)}, bf16[768,256]{1,0:T(8,128)(2,1)S(1)}, u32[]{:S(2)}, u32[]{:S(2)}) collective-permute-start(bf16[768,256]{1,0:T(8,128)(2,1)S(1)} %get-tuple-element.99), channel_id=1, source_target_pairs={{0,96},{8,104},{1,97},{9,105},{2,98},{10,106},{3,99},{11,107},{16,... | collective-permute-start | bytes 1179656 | tf_op jit(solution)/shard_map/reduce_a_far_down/ppermute | solution.py:54
  83.5 0.2 gather_b_body.1.g
  83.8 1.0 far_b_body.1
  84.8 1.3 collective-permute-start.26
  86.1 2.0 %collective-permute-start.27 = (bf16[384,512]{1,0:T(8,128)(2,1)S(1)}, bf16[384,512]{1,0:T(8,128)(2,1)S(1)}, u32[]{:S(2)}, u32[]{:S(2)}) collective-permute-start(bf16[384,512]{1,0:T(8,128)(2,1)S(1)} %get-tuple-element.110), channel_id=1, source_target_pairs={{0,20},{8,28},{1,21},{9,29},{2,22},{10,30},{3,23},{11,31},{16,0},{... | collective-permute-start | bytes 1179656 | tf_op jit(solution)/shard_map/reduce_b_far_down/ppermute | solution.py:54
  88.1 2.6 %near_a_body.1 = (f32[768,512]{1,0:T(8,128)S(1)}, f32[768,512]{1,0:T(8,128)S(1)}, f32[768,512]{1,0:T(8,128)S(1)}) custom-call(bf16[768,1024]{1,0:T(8,128)(2,1)S(1)} %gather_a_body.1.g, bf16[1024,2048]{1,0:T(8,128)(2,1)S(1)} %get-tuple-element.93.x), custom_call_target="tpu_custom_call" | custom-call | flops 1000000000 | bytes 1000000 | tf_op jit(solution)/shard_map/near_a_body/pallas_call | solution.py:363
  90.7 2.5 %collective-permute-done.19.gu = bf16[768,256]{1,0:T(8,128)(2,1)S(1)} collective-permute-done((bf16[768,256]{1,0:T(8,128)(2,1)S(1)}, bf16[768,256]{1,0:T(8,128)(2,1)S(1)}, u32[]{:S(2)}, u32[]{:S(2)}) %collective-permute-start.19) | collective-permute-done | bytes 393248 | tf_op jit(solution)/shard_map/reduce_a_far_up/ppermute | solution.py:54
  93.2 0.2 add_near_body.2
  93.5 1.3 collective-permute-start.21
  94.8 2.0 %collective-permute-start.22 = (bf16[768,512]{1,0:T(8,128)(2,1)S(1)}, bf16[768,512]{1,0:T(8,128)(2,1)S(1)}, u32[]{:S(2)}, u32[]{:S(2)}) collective-permute-start(bf16[768,512]{1,0:T(8,128)(2,1)S(1)} %get-tuple-element.101), channel_id=1, source_target_pairs={{0,96},{8,104},{1,97},{9,105},{2,98},{10,106},{3,99},{11,107},{16,... | collective-permute-start | bytes 2359304 | tf_op jit(solution)/shard_map/reduce_a_down/ppermute | solution.py:54
  96.8 2.6 %near_b_body.1 = (f32[384,1024]{1,0:T(8,128)S(1)}, f32[384,1024]{1,0:T(8,128)S(1)}, f32[384,1024]{1,0:T(8,128)S(1)}) custom-call(bf16[768,1024]{1,0:T(8,128)(2,1)S(1)} %gather_b_body.1.g, bf16[1024,2048]{1,0:T(8,128)(2,1)S(1)} %get-tuple-element.93.x), custom_call_target="tpu_custom_call" | custom-call | flops 1000000000 | bytes 1000000 | tf_op jit(solution)/shard_map/near_b_body/pallas_call | solution.py:379
  99.4 0.2 add_near_body.3
  99.6 1.3 collective-permute-start.28
  100.9 2.0 %collective-permute-start.29 = (bf16[384,1024]{1,0:T(8,128)(2,1)S(1)}, bf16[384,1024]{1,0:T(8,128)(2,1)S(1)}, u32[]{:S(2)}, u32[]{:S(2)}) collective-permute-start(bf16[384,1024]{1,0:T(8,128)(2,1)S(1)} %get-tuple-element.112), channel_id=1, source_target_pairs={{0,20},{8,28},{1,21},{9,29},{2,22},{10,30},{3,23},{11,31},{16,0},{... | collective-permute-start | bytes 2359304 | tf_op jit(solution)/shard_map/reduce_b_down/ppermute | solution.py:54
  102.9 11.2 %collective-permute-done.21.refs_1_ = bf16[768,512]{1,0:T(8,128)(2,1)S(1)} collective-permute-done((bf16[768,512]{1,0:T(8,128)(2,1)S(1)}, bf16[768,512]{1,0:T(8,128)(2,1)S(1)}, u32[]{:S(2)}, u32[]{:S(2)}) %collective-permute-start.21) | collective-permute-done | bytes 786464 | tf_op jit(solution)/shard_map/reduce_a_up/ppermute | solution.py:54
  114.1 0.5 add_a_body.1
  114.6 1.3 collective-permute-start.23
  115.9 2.0 %collective-permute-start.24 = (bf16[384,256]{1,0:T(8,128)(2,1)S(1)}, bf16[384,256]{1,0:T(8,128)(2,1)S(1)}, u32[]{:S(2)}, u32[]{:S(2)}) collective-permute-start(bf16[384,256]{1,0:T(8,128)(2,1)S(1)} %get-tuple-element.104), channel_id=1, source_target_pairs={{0,20},{8,28},{1,21},{9,29},{2,22},{10,30},{3,23},{11,31},{16,0},{... | collective-permute-start | bytes 589832 | tf_op jit(solution)/shard_map/second_a_x3/ppermute | solution.py:54
  117.9 1.6 %collective-permute-start.25 = (bf16[384,256]{1,0:T(8,128)(2,1)S(1)}, bf16[384,256]{1,0:T(8,128)(2,1)S(1)}, u32[]{:S(2)}, u32[]{:S(2)}) collective-permute-start(bf16[384,256]{1,0:T(8,128)(2,1)S(1)} %get-tuple-element.105), channel_id=1, source_target_pairs={{0,4},{8,12},{1,5},{9,13},{2,6},{10,14},{3,7},{11,15},{16,20},{24,... | collective-permute-start | bytes 589832 | tf_op jit(solution)/shard_map/second_a_x2/ppermute | solution.py:54
  119.4 1.9 %collective-permute-done.28.refs_1_ = bf16[384,1024]{1,0:T(8,128)(2,1)S(1)} collective-permute-done((bf16[384,1024]{1,0:T(8,128)(2,1)S(1)}, bf16[384,1024]{1,0:T(8,128)(2,1)S(1)}, u32[]{:S(2)}, u32[]{:S(2)}) %collective-permute-start.28) | collective-permute-done | bytes 786464 | tf_op jit(solution)/shard_map/reduce_b_up/ppermute | solution.py:54
  121.4 0.5 add_b_body.1
  121.9 0.1 collective-permute-start.30
  122.0 3.2 %collective-permute-start.31 = (bf16[384,256]{1,0:T(8,128)(2,1)S(1)}, bf16[384,256]{1,0:T(8,128)(2,1)S(1)}, u32[]{:S(2)}, u32[]{:S(2)}) collective-permute-start(bf16[384,256]{1,0:T(8,128)(2,1)S(1)} %get-tuple-element.115), channel_id=1, source_target_pairs={{0,96},{8,104},{1,97},{9,105},{2,98},{10,106},{3,99},{11,107},{16,... | collective-permute-start | bytes 589832 | tf_op jit(solution)/shard_map/second_b_z3/ppermute | solution.py:54
  125.2 0.5 collective-permute-start.32
  125.7 1.7 %collective-permute-done.24.refs_2_ = bf16[384,256]{1,0:T(8,128)(2,1)S(1)} collective-permute-done((bf16[384,256]{1,0:T(8,128)(2,1)S(1)}, bf16[384,256]{1,0:T(8,128)(2,1)S(1)}, u32[]{:S(2)}, u32[]{:S(2)}) %collective-permute-start.24) | collective-permute-done | bytes 196640 | tf_op jit(solution)/shard_map/second_a_x3/ppermute | solution.py:54
  127.4 1.5 %collective-permute-done.25.refs_3_ = bf16[384,256]{1,0:T(8,128)(2,1)S(1)} collective-permute-done((bf16[384,256]{1,0:T(8,128)(2,1)S(1)}, bf16[384,256]{1,0:T(8,128)(2,1)S(1)}, u32[]{:S(2)}, u32[]{:S(2)}) %collective-permute-start.25) | collective-permute-done | bytes 196640 | tf_op jit(solution)/shard_map/second_a_x2/ppermute | solution.py:54
  128.9 4.0 %collective-permute-done.30.refs_5_ = bf16[384,256]{1,0:T(8,128)(2,1)S(1)} collective-permute-done((bf16[384,256]{1,0:T(8,128)(2,1)S(1)}, bf16[384,256]{1,0:T(8,128)(2,1)S(1)}, u32[]{:S(2)}, u32[]{:S(2)}) %collective-permute-start.30) | collective-permute-done | bytes 196640 | tf_op jit(solution)/shard_map/second_b_z1/ppermute | solution.py:54
  132.9 1.1 finish_body.1
  (37 shorter events, 0.2 us)
Async XLA Ops:
  4.6 7.4 %collective-permute-start.3 = (bf16[128,640]{1,0:T(8,128)(2,1)}, bf16[128,640]{1,0:T(8,128)(2,1)S(1)}, u32[]{:S(2)}, u32[]{:S(2)}) collective-permute-start(bf16[128,640]{1,0:T(8,128)(2,1)} %get-tuple-element.66), channel_id=1, source_target_pairs={{0,1},{8,9},{1,2},{9,10},{2,3},{10,11},{3,0},{11,8},{16,17},{24,25... | collective-permute-start | bytes 491528 | tf_op jit(solution)/shard_map/keys_y1/ppermute | solution.py:54
  4.9 12.8 %collective-permute-start.4 = (bf16[128,640]{1,0:T(8,128)(2,1)}, bf16[128,640]{1,0:T(8,128)(2,1)S(1)}, u32[]{:S(2)}, u32[]{:S(2)}) collective-permute-start(bf16[128,640]{1,0:T(8,128)(2,1)} %get-tuple-element.67), channel_id=1, source_target_pairs={{0,2},{8,10},{1,3},{9,11},{2,0},{10,8},{3,1},{11,9},{16,18},{24,26... | collective-permute-start | bytes 491528 | tf_op jit(solution)/shard_map/keys_y2/ppermute | solution.py:54
  7.5 10.2 %collective-permute-start.5 = (bf16[128,640]{1,0:T(8,128)(2,1)}, bf16[128,640]{1,0:T(8,128)(2,1)S(1)}, u32[]{:S(2)}, u32[]{:S(2)}) collective-permute-start(bf16[128,640]{1,0:T(8,128)(2,1)} %get-tuple-element.68), channel_id=1, source_target_pairs={{0,3},{8,11},{1,0},{9,8},{2,1},{10,9},{3,2},{11,10},{16,19},{24,27... | collective-permute-start | bytes 491528 | tf_op jit(solution)/shard_map/keys_y3/ppermute | solution.py:54
  7.5 13.7 %collective-permute-start = (bf16[128,1024]{1,0:T(8,128)(2,1)}, bf16[128,1024]{1,0:T(8,128)(2,1)S(1)}, u32[]{:S(2)}, u32[]{:S(2)}) collective-permute-start(bf16[128,1024]{1,0:T(8,128)(2,1)} %get-tuple-element.60), channel_id=1, source_target_pairs={{0,1},{8,9},{1,2},{9,10},{2,3},{10,11},{3,0},{11,8},{16,17},{24,25... | collective-permute-start | bytes 786440 | tf_op jit(solution)/shard_map/queries0_y1/ppermute | solution.py:54
  10.8 13.6 %collective-permute-start.2 = (bf16[128,1024]{1,0:T(8,128)(2,1)}, bf16[128,1024]{1,0:T(8,128)(2,1)S(1)}, u32[]{:S(2)}, u32[]{:S(2)}) collective-permute-start(bf16[128,1024]{1,0:T(8,128)(2,1)} %get-tuple-element.62), channel_id=1, source_target_pairs={{0,3},{8,11},{1,0},{9,8},{2,1},{10,9},{3,2},{11,10},{16,19},{24,27... | collective-permute-start | bytes 786440 | tf_op jit(solution)/shard_map/queries0_y3/ppermute | solution.py:54
  12.0 15.2 %collective-permute-start.1 = (bf16[128,1024]{1,0:T(8,128)(2,1)}, bf16[128,1024]{1,0:T(8,128)(2,1)S(1)}, u32[]{:S(2)}, u32[]{:S(2)}) collective-permute-start(bf16[128,1024]{1,0:T(8,128)(2,1)} %get-tuple-element.61), channel_id=1, source_target_pairs={{0,2},{8,10},{1,3},{9,11},{2,0},{10,8},{3,1},{11,9},{16,18},{24,26... | collective-permute-start | bytes 786440 | tf_op jit(solution)/shard_map/queries0_y2/ppermute | solution.py:54
  15.1 2.7 %copy-start.2 = (bf16[128,640]{1,0:T(8,128)(2,1)S(1)}, bf16[128,640]{1,0:T(8,128)(2,1)}, u32[]{:S(2)}) copy-start(bf16[128,640]{1,0:T(8,128)(2,1)} %get-tuple-element.65.kv) | copy-start | bytes 491524
  15.1 9.3 %copy-start.5 = (bf16[128,1024]{1,0:T(8,128)(2,1)S(1)}, bf16[128,1024]{1,0:T(8,128)(2,1)}, u32[]{:S(2)}) copy-start(bf16[128,1024]{1,0:T(8,128)(2,1)} %get-tuple-element.74) | copy-start | bytes 786436
  15.1 12.1 %copy-start.4 = (bf16[128,1024]{1,0:T(8,128)(2,1)S(1)}, bf16[128,1024]{1,0:T(8,128)(2,1)}, u32[]{:S(2)}) copy-start(bf16[128,1024]{1,0:T(8,128)(2,1)} %get-tuple-element.76) | copy-start | bytes 786436
  15.1 12.1 %copy-start = (bf16[1,128,4096]{2,1,0:T(8,128)(2,1)S(1)}, bf16[1,128,4096]{2,1,0:T(8,128)(2,1)}, u32[]{:S(2)}) copy-start(bf16[1,128,4096]{2,1,0:T(8,128)(2,1)} %q.3) | copy-start | bytes 3145732
  15.1 12.1 %copy-start.1 = (bf16[1,128,4096]{2,1,0:T(8,128)(2,1)S(1)}, bf16[1,128,4096]{2,1,0:T(8,128)(2,1)}, u32[]{:S(2)}) copy-start(bf16[1,128,4096]{2,1,0:T(8,128)(2,1)} %g.5) | copy-start | bytes 3145732
  17.6 9.9 %collective-permute-start.13 = (bf16[128,2048]{1,0:T(8,128)(2,1)}, bf16[128,2048]{1,0:T(8,128)(2,1)S(1)}, u32[]{:S(2)}, u32[]{:S(2)}) collective-permute-start(bf16[128,2048]{1,0:T(8,128)(2,1)} %get-tuple-element.86), channel_id=1, source_target_pairs={{0,8},{8,0},{1,9},{9,1},{2,10},{10,2},{3,11},{11,3},{16,24},{24,16... | collective-permute-start | bytes 1572872 | tf_op jit(solution)/shard_map/swap_inputs/ppermute | solution.py:54
  17.8 18.7 %collective-permute-start.6 = (bf16[512,640]{1,0:T(8,128)(2,1)S(1)}, bf16[512,640]{1,0:T(8,128)(2,1)S(1)}, u32[]{:S(2)}, u32[]{:S(2)}) collective-permute-start(bf16[512,640]{1,0:T(8,128)(2,1)S(1)} %pad_maximum_fusion.1), channel_id=1, source_target_pairs={{0,4},{8,12},{1,5},{9,13},{2,6},{10,14},{3,7},{11,15},{16,20},{24,... | collective-permute-start | bytes 1966088 | tf_op jit(solution)/shard_map/half/ppermute | solution.py:54
  21.2 24.2 %collective-permute-start.8 = (bf16[128,1024]{1,0:T(8,128)(2,1)}, bf16[128,1024]{1,0:T(8,128)(2,1)S(1)}, u32[]{:S(2)}, u32[]{:S(2)}) collective-permute-start(bf16[128,1024]{1,0:T(8,128)(2,1)} %get-tuple-element.72), channel_id=1, source_target_pairs={{0,1},{8,9},{1,2},{9,10},{2,3},{10,11},{3,0},{11,8},{16,17},{24,25... | collective-permute-start | bytes 786440 | tf_op jit(solution)/shard_map/queries1_y1/ppermute | solution.py:54
  24.4 21.0 %collective-permute-start.9 = (bf16[128,1024]{1,0:T(8,128)(2,1)S(1)}, bf16[128,1024]{1,0:T(8,128)(2,1)S(1)}, u32[]{:S(2)}, u32[]{:S(2)}) collective-permute-start(bf16[128,1024]{1,0:T(8,128)(2,1)S(1)} %copy-done.5), channel_id=1, source_target_pairs={{0,2},{8,10},{1,3},{9,11},{2,0},{10,8},{3,1},{11,9},{16,18},{24,26... | collective-permute-start | bytes 786440 | tf_op jit(solution)/shard_map/queries1_y2/ppermute | solution.py:54
  24.4 3.1 %copy-start.3 = (bf16[128,2048]{1,0:T(8,128)(2,1)S(1)}, bf16[128,2048]{1,0:T(8,128)(2,1)}, u32[]{:S(2)}) copy-start(bf16[128,2048]{1,0:T(8,128)(2,1)} %get-tuple-element.85) | copy-start | bytes 1572868
  27.2 18.2 %collective-permute-start.10 = (bf16[128,1024]{1,0:T(8,128)(2,1)S(1)}, bf16[128,1024]{1,0:T(8,128)(2,1)S(1)}, u32[]{:S(2)}, u32[]{:S(2)}) collective-permute-start(bf16[128,1024]{1,0:T(8,128)(2,1)S(1)} %copy-done.4), channel_id=1, source_target_pairs={{0,3},{8,11},{1,0},{9,8},{2,1},{10,9},{3,2},{11,10},{16,19},{24,27... | collective-permute-start | bytes 786440 | tf_op jit(solution)/shard_map/queries1_y3/ppermute | solution.py:54
  27.6 31.8 %collective-permute-start.14 = (bf16[256,2048]{1,0:T(8,128)(2,1)S(1)}, bf16[256,2048]{1,0:T(8,128)(2,1)S(1)}, u32[]{:S(2)}, u32[]{:S(2)}) collective-permute-start(bf16[256,2048]{1,0:T(8,128)(2,1)S(1)} %pad_maximum_fusion.own), channel_id=1, source_target_pairs={{0,1},{8,9},{1,2},{9,10},{2,3},{10,11},{3,0},{11,8},{16,17},{24,25... | collective-permute-start | bytes 3145736 | tf_op jit(solution)/shard_map/inputs_up/ppermute | solution.py:54
  36.5 26.5 %collective-permute-start.16 = (bf16[256,2048]{1,0:T(8,128)(2,1)S(1)}, bf16[256,2048]{1,0:T(8,128)(2,1)S(1)}, u32[]{:S(2)}, u32[]{:S(2)}) collective-permute-start(bf16[256,2048]{1,0:T(8,128)(2,1)S(1)} %pad_maximum_fusion.own), channel_id=1, source_target_pairs={{0,3},{8,11},{1,0},{9,8},{2,1},{10,9},{3,2},{11,10},{16,19},{24,27... | collective-permute-start | bytes 3145736 | tf_op jit(solution)/shard_map/inputs_down/ppermute | solution.py:54
  53.9 9.3 %collective-permute-start.11 = (bf16[512,512]{1,0:T(8,128)(2,1)S(1)}, bf16[512,512]{1,0:T(8,128)(2,1)S(1)}, u32[]{:S(2)}, u32[]{:S(2)}) collective-permute-start(bf16[512,512]{1,0:T(8,128)(2,1)S(1)} %get-tuple-element.79.a1), channel_id=1, source_target_pairs={{0,8},{8,0},{1,9},{9,1},{2,10},{10,2},{3,11},{11,3},{16,24},{24,16... | collective-permute-start | bytes 1572872 | tf_op jit(solution)/shard_map/swap_dq1/ppermute | solution.py:54
  54.0 15.9 %collective-permute-start.12 = (bf16[512,512]{1,0:T(8,128)(2,1)S(1)}, bf16[512,512]{1,0:T(8,128)(2,1)S(1)}, u32[]{:S(2)}, u32[]{:S(2)}) collective-permute-start(bf16[512,512]{1,0:T(8,128)(2,1)S(1)} %pad_maximum_fusion.2), channel_id=1, source_target_pairs={{0,4},{8,12},{1,5},{9,13},{2,6},{10,14},{3,7},{11,15},{16,20},{24,... | collective-permute-start | bytes 1572872 | tf_op jit(solution)/shard_map/back/ppermute | solution.py:54
  59.5 14.5 %collective-permute-start.15 = (bf16[128,2048]{1,0:T(8,128)(2,1)S(1)}, bf16[128,2048]{1,0:T(8,128)(2,1)S(1)}, u32[]{:S(2)}, u32[]{:S(2)}) collective-permute-start(bf16[128,2048]{1,0:T(8,128)(2,1)S(1)} %slice.8), channel_id=1, source_target_pairs={{0,1},{8,9},{1,2},{9,10},{2,3},{10,11},{3,0},{11,8},{16,17},{24,25... | collective-permute-start | bytes 1572872 | tf_op jit(solution)/shard_map/inputs_up2/ppermute | solution.py:54
  63.0 14.5 %collective-permute-start.17 = (bf16[128,2048]{1,0:T(8,128)(2,1)S(1)}, bf16[128,2048]{1,0:T(8,128)(2,1)S(1)}, u32[]{:S(2)}, u32[]{:S(2)}) collective-permute-start(bf16[128,2048]{1,0:T(8,128)(2,1)S(1)} %slice.9), channel_id=1, source_target_pairs={{0,3},{8,11},{1,0},{9,8},{2,1},{10,9},{3,2},{11,10},{16,19},{24,27... | collective-permute-start | bytes 1572872 | tf_op jit(solution)/shard_map/inputs_down2/ppermute | solution.py:54
  63.1 14.6 %collective-permute-start.7 = (bf16[512,512]{1,0:T(8,128)(2,1)S(1)}, bf16[512,512]{1,0:T(8,128)(2,1)S(1)}, u32[]{:S(2)}, u32[]{:S(2)}) collective-permute-start(bf16[512,512]{1,0:T(8,128)(2,1)S(1)} %get-tuple-element.69.a0), channel_id=1, source_target_pairs={{0,8},{8,0},{1,9},{9,1},{2,10},{10,2},{3,11},{11,3},{16,24},{24,16... | collective-permute-start | bytes 1572872 | tf_op jit(solution)/shard_map/swap_dq0/ppermute | solution.py:54
  77.7 5.9 %collective-permute-start.18 = (bf16[512,512]{1,0:T(8,128)(2,1)S(1)}, bf16[512,512]{1,0:T(8,128)(2,1)S(1)}, u32[]{:S(2)}, u32[]{:S(2)}) collective-permute-start(bf16[512,512]{1,0:T(8,128)(2,1)S(1)} %fusion.k), channel_id=1, source_target_pairs={{0,8},{8,0},{1,9},{9,1},{2,10},{10,2},{3,11},{11,3},{16,24},{24,16... | collective-permute-start | bytes 1572872 | tf_op jit(solution)/shard_map/swap_dkv/ppermute | solution.py:54
  79.4 13.9 %collective-permute-start.19 = (bf16[768,256]{1,0:T(8,128)(2,1)S(1)}, bf16[768,256]{1,0:T(8,128)(2,1)S(1)}, u32[]{:S(2)}, u32[]{:S(2)}) collective-permute-start(bf16[768,256]{1,0:T(8,128)(2,1)S(1)} %get-tuple-element.91), channel_id=1, source_target_pairs={{0,32},{8,40},{1,33},{9,41},{2,34},{10,42},{3,35},{11,43},{16,48},... | collective-permute-start | bytes 1179656 | tf_op jit(solution)/shard_map/reduce_a_far_up/ppermute | solution.py:54
  81.3 11.9 %collective-permute-start.20 = (bf16[768,256]{1,0:T(8,128)(2,1)S(1)}, bf16[768,256]{1,0:T(8,128)(2,1)S(1)}, u32[]{:S(2)}, u32[]{:S(2)}) collective-permute-start(bf16[768,256]{1,0:T(8,128)(2,1)S(1)} %get-tuple-element.99), channel_id=1, source_target_pairs={{0,96},{8,104},{1,97},{9,105},{2,98},{10,106},{3,99},{11,107},{16,... | collective-permute-start | bytes 1179656 | tf_op jit(solution)/shard_map/reduce_a_far_down/ppermute | solution.py:54
  84.8 14.6 %collective-permute-start.26 = (bf16[384,512]{1,0:T(8,128)(2,1)S(1)}, bf16[384,512]{1,0:T(8,128)(2,1)S(1)}, u32[]{:S(2)}, u32[]{:S(2)}) collective-permute-start(bf16[384,512]{1,0:T(8,128)(2,1)S(1)} %get-tuple-element.94), channel_id=1, source_target_pairs={{0,16},{8,24},{1,17},{9,25},{2,18},{10,26},{3,19},{11,27},{16,4},{... | collective-permute-start | bytes 1179656 | tf_op jit(solution)/shard_map/reduce_b_far_up/ppermute | solution.py:54
  86.1 13.2 %collective-permute-start.27 = (bf16[384,512]{1,0:T(8,128)(2,1)S(1)}, bf16[384,512]{1,0:T(8,128)(2,1)S(1)}, u32[]{:S(2)}, u32[]{:S(2)}) collective-permute-start(bf16[384,512]{1,0:T(8,128)(2,1)S(1)} %get-tuple-element.110), channel_id=1, source_target_pairs={{0,20},{8,28},{1,21},{9,29},{2,22},{10,30},{3,23},{11,31},{16,0},{... | collective-permute-start | bytes 1179656 | tf_op jit(solution)/shard_map/reduce_b_far_down/ppermute | solution.py:54
  93.5 20.6 %collective-permute-start.21 = (bf16[768,512]{1,0:T(8,128)(2,1)S(1)}, bf16[768,512]{1,0:T(8,128)(2,1)S(1)}, u32[]{:S(2)}, u32[]{:S(2)}) collective-permute-start(bf16[768,512]{1,0:T(8,128)(2,1)S(1)} %get-tuple-element.100), channel_id=1, source_target_pairs={{0,32},{8,40},{1,33},{9,41},{2,34},{10,42},{3,35},{11,43},{16,48},... | collective-permute-start | bytes 2359304 | tf_op jit(solution)/shard_map/reduce_a_up/ppermute | solution.py:54
  94.8 19.3 %collective-permute-start.22 = (bf16[768,512]{1,0:T(8,128)(2,1)S(1)}, bf16[768,512]{1,0:T(8,128)(2,1)S(1)}, u32[]{:S(2)}, u32[]{:S(2)}) collective-permute-start(bf16[768,512]{1,0:T(8,128)(2,1)S(1)} %get-tuple-element.101), channel_id=1, source_target_pairs={{0,96},{8,104},{1,97},{9,105},{2,98},{10,106},{3,99},{11,107},{16,... | collective-permute-start | bytes 2359304 | tf_op jit(solution)/shard_map/reduce_a_down/ppermute | solution.py:54
  99.6 21.8 %collective-permute-start.28 = (bf16[384,1024]{1,0:T(8,128)(2,1)S(1)}, bf16[384,1024]{1,0:T(8,128)(2,1)S(1)}, u32[]{:S(2)}, u32[]{:S(2)}) collective-permute-start(bf16[384,1024]{1,0:T(8,128)(2,1)S(1)} %get-tuple-element.111), channel_id=1, source_target_pairs={{0,16},{8,24},{1,17},{9,25},{2,18},{10,26},{3,19},{11,27},{16,4},{... | collective-permute-start | bytes 2359304 | tf_op jit(solution)/shard_map/reduce_b_up/ppermute | solution.py:54
  100.9 20.5 %collective-permute-start.29 = (bf16[384,1024]{1,0:T(8,128)(2,1)S(1)}, bf16[384,1024]{1,0:T(8,128)(2,1)S(1)}, u32[]{:S(2)}, u32[]{:S(2)}) collective-permute-start(bf16[384,1024]{1,0:T(8,128)(2,1)S(1)} %get-tuple-element.112), channel_id=1, source_target_pairs={{0,20},{8,28},{1,21},{9,29},{2,22},{10,30},{3,23},{11,31},{16,0},{... | collective-permute-start | bytes 2359304 | tf_op jit(solution)/shard_map/reduce_b_down/ppermute | solution.py:54
  114.6 10.7 %collective-permute-start.23 = (bf16[384,256]{1,0:T(8,128)(2,1)S(1)}, bf16[384,256]{1,0:T(8,128)(2,1)S(1)}, u32[]{:S(2)}, u32[]{:S(2)}) collective-permute-start(bf16[384,256]{1,0:T(8,128)(2,1)S(1)} %get-tuple-element.103), channel_id=1, source_target_pairs={{0,16},{8,24},{1,17},{9,25},{2,18},{10,26},{3,19},{11,27},{16,4},{... | collective-permute-start | bytes 589832 | tf_op jit(solution)/shard_map/second_a_x1/ppermute | solution.py:54
  115.9 11.5 %collective-permute-start.24 = (bf16[384,256]{1,0:T(8,128)(2,1)S(1)}, bf16[384,256]{1,0:T(8,128)(2,1)S(1)}, u32[]{:S(2)}, u32[]{:S(2)}) collective-permute-start(bf16[384,256]{1,0:T(8,128)(2,1)S(1)} %get-tuple-element.104), channel_id=1, source_target_pairs={{0,20},{8,28},{1,21},{9,29},{2,22},{10,30},{3,23},{11,31},{16,0},{... | collective-permute-start | bytes 589832 | tf_op jit(solution)/shard_map/second_a_x3/ppermute | solution.py:54
  117.9 11.0 %collective-permute-start.25 = (bf16[384,256]{1,0:T(8,128)(2,1)S(1)}, bf16[384,256]{1,0:T(8,128)(2,1)S(1)}, u32[]{:S(2)}, u32[]{:S(2)}) collective-permute-start(bf16[384,256]{1,0:T(8,128)(2,1)S(1)} %get-tuple-element.105), channel_id=1, source_target_pairs={{0,4},{8,12},{1,5},{9,13},{2,6},{10,14},{3,7},{11,15},{16,20},{24,... | collective-permute-start | bytes 589832 | tf_op jit(solution)/shard_map/second_a_x2/ppermute | solution.py:54
  121.9 11.0 %collective-permute-start.30 = (bf16[384,256]{1,0:T(8,128)(2,1)S(1)}, bf16[384,256]{1,0:T(8,128)(2,1)S(1)}, u32[]{:S(2)}, u32[]{:S(2)}) collective-permute-start(bf16[384,256]{1,0:T(8,128)(2,1)S(1)} %get-tuple-element.114), channel_id=1, source_target_pairs={{0,32},{8,40},{1,33},{9,41},{2,34},{10,42},{3,35},{11,43},{16,48},... | collective-permute-start | bytes 589832 | tf_op jit(solution)/shard_map/second_b_z1/ppermute | solution.py:54
  122.0 10.9 %collective-permute-start.31 = (bf16[384,256]{1,0:T(8,128)(2,1)S(1)}, bf16[384,256]{1,0:T(8,128)(2,1)S(1)}, u32[]{:S(2)}, u32[]{:S(2)}) collective-permute-start(bf16[384,256]{1,0:T(8,128)(2,1)S(1)} %get-tuple-element.115), channel_id=1, source_target_pairs={{0,96},{8,104},{1,97},{9,105},{2,98},{10,106},{3,99},{11,107},{16,... | collective-permute-start | bytes 589832 | tf_op jit(solution)/shard_map/second_b_z3/ppermute | solution.py:54
  125.2 7.7 %collective-permute-start.32 = (bf16[384,256]{1,0:T(8,128)(2,1)S(1)}, bf16[384,256]{1,0:T(8,128)(2,1)S(1)}, u32[]{:S(2)}, u32[]{:S(2)}) collective-permute-start(bf16[384,256]{1,0:T(8,128)(2,1)S(1)} %get-tuple-element.116), channel_id=1, source_target_pairs={{0,64},{8,72},{1,65},{9,73},{2,66},{10,74},{3,67},{11,75},{16,80},... | collective-permute-start | bytes 589832 | tf_op jit(solution)/shard_map/second_b_z2/ppermute | solution.py:54

commit v4 on v3

--- a/solution.py
+++ b/solution.py
@@ -67,11 +67,15 @@
     )
 
 
-def run_copies(todo, sems):
+def start_copies(todo, sems):
     made = [pltpu.make_async_copy(a, b, sems.at[i]) for i, (a, b) in enumerate(todo)]
     for m in made:
         m.start()
-    for m in made:
+    return made
+
+
+def run_copies(todo, sems):
+    for m in start_copies(todo, sems):
         m.wait()
 
 
@@ -79,9 +83,8 @@
     return pl.multiple_of(i * n, n)
 
 
-def pack_heads(queries, keys, values, grads, ids):
-    def pack_heads_body(q, k, v, g, i, k1, k2, k3, k0, *refs):
-        qs, sems = refs[:6], refs[6]
+def pack_keys(keys, values, ids):
+    def pack_keys_body(k, v, i, k1, k2, k3, k0, sems):
         y = place()["y"]
         todo = []
         for d, o in ((1, k1), (3, k3), (2, k2), (0, k0)):
@@ -91,26 +94,47 @@
                     (k.at[0, :, cols], o.at[:, h * 256 : h * 256 + 128]),
                     (v.at[0, :, cols], o.at[:, h * 256 + 128 : h * 256 + 256]),
                 ]
-        for h in range(2):
-            for d in (1, 2, 3):
-                o = qs[h * 3 + d - 1]
-                cols = pl.ds(mult(h * 4 + lax.rem(y + d, 4), 512), 512)
-                todo += [(q.at[0, :, cols], o.at[:, 0:512]), (g.at[0, :, cols], o.at[:, 512:1024])]
+        made = start_copies(todo, sems)
         spread = jnp.broadcast_to(i[...].astype(F32), (128, 128)).T.astype(BF16)
         for o in (k1, k2, k3, k0):
             o[:, 512:640] = spread
+        for m in made:
+            m.wait()
+
+    return call(
+        pack_keys_body,
+        [jax.ShapeDtypeStruct((128, 640), BF16)] * 4,
+        [pltpu.SemaphoreType.DMA((16,))],
+        10**8,
+        10**6,
+        [ANY] * 2 + [VMEM],
+        [VMEM] * 4,
+        BIG,
+    )(keys, values, ids)
+
+
+def pack_queries(queries, grads):
+    def pack_queries_body(q, g, *refs):
+        outs, sems = refs[:6], refs[6]
+        y = place()["y"]
+        todo = []
+        for h in range(2):
+            for d in (1, 2, 3):
+                o = outs[h * 3 + d - 1]
+                cols = pl.ds(mult(h * 4 + lax.rem(y + d, 4), 512), 512)
+                todo += [(q.at[0, :, cols], o.at[:, 0:512]), (g.at[0, :, cols], o.at[:, 512:1024])]
         run_copies(todo, sems)
 
     return call(
-        pack_heads_body,
-        [jax.ShapeDtypeStruct((128, 640), BF16)] * 4 + [jax.ShapeDtypeStruct((128, 1024), BF16)] * 6,
-        [pltpu.SemaphoreType.DMA((28,))],
+        pack_queries_body,
+        [jax.ShapeDtypeStruct((128, 1024), BF16)] * 6,
+        [pltpu.SemaphoreType.DMA((12,))],
         10**8,
         10**6,
-        [ANY] * 4 + [VMEM],
-        [VMEM] * 10,
+        [ANY] * 2,
+        [VMEM] * 6,
         BIG,
-    )(queries, keys, values, grads, ids)
+    )(queries, grads)
 
 
 def pack_inputs(hidden):
@@ -498,9 +522,8 @@
 
 
 def per_device(hidden_in, queries, key_heads, saved_value_heads, out_grads, doc_ids):
-    *kmsg, own, q01, q02, q03, q11, q12, q13 = pack_heads(
-        queries, key_heads, saved_value_heads, out_grads, doc_ids
-    )
+    *kmsg, own = pack_keys(key_heads, saved_value_heads, doc_ids)
+    q01, q02, q03, q11, q12, q13 = pack_queries(after(queries, own), out_grads)
     keys = [send("keys_y%d" % (d + 1), m, dy=d + 1) for d, m in enumerate(kmsg)]
     keep, give = pack_inputs(after(hidden_in, own))
     got = send("swap_inputs", give, dc=1)

time: 134 us -> 133 us (level)
  waiting for transfers between devices: 49.4 us -> 44.3 us
  starting transfers between devices: 49.3 us -> 52.3 us
    ppermute x33, waiting for transfers between devices: 49.4 us -> 44.3 us  [send(): return lax.ppermute(a, ('grp', 'sp'), pairs(**k))]
    ppermute x33, starting transfers between devices: 49.3 us -> 52.3 us  [send(): return lax.ppermute(a, ('grp', 'sp'), pairs(**k))]
    pallas_call x1 -> x2, Pallas kernels: 4 us -> 5.33 us  [the longest x1 2.69 us: pack_queries(): call(pack_queries_body, [jax.ShapeDtypeStruct((128, 1024), BF16)] * 6, [p...]
  transfers between devices with their start and end apart: 33 -> 33, of which waited for: 15 -> 13; matrix products, arithmetic and copies ran while one was open for 0% -> 0% of each run, Pallas kernels for 21% -> 23%
where the time goes in v4:
time: 133 us
  starting transfers between devices  52.3 us (39%)
  waiting for transfers between devices  44.3 us (33%)
  Pallas kernels  34.9 us (26%)
    ppermute x33, starting transfers between devices, send(): return lax.ppermute(a, ('grp', 'sp'), pairs(**k))  52.3 us
    ppermute x33, waiting for transfers between devices, send(): return lax.ppermute(a, ('grp', 'sp'), pairs(**k))  44.3 us
    pallas_call x2, Pallas kernels, attention(): call(attention_body, [jax.ShapeDtypeStruct((512, 512), BF16), jax.ShapeDt...  16.1 us
    pallas_call x1, Pallas kernels, pack_queries(): call(pack_queries_body, [jax.ShapeDtypeStruct((128, 1024), BF16)] * 6, [p...  2.69 us
  transfers between devices with their start and end apart: 33, of which 13 were waited for; matrix products, arithmetic and copies ran while one was open for 0% of the time, Pallas kernels for 23%

profile of v4, /device:TPU:24, one launch (start us, length us, event | category | flops | bytes accessed | tf_op | source)
XLA Modules:
  0.0 133.0 jit_solution(1834302218621330862)
XLA Ops:
  0.6 2.6 %pack_keys_body.1 = (bf16[128,640]{1,0:T(8,128)(2,1)}, bf16[128,640]{1,0:T(8,128)(2,1)}, bf16[128,640]{1,0:T(8,128)(2,1)}, bf16[128,640]{1,0:T(8,128)(2,1)}) custom-call(bf16[1,128,1024]{2,1,0:T(8,128)(2,1)} %k.1, bf16[1,128,1024]{2,1,0:T(8,128)(2,1)} %v.1, s32[1,128]{1,0:T(1,128)} %i.1), custom_call_target="tpu_custom_call" | custom-call | flops 100000000 | bytes 1000000 | tf_op jit(solution)/shard_map/pack_keys_body/pallas_call | solution.py:104
  3.3 0.2 collective-permute-start.3
  3.5 2.7 %collective-permute-start.4 = (bf16[128,640]{1,0:T(8,128)(2,1)}, bf16[128,640]{1,0:T(8,128)(2,1)S(1)}, u32[]{:S(2)}, u32[]{:S(2)}) collective-permute-start(bf16[128,640]{1,0:T(8,128)(2,1)} %get-tuple-element.69), channel_id=1, source_target_pairs={{0,2},{8,10},{1,3},{9,11},{2,0},{10,8},{3,1},{11,9},{16,18},{24,26... | collective-permute-start | bytes 491528 | tf_op jit(solution)/shard_map/keys_y2/ppermute | solution.py:54
  6.2 2.7 %pack_queries_body.1 = (bf16[128,1024]{1,0:T(8,128)(2,1)}, bf16[128,1024]{1,0:T(8,128)(2,1)}, bf16[128,1024]{1,0:T(8,128)(2,1)}, bf16[128,1024]{1,0:T(8,128)(2,1...) custom-call(bf16[1,128,4096]{2,1,0:T(8,128)(2,1)} %q.2, bf16[1,128,4096]{2,1,0:T(8,128)(2,1)} %g.5), custom_call_target="tpu_custom_call" | custom-call | flops 100000000 | bytes 1000000 | tf_op jit(solution)/shard_map/pack_queries_body/pallas_call | solution.py:128
  8.9 3.3 %collective-permute-start = (bf16[128,1024]{1,0:T(8,128)(2,1)}, bf16[128,1024]{1,0:T(8,128)(2,1)S(1)}, u32[]{:S(2)}, u32[]{:S(2)}) collective-permute-start(bf16[128,1024]{1,0:T(8,128)(2,1)} %get-tuple-element.63), channel_id=1, source_target_pairs={{0,1},{8,9},{1,2},{9,10},{2,3},{10,11},{3,0},{11,8},{16,17},{24,25... | collective-permute-start | bytes 786440 | tf_op jit(solution)/shard_map/queries0_y1/ppermute | solution.py:54
  12.2 0.0 copy-start.1
  12.2 2.2 %collective-permute-start.1 = (bf16[128,1024]{1,0:T(8,128)(2,1)}, bf16[128,1024]{1,0:T(8,128)(2,1)S(1)}, u32[]{:S(2)}, u32[]{:S(2)}) collective-permute-start(bf16[128,1024]{1,0:T(8,128)(2,1)} %get-tuple-element.64), channel_id=1, source_target_pairs={{0,2},{8,10},{1,3},{9,11},{2,0},{10,8},{3,1},{11,9},{16,18},{24,26... | collective-permute-start | bytes 786440 | tf_op jit(solution)/shard_map/queries0_y2/ppermute | solution.py:54
  14.4 2.3 %pack_inputs_body.1 = (bf16[128,2048]{1,0:T(8,128)(2,1)}, bf16[128,2048]{1,0:T(8,128)(2,1)}) custom-call(bf16[1,128,4096]{2,1,0:T(8,128)(2,1)} %x), custom_call_target="tpu_custom_call" | custom-call | flops 1000000000 | bytes 1000000 | tf_op jit(solution)/shard_map/pack_inputs_body/pallas_call | solution.py:152
  16.8 0.1 collective-permute-start.13
  16.9 0.1 pad_maximum_fusion.1
  17.0 3.1 %collective-permute-start.6 = (bf16[512,640]{1,0:T(8,128)(2,1)S(1)}, bf16[512,640]{1,0:T(8,128)(2,1)S(1)}, u32[]{:S(2)}, u32[]{:S(2)}) collective-permute-start(bf16[512,640]{1,0:T(8,128)(2,1)S(1)} %pad_maximum_fusion.1), channel_id=1, source_target_pairs={{0,4},{8,12},{1,5},{9,13},{2,6},{10,14},{3,7},{11,15},{16,20},{24,... | collective-permute-start | bytes 1966088 | tf_op jit(solution)/shard_map/half/ppermute | solution.py:54
  20.1 2.8 %collective-permute-done.q1 = bf16[128,1024]{1,0:T(8,128)(2,1)S(1)} collective-permute-done((bf16[128,1024]{1,0:T(8,128)(2,1)}, bf16[128,1024]{1,0:T(8,128)(2,1)S(1)}, u32[]{:S(2)}, u32[]{:S(2)}) %collective-permute-start) | collective-permute-done | bytes 262176 | tf_op jit(solution)/shard_map/queries0_y1/ppermute | solution.py:54
  22.8 3.9 %collective-permute-start.8 = (bf16[128,1024]{1,0:T(8,128)(2,1)}, bf16[128,1024]{1,0:T(8,128)(2,1)S(1)}, u32[]{:S(2)}, u32[]{:S(2)}) collective-permute-start(bf16[128,1024]{1,0:T(8,128)(2,1)} %get-tuple-element.74), channel_id=1, source_target_pairs={{0,1},{8,9},{1,2},{9,10},{2,3},{10,11},{3,0},{11,8},{16,17},{24,25... | collective-permute-start | bytes 786440 | tf_op jit(solution)/shard_map/queries1_y1/ppermute | solution.py:54
  26.7 0.0 copy-start.3
  26.8 1.0 collective-permute-start.10
  27.7 0.2 arrange_body.2
  28.0 0.1 pad_maximum_fusion.own
  28.1 2.4 %collective-permute-start.14 = (bf16[256,2048]{1,0:T(8,128)(2,1)S(1)}, bf16[256,2048]{1,0:T(8,128)(2,1)S(1)}, u32[]{:S(2)}, u32[]{:S(2)}) collective-permute-start(bf16[256,2048]{1,0:T(8,128)(2,1)S(1)} %pad_maximum_fusion.own), channel_id=1, source_target_pairs={{0,1},{8,9},{1,2},{9,10},{2,3},{10,11},{3,0},{11,8},{16,17},{24,25... | collective-permute-start | bytes 3145736 | tf_op jit(solution)/shard_map/inputs_up/ppermute | solution.py:54
  30.5 5.1 %collective-permute-done.6.pv = bf16[512,640]{1,0:T(8,128)(2,1)S(1)} collective-permute-done((bf16[512,640]{1,0:T(8,128)(2,1)S(1)}, bf16[512,640]{1,0:T(8,128)(2,1)S(1)}, u32[]{:S(2)}, u32[]{:S(2)}) %collective-permute-start.6) | collective-permute-done | bytes 655392 | tf_op jit(solution)/shard_map/half/ppermute | solution.py:54
  35.7 2.0 %collective-permute-start.16 = (bf16[256,2048]{1,0:T(8,128)(2,1)S(1)}, bf16[256,2048]{1,0:T(8,128)(2,1)S(1)}, u32[]{:S(2)}, u32[]{:S(2)}) collective-permute-start(bf16[256,2048]{1,0:T(8,128)(2,1)S(1)} %pad_maximum_fusion.own), channel_id=1, source_target_pairs={{0,3},{8,11},{1,0},{9,8},{2,1},{10,9},{3,2},{11,10},{16,19},{24,27... | collective-permute-start | bytes 3145736 | tf_op jit(solution)/shard_map/inputs_down/ppermute | solution.py:54
  37.6 8.0 %attention_body.2 = (bf16[512,512]{1,0:T(8,128)(2,1)S(1)}, f32[256,512]{1,0:T(8,128)S(1)}, bf16[256,512]{1,0:T(8,128)(2,1)S(1)}) custom-call(bf16[512,512]{1,0:T(8,128)(2,1)S(1)} %get-tuple-element.66.qs, bf16[512,512]{1,0:T(8,128)(2,1)S(1)} %get-tuple-element.67.gs, bf16[128,640]{1,0:T(8,128)(2,1)S(1)} %copy-done.2, ...), custom_call_target="tpu_custom_call" | custom-call | flops 12000000000 | bytes 1000000 | tf_op jit(solution)/shard_map/attention_body/pallas_call | solution.py:255
  45.7 0.5 arrange_body.3
  46.2 8.0 %attention_body.3 = (bf16[512,512]{1,0:T(8,128)(2,1)S(1)}, f32[256,512]{1,0:T(8,128)S(1)}, bf16[256,512]{1,0:T(8,128)(2,1)S(1)}) custom-call(bf16[512,512]{1,0:T(8,128)(2,1)S(1)} %get-tuple-element.79.qs, bf16[512,512]{1,0:T(8,128)(2,1)S(1)} %get-tuple-element.80.gs, bf16[128,640]{1,0:T(8,128)(2,1)S(1)} %copy-done.2, ...), custom_call_target="tpu_custom_call" | custom-call | flops 12000000000 | bytes 1000000 | tf_op jit(solution)/shard_map/attention_body/pallas_call | solution.py:255
  54.2 0.1 collective-permute-start.11
  54.3 3.1 %collective-permute-start.12 = (bf16[512,512]{1,0:T(8,128)(2,1)S(1)}, bf16[512,512]{1,0:T(8,128)(2,1)S(1)}, u32[]{:S(2)}, u32[]{:S(2)}) collective-permute-start(bf16[512,512]{1,0:T(8,128)(2,1)S(1)} %pad_maximum_fusion.2), channel_id=1, source_target_pairs={{0,4},{8,12},{1,5},{9,13},{2,6},{10,14},{3,7},{11,15},{16,20},{24,... | collective-permute-start | bytes 1572872 | tf_op jit(solution)/shard_map/back/ppermute | solution.py:54
  57.4 0.7 collective-permute-done.14.r1
  58.2 3.8 %collective-permute-start.15 = (bf16[128,2048]{1,0:T(8,128)(2,1)S(1)}, bf16[128,2048]{1,0:T(8,128)(2,1)S(1)}, u32[]{:S(2)}, u32[]{:S(2)}) collective-permute-start(bf16[128,2048]{1,0:T(8,128)(2,1)S(1)} %slice.8), channel_id=1, source_target_pairs={{0,1},{8,9},{1,2},{9,10},{2,3},{10,11},{3,0},{11,8},{16,17},{24,25... | collective-permute-start | bytes 1572872 | tf_op jit(solution)/shard_map/inputs_up2/ppermute | solution.py:54
  62.0 0.5 collective-permute-start.17
  62.5 7.8 %collective-permute-done.12 = bf16[512,512]{1,0:T(8,128)(2,1)S(1)} collective-permute-done((bf16[512,512]{1,0:T(8,128)(2,1)S(1)}, bf16[512,512]{1,0:T(8,128)(2,1)S(1)}, u32[]{:S(2)}, u32[]{:S(2)}) %collective-permute-start.12) | collective-permute-done | bytes 524320 | tf_op jit(solution)/shard_map/back/ppermute | solution.py:54
  70.2 1.4 %collective-permute-done.15.r2a = bf16[128,2048]{1,0:T(8,128)(2,1)S(1)} collective-permute-done((bf16[128,2048]{1,0:T(8,128)(2,1)S(1)}, bf16[128,2048]{1,0:T(8,128)(2,1)S(1)}, u32[]{:S(2)}, u32[]{:S(2)}) %collective-permute-start.15) | collective-permute-done | bytes 524320 | tf_op jit(solution)/shard_map/inputs_up2/ppermute | solution.py:54
  71.6 4.0 %collective-permute-done.17.r2b = bf16[128,2048]{1,0:T(8,128)(2,1)S(1)} collective-permute-done((bf16[128,2048]{1,0:T(8,128)(2,1)S(1)}, bf16[128,2048]{1,0:T(8,128)(2,1)S(1)}, u32[]{:S(2)}, u32[]{:S(2)}) %collective-permute-start.17) | collective-permute-done | bytes 524320 | tf_op jit(solution)/shard_map/inputs_down2/ppermute | solution.py:54
  75.6 0.2 fusion.k
  75.8 0.1 collective-permute-start.18
  75.9 0.2 gather_a_body.1.g
  76.0 1.4 %far_a_body.1 = (bf16[1024,2048]{1,0:T(8,128)(2,1)S(1)}, bf16[768,256]{1,0:T(8,128)(2,1)S(1)}, bf16[768,256]{1,0:T(8,128)(2,1)S(1)}) custom-call(bf16[768,1024]{1,0:T(8,128)(2,1)S(1)} %gather_a_body.1.g, bf16[256,2048]{1,0:T(8,128)(2,1)S(1)} %pad_maximum_fusion.own, bf16[256,2048]{1,0:T(8,128)(2,1)S(1)} %collective-permute-done.14.r1, ...), custom_call_target="tpu_custom_call" | custom-call | flops 1000000000 | bytes 1000000 | tf_op jit(solution)/shard_map/far_a_body/pallas_call | solution.py:348
  77.4 2.0 %collective-permute-start.19 = (bf16[768,256]{1,0:T(8,128)(2,1)S(1)}, bf16[768,256]{1,0:T(8,128)(2,1)S(1)}, u32[]{:S(2)}, u32[]{:S(2)}) collective-permute-start(bf16[768,256]{1,0:T(8,128)(2,1)S(1)} %get-tuple-element.93), channel_id=1, source_target_pairs={{0,32},{8,40},{1,33},{9,41},{2,34},{10,42},{3,35},{11,43},{16,48},... | collective-permute-start | bytes 1179656 | tf_op jit(solution)/shard_map/reduce_a_far_up/ppermute | solution.py:54
  79.4 2.2 %collective-permute-start.20 = (bf16[768,256]{1,0:T(8,128)(2,1)S(1)}, bf16[768,256]{1,0:T(8,128)(2,1)S(1)}, u32[]{:S(2)}, u32[]{:S(2)}) collective-permute-start(bf16[768,256]{1,0:T(8,128)(2,1)S(1)} %get-tuple-element.101), channel_id=1, source_target_pairs={{0,96},{8,104},{1,97},{9,105},{2,98},{10,106},{3,99},{11,107},{16,... | collective-permute-start | bytes 1179656 | tf_op jit(solution)/shard_map/reduce_a_far_down/ppermute | solution.py:54
  81.6 0.2 gather_b_body.1.g
  81.9 1.0 far_b_body.1
  82.9 2.3 %collective-permute-start.26 = (bf16[384,512]{1,0:T(8,128)(2,1)S(1)}, bf16[384,512]{1,0:T(8,128)(2,1)S(1)}, u32[]{:S(2)}, u32[]{:S(2)}) collective-permute-start(bf16[384,512]{1,0:T(8,128)(2,1)S(1)} %get-tuple-element.96), channel_id=1, source_target_pairs={{0,16},{8,24},{1,17},{9,25},{2,18},{10,26},{3,19},{11,27},{16,4},{... | collective-permute-start | bytes 1179656 | tf_op jit(solution)/shard_map/reduce_b_far_up/ppermute | solution.py:54
  85.2 1.3 %collective-permute-start.27 = (bf16[384,512]{1,0:T(8,128)(2,1)S(1)}, bf16[384,512]{1,0:T(8,128)(2,1)S(1)}, u32[]{:S(2)}, u32[]{:S(2)}) collective-permute-start(bf16[384,512]{1,0:T(8,128)(2,1)S(1)} %get-tuple-element.112), channel_id=1, source_target_pairs={{0,20},{8,28},{1,21},{9,29},{2,22},{10,30},{3,23},{11,31},{16,0},{... | collective-permute-start | bytes 1179656 | tf_op jit(solution)/shard_map/reduce_b_far_down/ppermute | solution.py:54
  86.6 2.6 %near_a_body.1 = (f32[768,512]{1,0:T(8,128)S(1)}, f32[768,512]{1,0:T(8,128)S(1)}, f32[768,512]{1,0:T(8,128)S(1)}) custom-call(bf16[768,1024]{1,0:T(8,128)(2,1)S(1)} %gather_a_body.1.g, bf16[1024,2048]{1,0:T(8,128)(2,1)S(1)} %get-tuple-element.95.x), custom_call_target="tpu_custom_call" | custom-call | flops 1000000000 | bytes 1000000 | tf_op jit(solution)/shard_map/near_a_body/pallas_call | solution.py:387
  89.2 2.1 %collective-permute-done.19.gu = bf16[768,256]{1,0:T(8,128)(2,1)S(1)} collective-permute-done((bf16[768,256]{1,0:T(8,128)(2,1)S(1)}, bf16[768,256]{1,0:T(8,128)(2,1)S(1)}, u32[]{:S(2)}, u32[]{:S(2)}) %collective-permute-start.19) | collective-permute-done | bytes 393248 | tf_op jit(solution)/shard_map/reduce_a_far_up/ppermute | solution.py:54
  91.3 0.2 add_near_body.2
  91.5 1.3 collective-permute-start.21
  92.9 2.0 %collective-permute-start.22 = (bf16[768,512]{1,0:T(8,128)(2,1)S(1)}, bf16[768,512]{1,0:T(8,128)(2,1)S(1)}, u32[]{:S(2)}, u32[]{:S(2)}) collective-permute-start(bf16[768,512]{1,0:T(8,128)(2,1)S(1)} %get-tuple-element.103), channel_id=1, source_target_pairs={{0,96},{8,104},{1,97},{9,105},{2,98},{10,106},{3,99},{11,107},{16,... | collective-permute-start | bytes 2359304 | tf_op jit(solution)/shard_map/reduce_a_down/ppermute | solution.py:54
  94.9 2.6 %near_b_body.1 = (f32[384,1024]{1,0:T(8,128)S(1)}, f32[384,1024]{1,0:T(8,128)S(1)}, f32[384,1024]{1,0:T(8,128)S(1)}) custom-call(bf16[768,1024]{1,0:T(8,128)(2,1)S(1)} %gather_b_body.1.g, bf16[1024,2048]{1,0:T(8,128)(2,1)S(1)} %get-tuple-element.95.x), custom_call_target="tpu_custom_call" | custom-call | flops 1000000000 | bytes 1000000 | tf_op jit(solution)/shard_map/near_b_body/pallas_call | solution.py:403
  97.5 0.2 add_near_body.3
  97.7 2.3 %collective-permute-start.28 = (bf16[384,1024]{1,0:T(8,128)(2,1)S(1)}, bf16[384,1024]{1,0:T(8,128)(2,1)S(1)}, u32[]{:S(2)}, u32[]{:S(2)}) collective-permute-start(bf16[384,1024]{1,0:T(8,128)(2,1)S(1)} %get-tuple-element.113), channel_id=1, source_target_pairs={{0,16},{8,24},{1,17},{9,25},{2,18},{10,26},{3,19},{11,27},{16,4},{... | collective-permute-start | bytes 2359304 | tf_op jit(solution)/shard_map/reduce_b_up/ppermute | solution.py:54
  100.0 1.3 %collective-permute-start.29 = (bf16[384,1024]{1,0:T(8,128)(2,1)S(1)}, bf16[384,1024]{1,0:T(8,128)(2,1)S(1)}, u32[]{:S(2)}, u32[]{:S(2)}) collective-permute-start(bf16[384,1024]{1,0:T(8,128)(2,1)S(1)} %get-tuple-element.114), channel_id=1, source_target_pairs={{0,20},{8,28},{1,21},{9,29},{2,22},{10,30},{3,23},{11,31},{16,0},{... | collective-permute-start | bytes 2359304 | tf_op jit(solution)/shard_map/reduce_b_down/ppermute | solution.py:54
  101.4 10.8 %collective-permute-done.21.refs_1_ = bf16[768,512]{1,0:T(8,128)(2,1)S(1)} collective-permute-done((bf16[768,512]{1,0:T(8,128)(2,1)S(1)}, bf16[768,512]{1,0:T(8,128)(2,1)S(1)}, u32[]{:S(2)}, u32[]{:S(2)}) %collective-permute-start.21) | collective-permute-done | bytes 786464 | tf_op jit(solution)/shard_map/reduce_a_up/ppermute | solution.py:54
  112.2 0.5 add_a_body.1
  112.6 2.3 %collective-permute-start.23 = (bf16[384,256]{1,0:T(8,128)(2,1)S(1)}, bf16[384,256]{1,0:T(8,128)(2,1)S(1)}, u32[]{:S(2)}, u32[]{:S(2)}) collective-permute-start(bf16[384,256]{1,0:T(8,128)(2,1)S(1)} %get-tuple-element.105), channel_id=1, source_target_pairs={{0,16},{8,24},{1,17},{9,25},{2,18},{10,26},{3,19},{11,27},{16,4},{... | collective-permute-start | bytes 589832 | tf_op jit(solution)/shard_map/second_a_x1/ppermute | solution.py:54
  115.0 1.3 %collective-permute-start.24 = (bf16[384,256]{1,0:T(8,128)(2,1)S(1)}, bf16[384,256]{1,0:T(8,128)(2,1)S(1)}, u32[]{:S(2)}, u32[]{:S(2)}) collective-permute-start(bf16[384,256]{1,0:T(8,128)(2,1)S(1)} %get-tuple-element.106), channel_id=1, source_target_pairs={{0,20},{8,28},{1,21},{9,29},{2,22},{10,30},{3,23},{11,31},{16,0},{... | collective-permute-start | bytes 589832 | tf_op jit(solution)/shard_map/second_a_x3/ppermute | solution.py:54
  116.3 2.2 %collective-permute-start.25 = (bf16[384,256]{1,0:T(8,128)(2,1)S(1)}, bf16[384,256]{1,0:T(8,128)(2,1)S(1)}, u32[]{:S(2)}, u32[]{:S(2)}) collective-permute-start(bf16[384,256]{1,0:T(8,128)(2,1)S(1)} %get-tuple-element.107), channel_id=1, source_target_pairs={{0,4},{8,12},{1,5},{9,13},{2,6},{10,14},{3,7},{11,15},{16,20},{24,... | collective-permute-start | bytes 589832 | tf_op jit(solution)/shard_map/second_a_x2/ppermute | solution.py:54
  118.5 1.2 collective-permute-done.28.refs_1_
  119.7 0.8 collective-permute-done.29.refs_2_
  120.5 0.5 add_b_body.1
  121.0 0.1 collective-permute-start.30
  121.1 3.2 %collective-permute-start.31 = (bf16[384,256]{1,0:T(8,128)(2,1)S(1)}, bf16[384,256]{1,0:T(8,128)(2,1)S(1)}, u32[]{:S(2)}, u32[]{:S(2)}) collective-permute-start(bf16[384,256]{1,0:T(8,128)(2,1)S(1)} %get-tuple-element.117), channel_id=1, source_target_pairs={{0,96},{8,104},{1,97},{9,105},{2,98},{10,106},{3,99},{11,107},{16,... | collective-permute-start | bytes 589832 | tf_op jit(solution)/shard_map/second_b_z3/ppermute | solution.py:54
  124.3 0.4 collective-permute-done.24.refs_2_
  124.7 3.2 %collective-permute-done.25.refs_3_ = bf16[384,256]{1,0:T(8,128)(2,1)S(1)} collective-permute-done((bf16[384,256]{1,0:T(8,128)(2,1)S(1)}, bf16[384,256]{1,0:T(8,128)(2,1)S(1)}, u32[]{:S(2)}, u32[]{:S(2)}) %collective-permute-start.25) | collective-permute-done | bytes 196640 | tf_op jit(solution)/shard_map/second_a_x2/ppermute | solution.py:54
  127.9 4.0 %collective-permute-done.30.refs_5_ = bf16[384,256]{1,0:T(8,128)(2,1)S(1)} collective-permute-done((bf16[384,256]{1,0:T(8,128)(2,1)S(1)}, bf16[384,256]{1,0:T(8,128)(2,1)S(1)}, u32[]{:S(2)}, u32[]{:S(2)}) %collective-permute-start.30) | collective-permute-done | bytes 196640 | tf_op jit(solution)/shard_map/second_b_z1/ppermute | solution.py:54
  131.9 1.1 finish_body.1
  (38 shorter events, 0.2 us)
Async XLA Ops:
  3.3 8.9 %collective-permute-start.3 = (bf16[128,640]{1,0:T(8,128)(2,1)}, bf16[128,640]{1,0:T(8,128)(2,1)S(1)}, u32[]{:S(2)}, u32[]{:S(2)}) collective-permute-start(bf16[128,640]{1,0:T(8,128)(2,1)} %get-tuple-element.68), channel_id=1, source_target_pairs={{0,1},{8,9},{1,2},{9,10},{2,3},{10,11},{3,0},{11,8},{16,17},{24,25... | collective-permute-start | bytes 491528 | tf_op jit(solution)/shard_map/keys_y1/ppermute | solution.py:54
  3.5 13.3 %collective-permute-start.4 = (bf16[128,640]{1,0:T(8,128)(2,1)}, bf16[128,640]{1,0:T(8,128)(2,1)S(1)}, u32[]{:S(2)}, u32[]{:S(2)}) collective-permute-start(bf16[128,640]{1,0:T(8,128)(2,1)} %get-tuple-element.69), channel_id=1, source_target_pairs={{0,2},{8,10},{1,3},{9,11},{2,0},{10,8},{3,1},{11,9},{16,18},{24,26... | collective-permute-start | bytes 491528 | tf_op jit(solution)/shard_map/keys_y2/ppermute | solution.py:54
  6.2 10.7 %collective-permute-start.5 = (bf16[128,640]{1,0:T(8,128)(2,1)}, bf16[128,640]{1,0:T(8,128)(2,1)S(1)}, u32[]{:S(2)}, u32[]{:S(2)}) collective-permute-start(bf16[128,640]{1,0:T(8,128)(2,1)} %get-tuple-element.70), channel_id=1, source_target_pairs={{0,3},{8,11},{1,0},{9,8},{2,1},{10,9},{3,2},{11,10},{16,19},{24,27... | collective-permute-start | bytes 491528 | tf_op jit(solution)/shard_map/keys_y3/ppermute | solution.py:54
  8.9 14.0 %collective-permute-start = (bf16[128,1024]{1,0:T(8,128)(2,1)}, bf16[128,1024]{1,0:T(8,128)(2,1)S(1)}, u32[]{:S(2)}, u32[]{:S(2)}) collective-permute-start(bf16[128,1024]{1,0:T(8,128)(2,1)} %get-tuple-element.63), channel_id=1, source_target_pairs={{0,1},{8,9},{1,2},{9,10},{2,3},{10,11},{3,0},{11,8},{16,17},{24,25... | collective-permute-start | bytes 786440 | tf_op jit(solution)/shard_map/queries0_y1/ppermute | solution.py:54
  12.2 14.6 %collective-permute-start.2 = (bf16[128,1024]{1,0:T(8,128)(2,1)}, bf16[128,1024]{1,0:T(8,128)(2,1)S(1)}, u32[]{:S(2)}, u32[]{:S(2)}) collective-permute-start(bf16[128,1024]{1,0:T(8,128)(2,1)} %get-tuple-element.65), channel_id=1, source_target_pairs={{0,3},{8,11},{1,0},{9,8},{2,1},{10,9},{3,2},{11,10},{16,19},{24,27... | collective-permute-start | bytes 786440 | tf_op jit(solution)/shard_map/queries0_y3/ppermute | solution.py:54
  12.2 4.7 %copy-start.2 = (bf16[128,640]{1,0:T(8,128)(2,1)S(1)}, bf16[128,640]{1,0:T(8,128)(2,1)}, u32[]{:S(2)}) copy-start(bf16[128,640]{1,0:T(8,128)(2,1)} %get-tuple-element.61.kv) | copy-start | bytes 491524
  12.2 14.5 %copy-start.5 = (bf16[128,1024]{1,0:T(8,128)(2,1)S(1)}, bf16[128,1024]{1,0:T(8,128)(2,1)}, u32[]{:S(2)}) copy-start(bf16[128,1024]{1,0:T(8,128)(2,1)} %get-tuple-element.76) | copy-start | bytes 786436
  12.2 14.6 %copy-start.4 = (bf16[128,1024]{1,0:T(8,128)(2,1)S(1)}, bf16[128,1024]{1,0:T(8,128)(2,1)}, u32[]{:S(2)}) copy-start(bf16[128,1024]{1,0:T(8,128)(2,1)} %get-tuple-element.78) | copy-start | bytes 786436
  12.2 15.5 %copy-start = (bf16[1,128,4096]{2,1,0:T(8,128)(2,1)S(1)}, bf16[1,128,4096]{2,1,0:T(8,128)(2,1)}, u32[]{:S(2)}) copy-start(bf16[1,128,4096]{2,1,0:T(8,128)(2,1)} %q.2) | copy-start | bytes 3145732
  12.2 15.5 %copy-start.1 = (bf16[1,128,4096]{2,1,0:T(8,128)(2,1)S(1)}, bf16[1,128,4096]{2,1,0:T(8,128)(2,1)}, u32[]{:S(2)}) copy-start(bf16[1,128,4096]{2,1,0:T(8,128)(2,1)} %g.5) | copy-start | bytes 3145732
  12.2 14.5 %collective-permute-start.1 = (bf16[128,1024]{1,0:T(8,128)(2,1)}, bf16[128,1024]{1,0:T(8,128)(2,1)S(1)}, u32[]{:S(2)}, u32[]{:S(2)}) collective-permute-start(bf16[128,1024]{1,0:T(8,128)(2,1)} %get-tuple-element.64), channel_id=1, source_target_pairs={{0,2},{8,10},{1,3},{9,11},{2,0},{10,8},{3,1},{11,9},{16,18},{24,26... | collective-permute-start | bytes 786440 | tf_op jit(solution)/shard_map/queries0_y2/ppermute | solution.py:54
  16.8 11.2 %collective-permute-start.13 = (bf16[128,2048]{1,0:T(8,128)(2,1)}, bf16[128,2048]{1,0:T(8,128)(2,1)S(1)}, u32[]{:S(2)}, u32[]{:S(2)}) collective-permute-start(bf16[128,2048]{1,0:T(8,128)(2,1)} %get-tuple-element.88), channel_id=1, source_target_pairs={{0,8},{8,0},{1,9},{9,1},{2,10},{10,2},{3,11},{11,3},{16,24},{24,16... | collective-permute-start | bytes 1572872 | tf_op jit(solution)/shard_map/swap_inputs/ppermute | solution.py:54
  17.0 18.7 %collective-permute-start.6 = (bf16[512,640]{1,0:T(8,128)(2,1)S(1)}, bf16[512,640]{1,0:T(8,128)(2,1)S(1)}, u32[]{:S(2)}, u32[]{:S(2)}) collective-permute-start(bf16[512,640]{1,0:T(8,128)(2,1)S(1)} %pad_maximum_fusion.1), channel_id=1, source_target_pairs={{0,4},{8,12},{1,5},{9,13},{2,6},{10,14},{3,7},{11,15},{16,20},{24,... | collective-permute-start | bytes 1966088 | tf_op jit(solution)/shard_map/half/ppermute | solution.py:54
  22.8 22.8 %collective-permute-start.8 = (bf16[128,1024]{1,0:T(8,128)(2,1)}, bf16[128,1024]{1,0:T(8,128)(2,1)S(1)}, u32[]{:S(2)}, u32[]{:S(2)}) collective-permute-start(bf16[128,1024]{1,0:T(8,128)(2,1)} %get-tuple-element.74), channel_id=1, source_target_pairs={{0,1},{8,9},{1,2},{9,10},{2,3},{10,11},{3,0},{11,8},{16,17},{24,25... | collective-permute-start | bytes 786440 | tf_op jit(solution)/shard_map/queries1_y1/ppermute | solution.py:54
  26.7 18.9 %collective-permute-start.9 = (bf16[128,1024]{1,0:T(8,128)(2,1)S(1)}, bf16[128,1024]{1,0:T(8,128)(2,1)S(1)}, u32[]{:S(2)}, u32[]{:S(2)}) collective-permute-start(bf16[128,1024]{1,0:T(8,128)(2,1)S(1)} %copy-done.5), channel_id=1, source_target_pairs={{0,2},{8,10},{1,3},{9,11},{2,0},{10,8},{3,1},{11,9},{16,18},{24,26... | collective-permute-start | bytes 786440 | tf_op jit(solution)/shard_map/queries1_y2/ppermute | solution.py:54
  26.7 1.3 copy-start.3
  26.8 18.9 %collective-permute-start.10 = (bf16[128,1024]{1,0:T(8,128)(2,1)S(1)}, bf16[128,1024]{1,0:T(8,128)(2,1)S(1)}, u32[]{:S(2)}, u32[]{:S(2)}) collective-permute-start(bf16[128,1024]{1,0:T(8,128)(2,1)S(1)} %copy-done.4), channel_id=1, source_target_pairs={{0,3},{8,11},{1,0},{9,8},{2,1},{10,9},{3,2},{11,10},{16,19},{24,27... | collective-permute-start | bytes 786440 | tf_op jit(solution)/shard_map/queries1_y3/ppermute | solution.py:54
  28.1 30.0 %collective-permute-start.14 = (bf16[256,2048]{1,0:T(8,128)(2,1)S(1)}, bf16[256,2048]{1,0:T(8,128)(2,1)S(1)}, u32[]{:S(2)}, u32[]{:S(2)}) collective-permute-start(bf16[256,2048]{1,0:T(8,128)(2,1)S(1)} %pad_maximum_fusion.own), channel_id=1, source_target_pairs={{0,1},{8,9},{1,2},{9,10},{2,3},{10,11},{3,0},{11,8},{16,17},{24,25... | collective-permute-start | bytes 3145736 | tf_op jit(solution)/shard_map/inputs_up/ppermute | solution.py:54
  35.7 26.3 %collective-permute-start.16 = (bf16[256,2048]{1,0:T(8,128)(2,1)S(1)}, bf16[256,2048]{1,0:T(8,128)(2,1)S(1)}, u32[]{:S(2)}, u32[]{:S(2)}) collective-permute-start(bf16[256,2048]{1,0:T(8,128)(2,1)S(1)} %pad_maximum_fusion.own), channel_id=1, source_target_pairs={{0,3},{8,11},{1,0},{9,8},{2,1},{10,9},{3,2},{11,10},{16,19},{24,27... | collective-permute-start | bytes 3145736 | tf_op jit(solution)/shard_map/inputs_down/ppermute | solution.py:54
  54.2 8.3 %collective-permute-start.11 = (bf16[512,512]{1,0:T(8,128)(2,1)S(1)}, bf16[512,512]{1,0:T(8,128)(2,1)S(1)}, u32[]{:S(2)}, u32[]{:S(2)}) collective-permute-start(bf16[512,512]{1,0:T(8,128)(2,1)S(1)} %get-tuple-element.81.a1), channel_id=1, source_target_pairs={{0,8},{8,0},{1,9},{9,1},{2,10},{10,2},{3,11},{11,3},{16,24},{24,16... | collective-permute-start | bytes 1572872 | tf_op jit(solution)/shard_map/swap_dq1/ppermute | solution.py:54
  54.3 15.9 %collective-permute-start.12 = (bf16[512,512]{1,0:T(8,128)(2,1)S(1)}, bf16[512,512]{1,0:T(8,128)(2,1)S(1)}, u32[]{:S(2)}, u32[]{:S(2)}) collective-permute-start(bf16[512,512]{1,0:T(8,128)(2,1)S(1)} %pad_maximum_fusion.2), channel_id=1, source_target_pairs={{0,4},{8,12},{1,5},{9,13},{2,6},{10,14},{3,7},{11,15},{16,20},{24,... | collective-permute-start | bytes 1572872 | tf_op jit(solution)/shard_map/back/ppermute | solution.py:54
  58.2 13.4 %collective-permute-start.15 = (bf16[128,2048]{1,0:T(8,128)(2,1)S(1)}, bf16[128,2048]{1,0:T(8,128)(2,1)S(1)}, u32[]{:S(2)}, u32[]{:S(2)}) collective-permute-start(bf16[128,2048]{1,0:T(8,128)(2,1)S(1)} %slice.8), channel_id=1, source_target_pairs={{0,1},{8,9},{1,2},{9,10},{2,3},{10,11},{3,0},{11,8},{16,17},{24,25... | collective-permute-start | bytes 1572872 | tf_op jit(solution)/shard_map/inputs_up2/ppermute | solution.py:54
  62.0 13.6 %collective-permute-start.17 = (bf16[128,2048]{1,0:T(8,128)(2,1)S(1)}, bf16[128,2048]{1,0:T(8,128)(2,1)S(1)}, u32[]{:S(2)}, u32[]{:S(2)}) collective-permute-start(bf16[128,2048]{1,0:T(8,128)(2,1)S(1)} %slice.9), channel_id=1, source_target_pairs={{0,3},{8,11},{1,0},{9,8},{2,1},{10,9},{3,2},{11,10},{16,19},{24,27... | collective-permute-start | bytes 1572872 | tf_op jit(solution)/shard_map/inputs_down2/ppermute | solution.py:54
  62.5 13.4 %collective-permute-start.7 = (bf16[512,512]{1,0:T(8,128)(2,1)S(1)}, bf16[512,512]{1,0:T(8,128)(2,1)S(1)}, u32[]{:S(2)}, u32[]{:S(2)}) collective-permute-start(bf16[512,512]{1,0:T(8,128)(2,1)S(1)} %get-tuple-element.71.a0), channel_id=1, source_target_pairs={{0,8},{8,0},{1,9},{9,1},{2,10},{10,2},{3,11},{11,3},{16,24},{24,16... | collective-permute-start | bytes 1572872 | tf_op jit(solution)/shard_map/swap_dq0/ppermute | solution.py:54
  75.8 5.9 %collective-permute-start.18 = (bf16[512,512]{1,0:T(8,128)(2,1)S(1)}, bf16[512,512]{1,0:T(8,128)(2,1)S(1)}, u32[]{:S(2)}, u32[]{:S(2)}) collective-permute-start(bf16[512,512]{1,0:T(8,128)(2,1)S(1)} %fusion.k), channel_id=1, source_target_pairs={{0,8},{8,0},{1,9},{9,1},{2,10},{10,2},{3,11},{11,3},{16,24},{24,16... | collective-permute-start | bytes 1572872 | tf_op jit(solution)/shard_map/swap_dkv/ppermute | solution.py:54
  77.4 13.9 %collective-permute-start.19 = (bf16[768,256]{1,0:T(8,128)(2,1)S(1)}, bf16[768,256]{1,0:T(8,128)(2,1)S(1)}, u32[]{:S(2)}, u32[]{:S(2)}) collective-permute-start(bf16[768,256]{1,0:T(8,128)(2,1)S(1)} %get-tuple-element.93), channel_id=1, source_target_pairs={{0,32},{8,40},{1,33},{9,41},{2,34},{10,42},{3,35},{11,43},{16,48},... | collective-permute-start | bytes 1179656 | tf_op jit(solution)/shard_map/reduce_a_far_up/ppermute | solution.py:54
  79.4 11.9 %collective-permute-start.20 = (bf16[768,256]{1,0:T(8,128)(2,1)S(1)}, bf16[768,256]{1,0:T(8,128)(2,1)S(1)}, u32[]{:S(2)}, u32[]{:S(2)}) collective-permute-start(bf16[768,256]{1,0:T(8,128)(2,1)S(1)} %get-tuple-element.101), channel_id=1, source_target_pairs={{0,96},{8,104},{1,97},{9,105},{2,98},{10,106},{3,99},{11,107},{16,... | collective-permute-start | bytes 1179656 | tf_op jit(solution)/shard_map/reduce_a_far_down/ppermute | solution.py:54
  82.9 14.6 %collective-permute-start.26 = (bf16[384,512]{1,0:T(8,128)(2,1)S(1)}, bf16[384,512]{1,0:T(8,128)(2,1)S(1)}, u32[]{:S(2)}, u32[]{:S(2)}) collective-permute-start(bf16[384,512]{1,0:T(8,128)(2,1)S(1)} %get-tuple-element.96), channel_id=1, source_target_pairs={{0,16},{8,24},{1,17},{9,25},{2,18},{10,26},{3,19},{11,27},{16,4},{... | collective-permute-start | bytes 1179656 | tf_op jit(solution)/shard_map/reduce_b_far_up/ppermute | solution.py:54
  85.2 12.2 %collective-permute-start.27 = (bf16[384,512]{1,0:T(8,128)(2,1)S(1)}, bf16[384,512]{1,0:T(8,128)(2,1)S(1)}, u32[]{:S(2)}, u32[]{:S(2)}) collective-permute-start(bf16[384,512]{1,0:T(8,128)(2,1)S(1)} %get-tuple-element.112), channel_id=1, source_target_pairs={{0,20},{8,28},{1,21},{9,29},{2,22},{10,30},{3,23},{11,31},{16,0},{... | collective-permute-start | bytes 1179656 | tf_op jit(solution)/shard_map/reduce_b_far_down/ppermute | solution.py:54
  91.5 20.6 %collective-permute-start.21 = (bf16[768,512]{1,0:T(8,128)(2,1)S(1)}, bf16[768,512]{1,0:T(8,128)(2,1)S(1)}, u32[]{:S(2)}, u32[]{:S(2)}) collective-permute-start(bf16[768,512]{1,0:T(8,128)(2,1)S(1)} %get-tuple-element.102), channel_id=1, source_target_pairs={{0,32},{8,40},{1,33},{9,41},{2,34},{10,42},{3,35},{11,43},{16,48},... | collective-permute-start | bytes 2359304 | tf_op jit(solution)/shard_map/reduce_a_up/ppermute | solution.py:54
  92.9 19.3 %collective-permute-start.22 = (bf16[768,512]{1,0:T(8,128)(2,1)S(1)}, bf16[768,512]{1,0:T(8,128)(2,1)S(1)}, u32[]{:S(2)}, u32[]{:S(2)}) collective-permute-start(bf16[768,512]{1,0:T(8,128)(2,1)S(1)} %get-tuple-element.103), channel_id=1, source_target_pairs={{0,96},{8,104},{1,97},{9,105},{2,98},{10,106},{3,99},{11,107},{16,... | collective-permute-start | bytes 2359304 | tf_op jit(solution)/shard_map/reduce_a_down/ppermute | solution.py:54
  97.7 22.0 %collective-permute-start.28 = (bf16[384,1024]{1,0:T(8,128)(2,1)S(1)}, bf16[384,1024]{1,0:T(8,128)(2,1)S(1)}, u32[]{:S(2)}, u32[]{:S(2)}) collective-permute-start(bf16[384,1024]{1,0:T(8,128)(2,1)S(1)} %get-tuple-element.113), channel_id=1, source_target_pairs={{0,16},{8,24},{1,17},{9,25},{2,18},{10,26},{3,19},{11,27},{16,4},{... | collective-permute-start | bytes 2359304 | tf_op jit(solution)/shard_map/reduce_b_up/ppermute | solution.py:54
  100.0 20.5 %collective-permute-start.29 = (bf16[384,1024]{1,0:T(8,128)(2,1)S(1)}, bf16[384,1024]{1,0:T(8,128)(2,1)S(1)}, u32[]{:S(2)}, u32[]{:S(2)}) collective-permute-start(bf16[384,1024]{1,0:T(8,128)(2,1)S(1)} %get-tuple-element.114), channel_id=1, source_target_pairs={{0,20},{8,28},{1,21},{9,29},{2,22},{10,30},{3,23},{11,31},{16,0},{... | collective-permute-start | bytes 2359304 | tf_op jit(solution)/shard_map/reduce_b_down/ppermute | solution.py:54
  112.6 11.7 %collective-permute-start.23 = (bf16[384,256]{1,0:T(8,128)(2,1)S(1)}, bf16[384,256]{1,0:T(8,128)(2,1)S(1)}, u32[]{:S(2)}, u32[]{:S(2)}) collective-permute-start(bf16[384,256]{1,0:T(8,128)(2,1)S(1)} %get-tuple-element.105), channel_id=1, source_target_pairs={{0,16},{8,24},{1,17},{9,25},{2,18},{10,26},{3,19},{11,27},{16,4},{... | collective-permute-start | bytes 589832 | tf_op jit(solution)/shard_map/second_a_x1/ppermute | solution.py:54
  115.0 9.7 %collective-permute-start.24 = (bf16[384,256]{1,0:T(8,128)(2,1)S(1)}, bf16[384,256]{1,0:T(8,128)(2,1)S(1)}, u32[]{:S(2)}, u32[]{:S(2)}) collective-permute-start(bf16[384,256]{1,0:T(8,128)(2,1)S(1)} %get-tuple-element.106), channel_id=1, source_target_pairs={{0,20},{8,28},{1,21},{9,29},{2,22},{10,30},{3,23},{11,31},{16,0},{... | collective-permute-start | bytes 589832 | tf_op jit(solution)/shard_map/second_a_x3/ppermute | solution.py:54
  116.3 11.6 %collective-permute-start.25 = (bf16[384,256]{1,0:T(8,128)(2,1)S(1)}, bf16[384,256]{1,0:T(8,128)(2,1)S(1)}, u32[]{:S(2)}, u32[]{:S(2)}) collective-permute-start(bf16[384,256]{1,0:T(8,128)(2,1)S(1)} %get-tuple-element.107), channel_id=1, source_target_pairs={{0,4},{8,12},{1,5},{9,13},{2,6},{10,14},{3,7},{11,15},{16,20},{24,... | collective-permute-start | bytes 589832 | tf_op jit(solution)/shard_map/second_a_x2/ppermute | solution.py:54
  121.0 10.9 %collective-permute-start.30 = (bf16[384,256]{1,0:T(8,128)(2,1)S(1)}, bf16[384,256]{1,0:T(8,128)(2,1)S(1)}, u32[]{:S(2)}, u32[]{:S(2)}) collective-permute-start(bf16[384,256]{1,0:T(8,128)(2,1)S(1)} %get-tuple-element.116), channel_id=1, source_target_pairs={{0,32},{8,40},{1,33},{9,41},{2,34},{10,42},{3,35},{11,43},{16,48},... | collective-permute-start | bytes 589832 | tf_op jit(solution)/shard_map/second_b_z1/ppermute | solution.py:54
  121.1 10.9 %collective-permute-start.31 = (bf16[384,256]{1,0:T(8,128)(2,1)S(1)}, bf16[384,256]{1,0:T(8,128)(2,1)S(1)}, u32[]{:S(2)}, u32[]{:S(2)}) collective-permute-start(bf16[384,256]{1,0:T(8,128)(2,1)S(1)} %get-tuple-element.117), channel_id=1, source_target_pairs={{0,96},{8,104},{1,97},{9,105},{2,98},{10,106},{3,99},{11,107},{16,... | collective-permute-start | bytes 589832 | tf_op jit(solution)/shard_map/second_b_z3/ppermute | solution.py:54
  124.3 7.6 %collective-permute-start.32 = (bf16[384,256]{1,0:T(8,128)(2,1)S(1)}, bf16[384,256]{1,0:T(8,128)(2,1)S(1)}, u32[]{:S(2)}, u32[]{:S(2)}) collective-permute-start(bf16[384,256]{1,0:T(8,128)(2,1)S(1)} %get-tuple-element.118), channel_id=1, source_target_pairs={{0,64},{8,72},{1,65},{9,73},{2,66},{10,74},{3,67},{11,75},{16,80},... | collective-permute-start | bytes 589832 | tf_op jit(solution)/shard_map/second_b_z2/ppermute | solution.py:54

commit v5 on v4

--- a/solution.py
+++ b/solution.py
@@ -91,19 +91,20 @@
             for h in range(2):
                 cols = pl.ds(mult(h * 4 + lax.rem(y + d, 4), 128), 128)
                 todo += [
-                    (k.at[0, :, cols], o.at[:, h * 256 : h * 256 + 128]),
-                    (v.at[0, :, cols], o.at[:, h * 256 + 128 : h * 256 + 256]),
+                    (k.at[0, :, cols], o.at[0:128, h * 256 : h * 256 + 128]),
+                    (v.at[0, :, cols], o.at[0:128, h * 256 + 128 : h * 256 + 256]),
                 ]
         made = start_copies(todo, sems)
-        spread = jnp.broadcast_to(i[...].astype(F32), (128, 128)).T.astype(BF16)
+        spread = jnp.broadcast_to(i[...].astype(F32), (16, 128)).astype(BF16)
         for o in (k1, k2, k3, k0):
-            o[:, 512:640] = spread
+            for part in range(4):
+                o[128:144, part * 128 : (part + 1) * 128] = spread
         for m in made:
             m.wait()
 
     return call(
         pack_keys_body,
-        [jax.ShapeDtypeStruct((128, 640), BF16)] * 4,
+        [jax.ShapeDtypeStruct((144, 512), BF16)] * 4,
         [pltpu.SemaphoreType.DMA((16,))],
         10**8,
         10**6,
@@ -190,27 +191,28 @@
         for d, k in ((0, kv), (1, k1), (2, k2), (3, k3)):
             r = mult(lax.rem(y - d + 4, 4), 128)
             todo += [
-                (k.at[:, h * 256 : h * 256 + 128], ks.at[pl.ds(r + 512, 128), :]),
-                (k.at[:, h * 256 + 128 : h * 256 + 256], vs.at[pl.ds(r + 512, 128), :]),
-                (k.at[:, 512:640], ids.at[pl.ds(r + 512, 128), :]),
+                (k.at[0:128, h * 256 : h * 256 + 128], ks.at[pl.ds(r + 512, 128), :]),
+                (k.at[0:128, h * 256 + 128 : h * 256 + 256], vs.at[pl.ds(r + 512, 128), :]),
+                (k.at[128:144, 0:128], ids.at[d * 16 + 64 : d * 16 + 80, :]),
             ]
-            rows = pl.ds(d * 128, 128)
+            lo = d * 144
             todo += [
-                (pv.at[rows, h * 256 : h * 256 + 128], ks.at[pl.ds(r, 128), :]),
-                (pv.at[rows, h * 256 + 128 : h * 256 + 256], vs.at[pl.ds(r, 128), :]),
-                (pv.at[rows, 512:640], ids.at[pl.ds(r, 128), :]),
+                (pv.at[lo : lo + 128, h * 256 : h * 256 + 128], ks.at[pl.ds(r, 128), :]),
+                (pv.at[lo : lo + 128, h * 256 + 128 : h * 256 + 256], vs.at[pl.ds(r, 128), :]),
+                (pv.at[lo + 128 : lo + 144, 0:128], ids.at[d * 16 : d * 16 + 16, :]),
             ]
         run_copies(todo, sems)
 
         low = xh * 512
-        own_ids = ids[512:1024, :].astype(F32)
-        prev_ids = ids[0:512, :].astype(F32)
+        own_ids = ids[64:128, :].astype(F32)
+        prev_ids = ids[0:64, :].astype(F32)
         second = xh.astype(F32)
 
         def count(top):
-            a = jnp.sum(jnp.where(own_ids <= top, 1.0, 0.0), axis=0, keepdims=True)
-            b = jnp.sum(jnp.where(prev_ids <= top, 1.0, 0.0), axis=0, keepdims=True)
-            return (a + second * b)[:, 0:1].astype(jnp.int32)
+            a = jnp.where(own_ids <= top, 1.0, 0.0)
+            b = jnp.where(prev_ids <= top, 1.0, 0.0)
+            each = jnp.sum(a + second * b, axis=1, keepdims=True)
+            return (jnp.sum(each, axis=0, keepdims=True) * (1.0 / 16)).astype(jnp.int32)
 
         first, both = count(0.5), count(1.5)
         acck[...] = jnp.zeros_like(acck)
@@ -262,7 +264,7 @@
         [
             pltpu.VMEM((1024, 128), BF16),
             pltpu.VMEM((1024, 128), BF16),
-            pltpu.VMEM((1024, 128), BF16),
+            pltpu.VMEM((128, 128), BF16),
             pltpu.VMEM((2, 768, 256), F32),
             pltpu.VMEM((1024, 128), F32),
             pltpu.VMEM((1024, 128), F32),

time: 133 us -> 132 us (level)
  starting transfers between devices: 52.3 us -> 49.9 us
  waiting for transfers between devices: 44.3 us -> 45.8 us
    ppermute x33, starting transfers between devices: 52.3 us -> 49.9 us  [send(): return lax.ppermute(a, ('grp', 'sp'), pairs(**k))]
    ppermute x33, waiting for transfers between devices: 44.3 us -> 45.8 us  [send(): return lax.ppermute(a, ('grp', 'sp'), pairs(**k))]
  transfers between devices with their start and end apart: 33 -> 33, of which waited for: 13 -> 15; matrix products, arithmetic and copies ran while one was open for 0% -> 0% of each run, Pallas kernels for 23% -> 23%
where the time goes in v5:
time: 132 us
  starting transfers between devices  49.9 us (38%)
  waiting for transfers between devices  45.8 us (35%)
  Pallas kernels  34.5 us (26%)
    ppermute x33, starting transfers between devices, send(): return lax.ppermute(a, ('grp', 'sp'), pairs(**k))  49.9 us
    ppermute x33, waiting for transfers between devices, send(): return lax.ppermute(a, ('grp', 'sp'), pairs(**k))  45.8 us
    pallas_call x2, Pallas kernels, attention(): call(attention_body, [jax.ShapeDtypeStruct((512, 512), BF16), jax.ShapeDt...  15.7 us
    pallas_call x1, Pallas kernels, pack_queries(): call(pack_queries_body, [jax.ShapeDtypeStruct((128, 1024), BF16)] * 6, [p...  2.69 us
  transfers between devices with their start and end apart: 33, of which 15 were waited for; matrix products, arithmetic and copies ran while one was open for 0% of the time, Pallas kernels for 23%

profile of v5, /device:TPU:24, one launch (start us, length us, event | category | flops | bytes accessed | tf_op | source)
XLA Modules:
  0.0 132.1 jit_solution(2118474583896722732)
XLA Ops:
  0.6 2.6 %pack_keys_body.1 = (bf16[144,512]{1,0:T(8,128)(2,1)}, bf16[144,512]{1,0:T(8,128)(2,1)}, bf16[144,512]{1,0:T(8,128)(2,1)}, bf16[144,512]{1,0:T(8,128)(2,1)}) custom-call(bf16[1,128,1024]{2,1,0:T(8,128)(2,1)} %k.1, bf16[1,128,1024]{2,1,0:T(8,128)(2,1)} %v.1, s32[1,128]{1,0:T(1,128)} %i.1), custom_call_target="tpu_custom_call" | custom-call | flops 100000000 | bytes 1000000 | tf_op jit(solution)/shard_map/pack_keys_body/pallas_call | solution.py:105
  3.2 0.2 collective-permute-start.3
  3.4 2.7 %collective-permute-start.4 = (bf16[144,512]{1,0:T(8,128)(2,1)}, bf16[144,512]{1,0:T(8,128)(2,1)S(1)}, u32[]{:S(2)}, u32[]{:S(2)}) collective-permute-start(bf16[144,512]{1,0:T(8,128)(2,1)} %get-tuple-element.69), channel_id=1, source_target_pairs={{0,2},{8,10},{1,3},{9,11},{2,0},{10,8},{3,1},{11,9},{16,18},{24,26... | collective-permute-start | bytes 442376 | tf_op jit(solution)/shard_map/keys_y2/ppermute | solution.py:54
  6.1 2.7 %pack_queries_body.1 = (bf16[128,1024]{1,0:T(8,128)(2,1)}, bf16[128,1024]{1,0:T(8,128)(2,1)}, bf16[128,1024]{1,0:T(8,128)(2,1)}, bf16[128,1024]{1,0:T(8,128)(2,1...) custom-call(bf16[1,128,4096]{2,1,0:T(8,128)(2,1)} %q.2, bf16[1,128,4096]{2,1,0:T(8,128)(2,1)} %g.5), custom_call_target="tpu_custom_call" | custom-call | flops 100000000 | bytes 1000000 | tf_op jit(solution)/shard_map/pack_queries_body/pallas_call | solution.py:129
  8.8 3.3 %collective-permute-start = (bf16[128,1024]{1,0:T(8,128)(2,1)}, bf16[128,1024]{1,0:T(8,128)(2,1)S(1)}, u32[]{:S(2)}, u32[]{:S(2)}) collective-permute-start(bf16[128,1024]{1,0:T(8,128)(2,1)} %get-tuple-element.63), channel_id=1, source_target_pairs={{0,1},{8,9},{1,2},{9,10},{2,3},{10,11},{3,0},{11,8},{16,17},{24,25... | collective-permute-start | bytes 786440 | tf_op jit(solution)/shard_map/queries0_y1/ppermute | solution.py:54
  12.2 2.2 %collective-permute-start.1 = (bf16[128,1024]{1,0:T(8,128)(2,1)}, bf16[128,1024]{1,0:T(8,128)(2,1)S(1)}, u32[]{:S(2)}, u32[]{:S(2)}) collective-permute-start(bf16[128,1024]{1,0:T(8,128)(2,1)} %get-tuple-element.64), channel_id=1, source_target_pairs={{0,2},{8,10},{1,3},{9,11},{2,0},{10,8},{3,1},{11,9},{16,18},{24,26... | collective-permute-start | bytes 786440 | tf_op jit(solution)/shard_map/queries0_y2/ppermute | solution.py:54
  14.4 2.3 %pack_inputs_body.1 = (bf16[128,2048]{1,0:T(8,128)(2,1)}, bf16[128,2048]{1,0:T(8,128)(2,1)}) custom-call(bf16[1,128,4096]{2,1,0:T(8,128)(2,1)} %x), custom_call_target="tpu_custom_call" | custom-call | flops 1000000000 | bytes 1000000 | tf_op jit(solution)/shard_map/pack_inputs_body/pallas_call | solution.py:153
  16.7 0.1 collective-permute-start.13
  16.9 3.1 %collective-permute-start.6 = (bf16[576,512]{1,0:T(8,128)(2,1)S(1)}, bf16[576,512]{1,0:T(8,128)(2,1)S(1)}, u32[]{:S(2)}, u32[]{:S(2)}) collective-permute-start(bf16[576,512]{1,0:T(8,128)(2,1)S(1)} %pad_maximum_fusion.1), channel_id=1, source_target_pairs={{0,4},{8,12},{1,5},{9,13},{2,6},{10,14},{3,7},{11,15},{16,20},{24,... | collective-permute-start | bytes 1769480 | tf_op jit(solution)/shard_map/half/ppermute | solution.py:54
  20.0 3.6 %collective-permute-done.q1 = bf16[128,1024]{1,0:T(8,128)(2,1)S(1)} collective-permute-done((bf16[128,1024]{1,0:T(8,128)(2,1)}, bf16[128,1024]{1,0:T(8,128)(2,1)S(1)}, u32[]{:S(2)}, u32[]{:S(2)}) %collective-permute-start) | collective-permute-done | bytes 262176 | tf_op jit(solution)/shard_map/queries0_y1/ppermute | solution.py:54
  23.6 3.7 %collective-permute-start.8 = (bf16[128,1024]{1,0:T(8,128)(2,1)}, bf16[128,1024]{1,0:T(8,128)(2,1)S(1)}, u32[]{:S(2)}, u32[]{:S(2)}) collective-permute-start(bf16[128,1024]{1,0:T(8,128)(2,1)} %get-tuple-element.74), channel_id=1, source_target_pairs={{0,1},{8,9},{1,2},{9,10},{2,3},{10,11},{3,0},{11,8},{16,17},{24,25... | collective-permute-start | bytes 786440 | tf_op jit(solution)/shard_map/queries1_y1/ppermute | solution.py:54
  27.4 1.8 %collective-permute-done.2.q3 = bf16[128,1024]{1,0:T(8,128)(2,1)S(1)} collective-permute-done((bf16[128,1024]{1,0:T(8,128)(2,1)}, bf16[128,1024]{1,0:T(8,128)(2,1)S(1)}, u32[]{:S(2)}, u32[]{:S(2)}) %collective-permute-start.2) | collective-permute-done | bytes 262176 | tf_op jit(solution)/shard_map/queries0_y3/ppermute | solution.py:54
  29.2 0.4 collective-permute-start.10
  29.6 0.2 arrange_body.2
  29.9 0.3 copy-done.3
  30.2 0.1 pad_maximum_fusion.own
  30.4 2.6 %collective-permute-start.14 = (bf16[256,2048]{1,0:T(8,128)(2,1)S(1)}, bf16[256,2048]{1,0:T(8,128)(2,1)S(1)}, u32[]{:S(2)}, u32[]{:S(2)}) collective-permute-start(bf16[256,2048]{1,0:T(8,128)(2,1)S(1)} %pad_maximum_fusion.own), channel_id=1, source_target_pairs={{0,1},{8,9},{1,2},{9,10},{2,3},{10,11},{3,0},{11,8},{16,17},{24,25... | collective-permute-start | bytes 3145736 | tf_op jit(solution)/shard_map/inputs_up/ppermute | solution.py:54
  33.0 1.2 collective-permute-done.6.pv
  34.2 2.0 %collective-permute-start.16 = (bf16[256,2048]{1,0:T(8,128)(2,1)S(1)}, bf16[256,2048]{1,0:T(8,128)(2,1)S(1)}, u32[]{:S(2)}, u32[]{:S(2)}) collective-permute-start(bf16[256,2048]{1,0:T(8,128)(2,1)S(1)} %pad_maximum_fusion.own), channel_id=1, source_target_pairs={{0,3},{8,11},{1,0},{9,8},{2,1},{10,9},{3,2},{11,10},{16,19},{24,27... | collective-permute-start | bytes 3145736 | tf_op jit(solution)/shard_map/inputs_down/ppermute | solution.py:54
  36.2 7.8 %attention_body.2 = (bf16[512,512]{1,0:T(8,128)(2,1)S(1)}, f32[256,512]{1,0:T(8,128)S(1)}, bf16[256,512]{1,0:T(8,128)(2,1)S(1)}) custom-call(bf16[512,512]{1,0:T(8,128)(2,1)S(1)} %get-tuple-element.66.qs, bf16[512,512]{1,0:T(8,128)(2,1)S(1)} %get-tuple-element.67.gs, bf16[144,512]{1,0:T(8,128)(2,1)S(1)} %copy-done.2, ...), custom_call_target="tpu_custom_call" | custom-call | flops 12000000000 | bytes 1000000 | tf_op jit(solution)/shard_map/attention_body/pallas_call | solution.py:257
  44.0 0.5 arrange_body.3
  44.5 7.9 %attention_body.3 = (bf16[512,512]{1,0:T(8,128)(2,1)S(1)}, f32[256,512]{1,0:T(8,128)S(1)}, bf16[256,512]{1,0:T(8,128)(2,1)S(1)}) custom-call(bf16[512,512]{1,0:T(8,128)(2,1)S(1)} %get-tuple-element.79.qs, bf16[512,512]{1,0:T(8,128)(2,1)S(1)} %get-tuple-element.80.gs, bf16[144,512]{1,0:T(8,128)(2,1)S(1)} %copy-done.2, ...), custom_call_target="tpu_custom_call" | custom-call | flops 12000000000 | bytes 1000000 | tf_op jit(solution)/shard_map/attention_body/pallas_call | solution.py:257
  52.4 0.1 collective-permute-start.11
  52.5 3.1 %collective-permute-start.12 = (bf16[512,512]{1,0:T(8,128)(2,1)S(1)}, bf16[512,512]{1,0:T(8,128)(2,1)S(1)}, u32[]{:S(2)}, u32[]{:S(2)}) collective-permute-start(bf16[512,512]{1,0:T(8,128)(2,1)S(1)} %pad_maximum_fusion.2), channel_id=1, source_target_pairs={{0,4},{8,12},{1,5},{9,13},{2,6},{10,14},{3,7},{11,15},{16,20},{24,... | collective-permute-start | bytes 1572872 | tf_op jit(solution)/shard_map/back/ppermute | solution.py:54
  55.6 1.7 %collective-permute-done.14.r1 = bf16[256,2048]{1,0:T(8,128)(2,1)S(1)} collective-permute-done((bf16[256,2048]{1,0:T(8,128)(2,1)S(1)}, bf16[256,2048]{1,0:T(8,128)(2,1)S(1)}, u32[]{:S(2)}, u32[]{:S(2)}) %collective-permute-start.14) | collective-permute-done | bytes 1048608 | tf_op jit(solution)/shard_map/inputs_up/ppermute | solution.py:54
  57.3 3.3 %collective-permute-start.15 = (bf16[128,2048]{1,0:T(8,128)(2,1)S(1)}, bf16[128,2048]{1,0:T(8,128)(2,1)S(1)}, u32[]{:S(2)}, u32[]{:S(2)}) collective-permute-start(bf16[128,2048]{1,0:T(8,128)(2,1)S(1)} %slice.8), channel_id=1, source_target_pairs={{0,1},{8,9},{1,2},{9,10},{2,3},{10,11},{3,0},{11,8},{16,17},{24,25... | collective-permute-start | bytes 1572872 | tf_op jit(solution)/shard_map/inputs_up2/ppermute | solution.py:54
  60.7 1.5 %collective-permute-done.16.r3 = bf16[256,2048]{1,0:T(8,128)(2,1)S(1)} collective-permute-done((bf16[256,2048]{1,0:T(8,128)(2,1)S(1)}, bf16[256,2048]{1,0:T(8,128)(2,1)S(1)}, u32[]{:S(2)}, u32[]{:S(2)}) %collective-permute-start.16) | collective-permute-done | bytes 1048608 | tf_op jit(solution)/shard_map/inputs_down/ppermute | solution.py:54
  62.3 0.1 collective-permute-start.7
  62.4 6.0 %collective-permute-done.12 = bf16[512,512]{1,0:T(8,128)(2,1)S(1)} collective-permute-done((bf16[512,512]{1,0:T(8,128)(2,1)S(1)}, bf16[512,512]{1,0:T(8,128)(2,1)S(1)}, u32[]{:S(2)}, u32[]{:S(2)}) %collective-permute-start.12) | collective-permute-done | bytes 524320 | tf_op jit(solution)/shard_map/back/ppermute | solution.py:54
  68.4 1.4 %collective-permute-done.15.r2a = bf16[128,2048]{1,0:T(8,128)(2,1)S(1)} collective-permute-done((bf16[128,2048]{1,0:T(8,128)(2,1)S(1)}, bf16[128,2048]{1,0:T(8,128)(2,1)S(1)}, u32[]{:S(2)}, u32[]{:S(2)}) %collective-permute-start.15) | collective-permute-done | bytes 524320 | tf_op jit(solution)/shard_map/inputs_up2/ppermute | solution.py:54
  69.8 5.7 %collective-permute-done.17.r2b = bf16[128,2048]{1,0:T(8,128)(2,1)S(1)} collective-permute-done((bf16[128,2048]{1,0:T(8,128)(2,1)S(1)}, bf16[128,2048]{1,0:T(8,128)(2,1)S(1)}, u32[]{:S(2)}, u32[]{:S(2)}) %collective-permute-start.17) | collective-permute-done | bytes 524320 | tf_op jit(solution)/shard_map/inputs_down2/ppermute | solution.py:54
  75.5 0.2 fusion.k
  75.7 0.1 collective-permute-start.18
  75.8 0.2 gather_a_body.1.g
  75.9 1.4 %far_a_body.1 = (bf16[1024,2048]{1,0:T(8,128)(2,1)S(1)}, bf16[768,256]{1,0:T(8,128)(2,1)S(1)}, bf16[768,256]{1,0:T(8,128)(2,1)S(1)}) custom-call(bf16[768,1024]{1,0:T(8,128)(2,1)S(1)} %gather_a_body.1.g, bf16[256,2048]{1,0:T(8,128)(2,1)S(1)} %pad_maximum_fusion.own, bf16[256,2048]{1,0:T(8,128)(2,1)S(1)} %collective-permute-done.14.r1, ...), custom_call_target="tpu_custom_call" | custom-call | flops 1000000000 | bytes 1000000 | tf_op jit(solution)/shard_map/far_a_body/pallas_call | solution.py:350
  77.4 2.0 %collective-permute-start.19 = (bf16[768,256]{1,0:T(8,128)(2,1)S(1)}, bf16[768,256]{1,0:T(8,128)(2,1)S(1)}, u32[]{:S(2)}, u32[]{:S(2)}) collective-permute-start(bf16[768,256]{1,0:T(8,128)(2,1)S(1)} %get-tuple-element.93), channel_id=1, source_target_pairs={{0,32},{8,40},{1,33},{9,41},{2,34},{10,42},{3,35},{11,43},{16,48},... | collective-permute-start | bytes 1179656 | tf_op jit(solution)/shard_map/reduce_a_far_up/ppermute | solution.py:54
  79.3 2.2 %collective-permute-start.20 = (bf16[768,256]{1,0:T(8,128)(2,1)S(1)}, bf16[768,256]{1,0:T(8,128)(2,1)S(1)}, u32[]{:S(2)}, u32[]{:S(2)}) collective-permute-start(bf16[768,256]{1,0:T(8,128)(2,1)S(1)} %get-tuple-element.101), channel_id=1, source_target_pairs={{0,96},{8,104},{1,97},{9,105},{2,98},{10,106},{3,99},{11,107},{16,... | collective-permute-start | bytes 1179656 | tf_op jit(solution)/shard_map/reduce_a_far_down/ppermute | solution.py:54
  81.6 0.2 gather_b_body.1.g
  81.8 1.0 far_b_body.1
  82.8 1.8 %collective-permute-start.26 = (bf16[384,512]{1,0:T(8,128)(2,1)S(1)}, bf16[384,512]{1,0:T(8,128)(2,1)S(1)}, u32[]{:S(2)}, u32[]{:S(2)}) collective-permute-start(bf16[384,512]{1,0:T(8,128)(2,1)S(1)} %get-tuple-element.96), channel_id=1, source_target_pairs={{0,16},{8,24},{1,17},{9,25},{2,18},{10,26},{3,19},{11,27},{16,4},{... | collective-permute-start | bytes 1179656 | tf_op jit(solution)/shard_map/reduce_b_far_up/ppermute | solution.py:54
  84.6 1.8 %collective-permute-start.27 = (bf16[384,512]{1,0:T(8,128)(2,1)S(1)}, bf16[384,512]{1,0:T(8,128)(2,1)S(1)}, u32[]{:S(2)}, u32[]{:S(2)}) collective-permute-start(bf16[384,512]{1,0:T(8,128)(2,1)S(1)} %get-tuple-element.112), channel_id=1, source_target_pairs={{0,20},{8,28},{1,21},{9,29},{2,22},{10,30},{3,23},{11,31},{16,0},{... | collective-permute-start | bytes 1179656 | tf_op jit(solution)/shard_map/reduce_b_far_down/ppermute | solution.py:54
  86.4 2.6 %near_a_body.1 = (f32[768,512]{1,0:T(8,128)S(1)}, f32[768,512]{1,0:T(8,128)S(1)}, f32[768,512]{1,0:T(8,128)S(1)}) custom-call(bf16[768,1024]{1,0:T(8,128)(2,1)S(1)} %gather_a_body.1.g, bf16[1024,2048]{1,0:T(8,128)(2,1)S(1)} %get-tuple-element.95.x), custom_call_target="tpu_custom_call" | custom-call | flops 1000000000 | bytes 1000000 | tf_op jit(solution)/shard_map/near_a_body/pallas_call | solution.py:389
  89.0 2.2 %collective-permute-done.19.gu = bf16[768,256]{1,0:T(8,128)(2,1)S(1)} collective-permute-done((bf16[768,256]{1,0:T(8,128)(2,1)S(1)}, bf16[768,256]{1,0:T(8,128)(2,1)S(1)}, u32[]{:S(2)}, u32[]{:S(2)}) %collective-permute-start.19) | collective-permute-done | bytes 393248 | tf_op jit(solution)/shard_map/reduce_a_far_up/ppermute | solution.py:54
  91.2 0.2 add_near_body.2
  91.5 1.3 collective-permute-start.21
  92.8 2.0 %collective-permute-start.22 = (bf16[768,512]{1,0:T(8,128)(2,1)S(1)}, bf16[768,512]{1,0:T(8,128)(2,1)S(1)}, u32[]{:S(2)}, u32[]{:S(2)}) collective-permute-start(bf16[768,512]{1,0:T(8,128)(2,1)S(1)} %get-tuple-element.103), channel_id=1, source_target_pairs={{0,96},{8,104},{1,97},{9,105},{2,98},{10,106},{3,99},{11,107},{16,... | collective-permute-start | bytes 2359304 | tf_op jit(solution)/shard_map/reduce_a_down/ppermute | solution.py:54
  94.8 2.6 %near_b_body.1 = (f32[384,1024]{1,0:T(8,128)S(1)}, f32[384,1024]{1,0:T(8,128)S(1)}, f32[384,1024]{1,0:T(8,128)S(1)}) custom-call(bf16[768,1024]{1,0:T(8,128)(2,1)S(1)} %gather_b_body.1.g, bf16[1024,2048]{1,0:T(8,128)(2,1)S(1)} %get-tuple-element.95.x), custom_call_target="tpu_custom_call" | custom-call | flops 1000000000 | bytes 1000000 | tf_op jit(solution)/shard_map/near_b_body/pallas_call | solution.py:405
  97.4 0.2 add_near_body.3
  97.6 1.5 %collective-permute-start.28 = (bf16[384,1024]{1,0:T(8,128)(2,1)S(1)}, bf16[384,1024]{1,0:T(8,128)(2,1)S(1)}, u32[]{:S(2)}, u32[]{:S(2)}) collective-permute-start(bf16[384,1024]{1,0:T(8,128)(2,1)S(1)} %get-tuple-element.113), channel_id=1, source_target_pairs={{0,16},{8,24},{1,17},{9,25},{2,18},{10,26},{3,19},{11,27},{16,4},{... | collective-permute-start | bytes 2359304 | tf_op jit(solution)/shard_map/reduce_b_up/ppermute | solution.py:54
  99.1 1.8 %collective-permute-start.29 = (bf16[384,1024]{1,0:T(8,128)(2,1)S(1)}, bf16[384,1024]{1,0:T(8,128)(2,1)S(1)}, u32[]{:S(2)}, u32[]{:S(2)}) collective-permute-start(bf16[384,1024]{1,0:T(8,128)(2,1)S(1)} %get-tuple-element.114), channel_id=1, source_target_pairs={{0,20},{8,28},{1,21},{9,29},{2,22},{10,30},{3,23},{11,31},{16,0},{... | collective-permute-start | bytes 2359304 | tf_op jit(solution)/shard_map/reduce_b_down/ppermute | solution.py:54
  100.9 11.2 %collective-permute-done.21.refs_1_ = bf16[768,512]{1,0:T(8,128)(2,1)S(1)} collective-permute-done((bf16[768,512]{1,0:T(8,128)(2,1)S(1)}, bf16[768,512]{1,0:T(8,128)(2,1)S(1)}, u32[]{:S(2)}, u32[]{:S(2)}) %collective-permute-start.21) | collective-permute-done | bytes 786464 | tf_op jit(solution)/shard_map/reduce_a_up/ppermute | solution.py:54
  112.1 0.5 add_a_body.1
  112.6 1.5 %collective-permute-start.23 = (bf16[384,256]{1,0:T(8,128)(2,1)S(1)}, bf16[384,256]{1,0:T(8,128)(2,1)S(1)}, u32[]{:S(2)}, u32[]{:S(2)}) collective-permute-start(bf16[384,256]{1,0:T(8,128)(2,1)S(1)} %get-tuple-element.105), channel_id=1, source_target_pairs={{0,16},{8,24},{1,17},{9,25},{2,18},{10,26},{3,19},{11,27},{16,4},{... | collective-permute-start | bytes 589832 | tf_op jit(solution)/shard_map/second_a_x1/ppermute | solution.py:54
  114.1 1.8 %collective-permute-start.24 = (bf16[384,256]{1,0:T(8,128)(2,1)S(1)}, bf16[384,256]{1,0:T(8,128)(2,1)S(1)}, u32[]{:S(2)}, u32[]{:S(2)}) collective-permute-start(bf16[384,256]{1,0:T(8,128)(2,1)S(1)} %get-tuple-element.106), channel_id=1, source_target_pairs={{0,20},{8,28},{1,21},{9,29},{2,22},{10,30},{3,23},{11,31},{16,0},{... | collective-permute-start | bytes 589832 | tf_op jit(solution)/shard_map/second_a_x3/ppermute | solution.py:54
  115.9 1.7 %collective-permute-start.25 = (bf16[384,256]{1,0:T(8,128)(2,1)S(1)}, bf16[384,256]{1,0:T(8,128)(2,1)S(1)}, u32[]{:S(2)}, u32[]{:S(2)}) collective-permute-start(bf16[384,256]{1,0:T(8,128)(2,1)S(1)} %get-tuple-element.107), channel_id=1, source_target_pairs={{0,4},{8,12},{1,5},{9,13},{2,6},{10,14},{3,7},{11,15},{16,20},{24,... | collective-permute-start | bytes 589832 | tf_op jit(solution)/shard_map/second_a_x2/ppermute | solution.py:54
  117.6 1.8 %collective-permute-done.28.refs_1_ = bf16[384,1024]{1,0:T(8,128)(2,1)S(1)} collective-permute-done((bf16[384,1024]{1,0:T(8,128)(2,1)S(1)}, bf16[384,1024]{1,0:T(8,128)(2,1)S(1)}, u32[]{:S(2)}, u32[]{:S(2)}) %collective-permute-start.28) | collective-permute-done | bytes 786464 | tf_op jit(solution)/shard_map/reduce_b_up/ppermute | solution.py:54
  119.4 0.2 collective-permute-done.29.refs_2_
  119.6 0.5 add_b_body.1
  120.2 3.2 %collective-permute-start.31 = (bf16[384,256]{1,0:T(8,128)(2,1)S(1)}, bf16[384,256]{1,0:T(8,128)(2,1)S(1)}, u32[]{:S(2)}, u32[]{:S(2)}) collective-permute-start(bf16[384,256]{1,0:T(8,128)(2,1)S(1)} %get-tuple-element.117), channel_id=1, source_target_pairs={{0,96},{8,104},{1,97},{9,105},{2,98},{10,106},{3,99},{11,107},{16,... | collective-permute-start | bytes 589832 | tf_op jit(solution)/shard_map/second_b_z3/ppermute | solution.py:54
  123.4 0.1 collective-permute-start.32
  123.5 1.9 %collective-permute-done.24.refs_2_ = bf16[384,256]{1,0:T(8,128)(2,1)S(1)} collective-permute-done((bf16[384,256]{1,0:T(8,128)(2,1)S(1)}, bf16[384,256]{1,0:T(8,128)(2,1)S(1)}, u32[]{:S(2)}, u32[]{:S(2)}) %collective-permute-start.24) | collective-permute-done | bytes 196640 | tf_op jit(solution)/shard_map/second_a_x3/ppermute | solution.py:54
  125.4 1.6 %collective-permute-done.25.refs_3_ = bf16[384,256]{1,0:T(8,128)(2,1)S(1)} collective-permute-done((bf16[384,256]{1,0:T(8,128)(2,1)S(1)}, bf16[384,256]{1,0:T(8,128)(2,1)S(1)}, u32[]{:S(2)}, u32[]{:S(2)}) %collective-permute-start.25) | collective-permute-done | bytes 196640 | tf_op jit(solution)/shard_map/second_a_x2/ppermute | solution.py:54
  127.0 4.0 %collective-permute-done.30.refs_5_ = bf16[384,256]{1,0:T(8,128)(2,1)S(1)} collective-permute-done((bf16[384,256]{1,0:T(8,128)(2,1)S(1)}, bf16[384,256]{1,0:T(8,128)(2,1)S(1)}, u32[]{:S(2)}, u32[]{:S(2)}) %collective-permute-start.30) | collective-permute-done | bytes 196640 | tf_op jit(solution)/shard_map/second_b_z1/ppermute | solution.py:54
  131.0 1.1 finish_body.1
  (38 shorter events, 0.4 us)
Async XLA Ops:
  3.2 8.9 %collective-permute-start.3 = (bf16[144,512]{1,0:T(8,128)(2,1)}, bf16[144,512]{1,0:T(8,128)(2,1)S(1)}, u32[]{:S(2)}, u32[]{:S(2)}) collective-permute-start(bf16[144,512]{1,0:T(8,128)(2,1)} %get-tuple-element.68), channel_id=1, source_target_pairs={{0,1},{8,9},{1,2},{9,10},{2,3},{10,11},{3,0},{11,8},{16,17},{24,25... | collective-permute-start | bytes 442376 | tf_op jit(solution)/shard_map/keys_y1/ppermute | solution.py:54
  3.4 13.3 %collective-permute-start.4 = (bf16[144,512]{1,0:T(8,128)(2,1)}, bf16[144,512]{1,0:T(8,128)(2,1)S(1)}, u32[]{:S(2)}, u32[]{:S(2)}) collective-permute-start(bf16[144,512]{1,0:T(8,128)(2,1)} %get-tuple-element.69), channel_id=1, source_target_pairs={{0,2},{8,10},{1,3},{9,11},{2,0},{10,8},{3,1},{11,9},{16,18},{24,26... | collective-permute-start | bytes 442376 | tf_op jit(solution)/shard_map/keys_y2/ppermute | solution.py:54
  6.1 10.7 %collective-permute-start.5 = (bf16[144,512]{1,0:T(8,128)(2,1)}, bf16[144,512]{1,0:T(8,128)(2,1)S(1)}, u32[]{:S(2)}, u32[]{:S(2)}) collective-permute-start(bf16[144,512]{1,0:T(8,128)(2,1)} %get-tuple-element.70), channel_id=1, source_target_pairs={{0,3},{8,11},{1,0},{9,8},{2,1},{10,9},{3,2},{11,10},{16,19},{24,27... | collective-permute-start | bytes 442376 | tf_op jit(solution)/shard_map/keys_y3/ppermute | solution.py:54
  8.8 14.8 %collective-permute-start = (bf16[128,1024]{1,0:T(8,128)(2,1)}, bf16[128,1024]{1,0:T(8,128)(2,1)S(1)}, u32[]{:S(2)}, u32[]{:S(2)}) collective-permute-start(bf16[128,1024]{1,0:T(8,128)(2,1)} %get-tuple-element.63), channel_id=1, source_target_pairs={{0,1},{8,9},{1,2},{9,10},{2,3},{10,11},{3,0},{11,8},{16,17},{24,25... | collective-permute-start | bytes 786440 | tf_op jit(solution)/shard_map/queries0_y1/ppermute | solution.py:54
  12.1 17.1 %collective-permute-start.2 = (bf16[128,1024]{1,0:T(8,128)(2,1)}, bf16[128,1024]{1,0:T(8,128)(2,1)S(1)}, u32[]{:S(2)}, u32[]{:S(2)}) collective-permute-start(bf16[128,1024]{1,0:T(8,128)(2,1)} %get-tuple-element.65), channel_id=1, source_target_pairs={{0,3},{8,11},{1,0},{9,8},{2,1},{10,9},{3,2},{11,10},{16,19},{24,27... | collective-permute-start | bytes 786440 | tf_op jit(solution)/shard_map/queries0_y3/ppermute | solution.py:54
  12.1 4.7 %copy-start.2 = (bf16[144,512]{1,0:T(8,128)(2,1)S(1)}, bf16[144,512]{1,0:T(8,128)(2,1)}, u32[]{:S(2)}) copy-start(bf16[144,512]{1,0:T(8,128)(2,1)} %get-tuple-element.61.kv) | copy-start | bytes 442372
  12.1 17.1 %copy-start.5 = (bf16[128,1024]{1,0:T(8,128)(2,1)S(1)}, bf16[128,1024]{1,0:T(8,128)(2,1)}, u32[]{:S(2)}) copy-start(bf16[128,1024]{1,0:T(8,128)(2,1)} %get-tuple-element.76) | copy-start | bytes 786436
  12.1 17.1 %copy-start.4 = (bf16[128,1024]{1,0:T(8,128)(2,1)S(1)}, bf16[128,1024]{1,0:T(8,128)(2,1)}, u32[]{:S(2)}) copy-start(bf16[128,1024]{1,0:T(8,128)(2,1)} %get-tuple-element.78) | copy-start | bytes 786436
  12.2 17.5 %copy-start = (bf16[1,128,4096]{2,1,0:T(8,128)(2,1)S(1)}, bf16[1,128,4096]{2,1,0:T(8,128)(2,1)}, u32[]{:S(2)}) copy-start(bf16[1,128,4096]{2,1,0:T(8,128)(2,1)} %q.2) | copy-start | bytes 3145732
  12.2 17.5 %copy-start.1 = (bf16[1,128,4096]{2,1,0:T(8,128)(2,1)S(1)}, bf16[1,128,4096]{2,1,0:T(8,128)(2,1)}, u32[]{:S(2)}) copy-start(bf16[1,128,4096]{2,1,0:T(8,128)(2,1)} %g.5) | copy-start | bytes 3145732
  12.2 17.0 %collective-permute-start.1 = (bf16[128,1024]{1,0:T(8,128)(2,1)}, bf16[128,1024]{1,0:T(8,128)(2,1)S(1)}, u32[]{:S(2)}, u32[]{:S(2)}) collective-permute-start(bf16[128,1024]{1,0:T(8,128)(2,1)} %get-tuple-element.64), channel_id=1, source_target_pairs={{0,2},{8,10},{1,3},{9,11},{2,0},{10,8},{3,1},{11,9},{16,18},{24,26... | collective-permute-start | bytes 786440 | tf_op jit(solution)/shard_map/queries0_y2/ppermute | solution.py:54
  16.7 13.1 %collective-permute-start.13 = (bf16[128,2048]{1,0:T(8,128)(2,1)}, bf16[128,2048]{1,0:T(8,128)(2,1)S(1)}, u32[]{:S(2)}, u32[]{:S(2)}) collective-permute-start(bf16[128,2048]{1,0:T(8,128)(2,1)} %get-tuple-element.88), channel_id=1, source_target_pairs={{0,8},{8,0},{1,9},{9,1},{2,10},{10,2},{3,11},{11,3},{16,24},{24,16... | collective-permute-start | bytes 1572872 | tf_op jit(solution)/shard_map/swap_inputs/ppermute | solution.py:54
  16.9 17.3 %collective-permute-start.6 = (bf16[576,512]{1,0:T(8,128)(2,1)S(1)}, bf16[576,512]{1,0:T(8,128)(2,1)S(1)}, u32[]{:S(2)}, u32[]{:S(2)}) collective-permute-start(bf16[576,512]{1,0:T(8,128)(2,1)S(1)} %pad_maximum_fusion.1), channel_id=1, source_target_pairs={{0,4},{8,12},{1,5},{9,13},{2,6},{10,14},{3,7},{11,15},{16,20},{24,... | collective-permute-start | bytes 1769480 | tf_op jit(solution)/shard_map/half/ppermute | solution.py:54
  23.6 20.4 %collective-permute-start.8 = (bf16[128,1024]{1,0:T(8,128)(2,1)}, bf16[128,1024]{1,0:T(8,128)(2,1)S(1)}, u32[]{:S(2)}, u32[]{:S(2)}) collective-permute-start(bf16[128,1024]{1,0:T(8,128)(2,1)} %get-tuple-element.74), channel_id=1, source_target_pairs={{0,1},{8,9},{1,2},{9,10},{2,3},{10,11},{3,0},{11,8},{16,17},{24,25... | collective-permute-start | bytes 786440 | tf_op jit(solution)/shard_map/queries1_y1/ppermute | solution.py:54
  29.2 14.8 %collective-permute-start.9 = (bf16[128,1024]{1,0:T(8,128)(2,1)S(1)}, bf16[128,1024]{1,0:T(8,128)(2,1)S(1)}, u32[]{:S(2)}, u32[]{:S(2)}) collective-permute-start(bf16[128,1024]{1,0:T(8,128)(2,1)S(1)} %copy-done.5), channel_id=1, source_target_pairs={{0,2},{8,10},{1,3},{9,11},{2,0},{10,8},{3,1},{11,9},{16,18},{24,26... | collective-permute-start | bytes 786440 | tf_op jit(solution)/shard_map/queries1_y2/ppermute | solution.py:54
  29.2 1.0 copy-start.3
  29.2 14.8 %collective-permute-start.10 = (bf16[128,1024]{1,0:T(8,128)(2,1)S(1)}, bf16[128,1024]{1,0:T(8,128)(2,1)S(1)}, u32[]{:S(2)}, u32[]{:S(2)}) collective-permute-start(bf16[128,1024]{1,0:T(8,128)(2,1)S(1)} %copy-done.4), channel_id=1, source_target_pairs={{0,3},{8,11},{1,0},{9,8},{2,1},{10,9},{3,2},{11,10},{16,19},{24,27... | collective-permute-start | bytes 786440 | tf_op jit(solution)/shard_map/queries1_y3/ppermute | solution.py:54
  30.4 26.9 %collective-permute-start.14 = (bf16[256,2048]{1,0:T(8,128)(2,1)S(1)}, bf16[256,2048]{1,0:T(8,128)(2,1)S(1)}, u32[]{:S(2)}, u32[]{:S(2)}) collective-permute-start(bf16[256,2048]{1,0:T(8,128)(2,1)S(1)} %pad_maximum_fusion.own), channel_id=1, source_target_pairs={{0,1},{8,9},{1,2},{9,10},{2,3},{10,11},{3,0},{11,8},{16,17},{24,25... | collective-permute-start | bytes 3145736 | tf_op jit(solution)/shard_map/inputs_up/ppermute | solution.py:54
  34.2 28.0 %collective-permute-start.16 = (bf16[256,2048]{1,0:T(8,128)(2,1)S(1)}, bf16[256,2048]{1,0:T(8,128)(2,1)S(1)}, u32[]{:S(2)}, u32[]{:S(2)}) collective-permute-start(bf16[256,2048]{1,0:T(8,128)(2,1)S(1)} %pad_maximum_fusion.own), channel_id=1, source_target_pairs={{0,3},{8,11},{1,0},{9,8},{2,1},{10,9},{3,2},{11,10},{16,19},{24,27... | collective-permute-start | bytes 3145736 | tf_op jit(solution)/shard_map/inputs_down/ppermute | solution.py:54
  52.4 10.0 %collective-permute-start.11 = (bf16[512,512]{1,0:T(8,128)(2,1)S(1)}, bf16[512,512]{1,0:T(8,128)(2,1)S(1)}, u32[]{:S(2)}, u32[]{:S(2)}) collective-permute-start(bf16[512,512]{1,0:T(8,128)(2,1)S(1)} %get-tuple-element.81.a1), channel_id=1, source_target_pairs={{0,8},{8,0},{1,9},{9,1},{2,10},{10,2},{3,11},{11,3},{16,24},{24,16... | collective-permute-start | bytes 1572872 | tf_op jit(solution)/shard_map/swap_dq1/ppermute | solution.py:54
  52.5 15.9 %collective-permute-start.12 = (bf16[512,512]{1,0:T(8,128)(2,1)S(1)}, bf16[512,512]{1,0:T(8,128)(2,1)S(1)}, u32[]{:S(2)}, u32[]{:S(2)}) collective-permute-start(bf16[512,512]{1,0:T(8,128)(2,1)S(1)} %pad_maximum_fusion.2), channel_id=1, source_target_pairs={{0,4},{8,12},{1,5},{9,13},{2,6},{10,14},{3,7},{11,15},{16,20},{24,... | collective-permute-start | bytes 1572872 | tf_op jit(solution)/shard_map/back/ppermute | solution.py:54
  57.3 12.5 %collective-permute-start.15 = (bf16[128,2048]{1,0:T(8,128)(2,1)S(1)}, bf16[128,2048]{1,0:T(8,128)(2,1)S(1)}, u32[]{:S(2)}, u32[]{:S(2)}) collective-permute-start(bf16[128,2048]{1,0:T(8,128)(2,1)S(1)} %slice.8), channel_id=1, source_target_pairs={{0,1},{8,9},{1,2},{9,10},{2,3},{10,11},{3,0},{11,8},{16,17},{24,25... | collective-permute-start | bytes 1572872 | tf_op jit(solution)/shard_map/inputs_up2/ppermute | solution.py:54
  62.2 13.3 %collective-permute-start.17 = (bf16[128,2048]{1,0:T(8,128)(2,1)S(1)}, bf16[128,2048]{1,0:T(8,128)(2,1)S(1)}, u32[]{:S(2)}, u32[]{:S(2)}) collective-permute-start(bf16[128,2048]{1,0:T(8,128)(2,1)S(1)} %slice.9), channel_id=1, source_target_pairs={{0,3},{8,11},{1,0},{9,8},{2,1},{10,9},{3,2},{11,10},{16,19},{24,27... | collective-permute-start | bytes 1572872 | tf_op jit(solution)/shard_map/inputs_down2/ppermute | solution.py:54
  62.3 13.5 %collective-permute-start.7 = (bf16[512,512]{1,0:T(8,128)(2,1)S(1)}, bf16[512,512]{1,0:T(8,128)(2,1)S(1)}, u32[]{:S(2)}, u32[]{:S(2)}) collective-permute-start(bf16[512,512]{1,0:T(8,128)(2,1)S(1)} %get-tuple-element.71.a0), channel_id=1, source_target_pairs={{0,8},{8,0},{1,9},{9,1},{2,10},{10,2},{3,11},{11,3},{16,24},{24,16... | collective-permute-start | bytes 1572872 | tf_op jit(solution)/shard_map/swap_dq0/ppermute | solution.py:54
  75.7 5.9 %collective-permute-start.18 = (bf16[512,512]{1,0:T(8,128)(2,1)S(1)}, bf16[512,512]{1,0:T(8,128)(2,1)S(1)}, u32[]{:S(2)}, u32[]{:S(2)}) collective-permute-start(bf16[512,512]{1,0:T(8,128)(2,1)S(1)} %fusion.k), channel_id=1, source_target_pairs={{0,8},{8,0},{1,9},{9,1},{2,10},{10,2},{3,11},{11,3},{16,24},{24,16... | collective-permute-start | bytes 1572872 | tf_op jit(solution)/shard_map/swap_dkv/ppermute | solution.py:54
  77.4 13.9 %collective-permute-start.19 = (bf16[768,256]{1,0:T(8,128)(2,1)S(1)}, bf16[768,256]{1,0:T(8,128)(2,1)S(1)}, u32[]{:S(2)}, u32[]{:S(2)}) collective-permute-start(bf16[768,256]{1,0:T(8,128)(2,1)S(1)} %get-tuple-element.93), channel_id=1, source_target_pairs={{0,32},{8,40},{1,33},{9,41},{2,34},{10,42},{3,35},{11,43},{16,48},... | collective-permute-start | bytes 1179656 | tf_op jit(solution)/shard_map/reduce_a_far_up/ppermute | solution.py:54
  79.3 11.9 %collective-permute-start.20 = (bf16[768,256]{1,0:T(8,128)(2,1)S(1)}, bf16[768,256]{1,0:T(8,128)(2,1)S(1)}, u32[]{:S(2)}, u32[]{:S(2)}) collective-permute-start(bf16[768,256]{1,0:T(8,128)(2,1)S(1)} %get-tuple-element.101), channel_id=1, source_target_pairs={{0,96},{8,104},{1,97},{9,105},{2,98},{10,106},{3,99},{11,107},{16,... | collective-permute-start | bytes 1179656 | tf_op jit(solution)/shard_map/reduce_a_far_down/ppermute | solution.py:54
  82.8 14.6 %collective-permute-start.26 = (bf16[384,512]{1,0:T(8,128)(2,1)S(1)}, bf16[384,512]{1,0:T(8,128)(2,1)S(1)}, u32[]{:S(2)}, u32[]{:S(2)}) collective-permute-start(bf16[384,512]{1,0:T(8,128)(2,1)S(1)} %get-tuple-element.96), channel_id=1, source_target_pairs={{0,16},{8,24},{1,17},{9,25},{2,18},{10,26},{3,19},{11,27},{16,4},{... | collective-permute-start | bytes 1179656 | tf_op jit(solution)/shard_map/reduce_b_far_up/ppermute | solution.py:54
  84.6 12.8 %collective-permute-start.27 = (bf16[384,512]{1,0:T(8,128)(2,1)S(1)}, bf16[384,512]{1,0:T(8,128)(2,1)S(1)}, u32[]{:S(2)}, u32[]{:S(2)}) collective-permute-start(bf16[384,512]{1,0:T(8,128)(2,1)S(1)} %get-tuple-element.112), channel_id=1, source_target_pairs={{0,20},{8,28},{1,21},{9,29},{2,22},{10,30},{3,23},{11,31},{16,0},{... | collective-permute-start | bytes 1179656 | tf_op jit(solution)/shard_map/reduce_b_far_down/ppermute | solution.py:54
  91.5 20.6 %collective-permute-start.21 = (bf16[768,512]{1,0:T(8,128)(2,1)S(1)}, bf16[768,512]{1,0:T(8,128)(2,1)S(1)}, u32[]{:S(2)}, u32[]{:S(2)}) collective-permute-start(bf16[768,512]{1,0:T(8,128)(2,1)S(1)} %get-tuple-element.102), channel_id=1, source_target_pairs={{0,32},{8,40},{1,33},{9,41},{2,34},{10,42},{3,35},{11,43},{16,48},... | collective-permute-start | bytes 2359304 | tf_op jit(solution)/shard_map/reduce_a_up/ppermute | solution.py:54
  92.8 19.3 %collective-permute-start.22 = (bf16[768,512]{1,0:T(8,128)(2,1)S(1)}, bf16[768,512]{1,0:T(8,128)(2,1)S(1)}, u32[]{:S(2)}, u32[]{:S(2)}) collective-permute-start(bf16[768,512]{1,0:T(8,128)(2,1)S(1)} %get-tuple-element.103), channel_id=1, source_target_pairs={{0,96},{8,104},{1,97},{9,105},{2,98},{10,106},{3,99},{11,107},{16,... | collective-permute-start | bytes 2359304 | tf_op jit(solution)/shard_map/reduce_a_down/ppermute | solution.py:54
  97.6 21.8 %collective-permute-start.28 = (bf16[384,1024]{1,0:T(8,128)(2,1)S(1)}, bf16[384,1024]{1,0:T(8,128)(2,1)S(1)}, u32[]{:S(2)}, u32[]{:S(2)}) collective-permute-start(bf16[384,1024]{1,0:T(8,128)(2,1)S(1)} %get-tuple-element.113), channel_id=1, source_target_pairs={{0,16},{8,24},{1,17},{9,25},{2,18},{10,26},{3,19},{11,27},{16,4},{... | collective-permute-start | bytes 2359304 | tf_op jit(solution)/shard_map/reduce_b_up/ppermute | solution.py:54
  99.1 20.5 %collective-permute-start.29 = (bf16[384,1024]{1,0:T(8,128)(2,1)S(1)}, bf16[384,1024]{1,0:T(8,128)(2,1)S(1)}, u32[]{:S(2)}, u32[]{:S(2)}) collective-permute-start(bf16[384,1024]{1,0:T(8,128)(2,1)S(1)} %get-tuple-element.114), channel_id=1, source_target_pairs={{0,20},{8,28},{1,21},{9,29},{2,22},{10,30},{3,23},{11,31},{16,0},{... | collective-permute-start | bytes 2359304 | tf_op jit(solution)/shard_map/reduce_b_down/ppermute | solution.py:54
  112.6 10.8 %collective-permute-start.23 = (bf16[384,256]{1,0:T(8,128)(2,1)S(1)}, bf16[384,256]{1,0:T(8,128)(2,1)S(1)}, u32[]{:S(2)}, u32[]{:S(2)}) collective-permute-start(bf16[384,256]{1,0:T(8,128)(2,1)S(1)} %get-tuple-element.105), channel_id=1, source_target_pairs={{0,16},{8,24},{1,17},{9,25},{2,18},{10,26},{3,19},{11,27},{16,4},{... | collective-permute-start | bytes 589832 | tf_op jit(solution)/shard_map/second_a_x1/ppermute | solution.py:54
  114.1 11.3 %collective-permute-start.24 = (bf16[384,256]{1,0:T(8,128)(2,1)S(1)}, bf16[384,256]{1,0:T(8,128)(2,1)S(1)}, u32[]{:S(2)}, u32[]{:S(2)}) collective-permute-start(bf16[384,256]{1,0:T(8,128)(2,1)S(1)} %get-tuple-element.106), channel_id=1, source_target_pairs={{0,20},{8,28},{1,21},{9,29},{2,22},{10,30},{3,23},{11,31},{16,0},{... | collective-permute-start | bytes 589832 | tf_op jit(solution)/shard_map/second_a_x3/ppermute | solution.py:54
  115.9 11.2 %collective-permute-start.25 = (bf16[384,256]{1,0:T(8,128)(2,1)S(1)}, bf16[384,256]{1,0:T(8,128)(2,1)S(1)}, u32[]{:S(2)}, u32[]{:S(2)}) collective-permute-start(bf16[384,256]{1,0:T(8,128)(2,1)S(1)} %get-tuple-element.107), channel_id=1, source_target_pairs={{0,4},{8,12},{1,5},{9,13},{2,6},{10,14},{3,7},{11,15},{16,20},{24,... | collective-permute-start | bytes 589832 | tf_op jit(solution)/shard_map/second_a_x2/ppermute | solution.py:54
  120.1 10.9 %collective-permute-start.30 = (bf16[384,256]{1,0:T(8,128)(2,1)S(1)}, bf16[384,256]{1,0:T(8,128)(2,1)S(1)}, u32[]{:S(2)}, u32[]{:S(2)}) collective-permute-start(bf16[384,256]{1,0:T(8,128)(2,1)S(1)} %get-tuple-element.116), channel_id=1, source_target_pairs={{0,32},{8,40},{1,33},{9,41},{2,34},{10,42},{3,35},{11,43},{16,48},... | collective-permute-start | bytes 589832 | tf_op jit(solution)/shard_map/second_b_z1/ppermute | solution.py:54
  120.2 10.8 %collective-permute-start.31 = (bf16[384,256]{1,0:T(8,128)(2,1)S(1)}, bf16[384,256]{1,0:T(8,128)(2,1)S(1)}, u32[]{:S(2)}, u32[]{:S(2)}) collective-permute-start(bf16[384,256]{1,0:T(8,128)(2,1)S(1)} %get-tuple-element.117), channel_id=1, source_target_pairs={{0,96},{8,104},{1,97},{9,105},{2,98},{10,106},{3,99},{11,107},{16,... | collective-permute-start | bytes 589832 | tf_op jit(solution)/shard_map/second_b_z3/ppermute | solution.py:54
  123.4 7.6 %collective-permute-start.32 = (bf16[384,256]{1,0:T(8,128)(2,1)S(1)}, bf16[384,256]{1,0:T(8,128)(2,1)S(1)}, u32[]{:S(2)}, u32[]{:S(2)}) collective-permute-start(bf16[384,256]{1,0:T(8,128)(2,1)S(1)} %get-tuple-element.118), channel_id=1, source_target_pairs={{0,64},{8,72},{1,65},{9,73},{2,66},{10,74},{3,67},{11,75},{16,80},... | collective-permute-start | bytes 589832 | tf_op jit(solution)/shard_map/second_b_z2/ppermute | solution.py:54

commit v6 on v5

--- a/solution.py
+++ b/solution.py
@@ -533,9 +533,9 @@
     a3 = send("queries0_y3", q03, dy=3)
     a2 = send("queries0_y2", q02, dy=2)
     before = send("half", jnp.concatenate([own] + keys, axis=0), dx=2)
-    b1 = send("queries1_y1", after(q11, a1), dy=1)
-    b3 = send("queries1_y3", after(q13, a1), dy=3)
-    b2 = send("queries1_y2", after(q12, a1, a3), dy=2)
+    b1 = send("queries1_y1", q11, dy=1)
+    b3 = send("queries1_y3", q13, dy=3)
+    b2 = send("queries1_y2", q12, dy=2)
     sent = after(jnp.concatenate([keep, got], axis=0), a1, a2, a3)
     up = send("inputs_up", sent, dy=1)
     down = send("inputs_down", sent, dy=-1)

time: 132 us -> 140 us (1.061)
  waiting for transfers between devices: 45.8 us -> 59.1 us
  starting transfers between devices: 49.9 us -> 45.1 us
    ppermute x33, waiting for transfers between devices: 45.8 us -> 59.1 us  [send(): return lax.ppermute(a, ('grp', 'sp'), pairs(**k))]
    ppermute x33, starting transfers between devices: 49.9 us -> 45.1 us  [send(): return lax.ppermute(a, ('grp', 'sp'), pairs(**k))]
  transfers between devices with their start and end apart: 33 -> 33, of which waited for: 15 -> 14; matrix products, arithmetic and copies ran while one was open for 0% -> 0% of each run, Pallas kernels for 23% -> 22%
where the time goes in v6:
time: 140 us
  waiting for transfers between devices  59.1 us (42%)
  starting transfers between devices  45.1 us (32%)
  Pallas kernels  34.6 us (25%)
    ppermute x33, waiting for transfers between devices, send(): return lax.ppermute(a, ('grp', 'sp'), pairs(**k))  59.1 us
    ppermute x33, starting transfers between devices, send(): return lax.ppermute(a, ('grp', 'sp'), pairs(**k))  45.1 us
    pallas_call x2, Pallas kernels, attention(): call(attention_body, [jax.ShapeDtypeStruct((512, 512), BF16), jax.ShapeDt...  15.7 us
  transfers between devices with their start and end apart: 33, of which 14 were waited for; matrix products, arithmetic and copies ran while one was open for 0% of the time, Pallas kernels for 22%

profile of v6, /device:TPU:24, one launch (start us, length us, event | category | flops | bytes accessed | tf_op | source)
XLA Modules:
  0.0 140.2 jit_solution(15523556888061507822)
XLA Ops:
  0.6 2.6 %pack_keys_body.1 = (bf16[144,512]{1,0:T(8,128)(2,1)}, bf16[144,512]{1,0:T(8,128)(2,1)}, bf16[144,512]{1,0:T(8,128)(2,1)}, bf16[144,512]{1,0:T(8,128)(2,1)}) custom-call(bf16[1,128,1024]{2,1,0:T(8,128)(2,1)} %k.1, bf16[1,128,1024]{2,1,0:T(8,128)(2,1)} %v.1, s32[1,128]{1,0:T(1,128)} %i.1), custom_call_target="tpu_custom_call" | custom-call | flops 100000000 | bytes 1000000 | tf_op jit(solution)/shard_map/pack_keys_body/pallas_call | solution.py:105
  3.2 0.2 collective-permute-start.3
  3.5 2.7 %collective-permute-start.4 = (bf16[144,512]{1,0:T(8,128)(2,1)}, bf16[144,512]{1,0:T(8,128)(2,1)S(1)}, u32[]{:S(2)}, u32[]{:S(2)}) collective-permute-start(bf16[144,512]{1,0:T(8,128)(2,1)} %get-tuple-element.66), channel_id=1, source_target_pairs={{0,2},{8,10},{1,3},{9,11},{2,0},{10,8},{3,1},{11,9},{16,18},{24,26... | collective-permute-start | bytes 442376 | tf_op jit(solution)/shard_map/keys_y2/ppermute | solution.py:54
  6.1 2.7 %pack_queries_body.1 = (bf16[128,1024]{1,0:T(8,128)(2,1)}, bf16[128,1024]{1,0:T(8,128)(2,1)}, bf16[128,1024]{1,0:T(8,128)(2,1)}, bf16[128,1024]{1,0:T(8,128)(2,1...) custom-call(bf16[1,128,4096]{2,1,0:T(8,128)(2,1)} %q.2, bf16[1,128,4096]{2,1,0:T(8,128)(2,1)} %g.5), custom_call_target="tpu_custom_call" | custom-call | flops 100000000 | bytes 1000000 | tf_op jit(solution)/shard_map/pack_queries_body/pallas_call | solution.py:129
  8.8 3.3 %collective-permute-start = (bf16[128,1024]{1,0:T(8,128)(2,1)}, bf16[128,1024]{1,0:T(8,128)(2,1)S(1)}, u32[]{:S(2)}, u32[]{:S(2)}) collective-permute-start(bf16[128,1024]{1,0:T(8,128)(2,1)} %get-tuple-element.60), channel_id=1, source_target_pairs={{0,1},{8,9},{1,2},{9,10},{2,3},{10,11},{3,0},{11,8},{16,17},{24,25... | collective-permute-start | bytes 786440 | tf_op jit(solution)/shard_map/queries0_y1/ppermute | solution.py:54
  12.1 0.2 collective-permute-start.1
  12.3 0.0 copy-start
  12.4 1.4 collective-permute-start.2
  13.8 2.3 %pack_inputs_body.1 = (bf16[128,2048]{1,0:T(8,128)(2,1)}, bf16[128,2048]{1,0:T(8,128)(2,1)}) custom-call(bf16[1,128,4096]{2,1,0:T(8,128)(2,1)} %x), custom_call_target="tpu_custom_call" | custom-call | flops 1000000000 | bytes 1000000 | tf_op jit(solution)/shard_map/pack_inputs_body/pallas_call | solution.py:153
  16.1 2.0 %collective-permute-start.8 = (bf16[128,1024]{1,0:T(8,128)(2,1)}, bf16[128,1024]{1,0:T(8,128)(2,1)S(1)}, u32[]{:S(2)}, u32[]{:S(2)}) collective-permute-start(bf16[128,1024]{1,0:T(8,128)(2,1)} %get-tuple-element.70), channel_id=1, source_target_pairs={{0,1},{8,9},{1,2},{9,10},{2,3},{10,11},{3,0},{11,8},{16,17},{24,25... | collective-permute-start | bytes 786440 | tf_op jit(solution)/shard_map/queries1_y1/ppermute | solution.py:54
  18.1 2.1 %collective-permute-start.9 = (bf16[128,1024]{1,0:T(8,128)(2,1)S(1)}, bf16[128,1024]{1,0:T(8,128)(2,1)S(1)}, u32[]{:S(2)}, u32[]{:S(2)}) collective-permute-start(bf16[128,1024]{1,0:T(8,128)(2,1)S(1)} %copy-done.5), channel_id=1, source_target_pairs={{0,2},{8,10},{1,3},{9,11},{2,0},{10,8},{3,1},{11,9},{16,18},{24,26... | collective-permute-start | bytes 786440 | tf_op jit(solution)/shard_map/queries1_y2/ppermute | solution.py:54
  20.3 4.0 %collective-permute-done.q1 = bf16[128,1024]{1,0:T(8,128)(2,1)S(1)} collective-permute-done((bf16[128,1024]{1,0:T(8,128)(2,1)}, bf16[128,1024]{1,0:T(8,128)(2,1)S(1)}, u32[]{:S(2)}, u32[]{:S(2)}) %collective-permute-start) | collective-permute-done | bytes 262176 | tf_op jit(solution)/shard_map/queries0_y1/ppermute | solution.py:54
  24.3 0.1 collective-permute-start.13
  24.4 4.4 %collective-permute-done.2.q3 = bf16[128,1024]{1,0:T(8,128)(2,1)S(1)} collective-permute-done((bf16[128,1024]{1,0:T(8,128)(2,1)}, bf16[128,1024]{1,0:T(8,128)(2,1)S(1)}, u32[]{:S(2)}, u32[]{:S(2)}) %collective-permute-start.2) | collective-permute-done | bytes 262176 | tf_op jit(solution)/shard_map/queries0_y3/ppermute | solution.py:54
  28.8 3.0 %collective-permute-start.6 = (bf16[576,512]{1,0:T(8,128)(2,1)S(1)}, bf16[576,512]{1,0:T(8,128)(2,1)S(1)}, u32[]{:S(2)}, u32[]{:S(2)}) collective-permute-start(bf16[576,512]{1,0:T(8,128)(2,1)S(1)} %pad_maximum_fusion.1), channel_id=1, source_target_pairs={{0,4},{8,12},{1,5},{9,13},{2,6},{10,14},{3,7},{11,15},{16,20},{24,... | collective-permute-start | bytes 1769480 | tf_op jit(solution)/shard_map/half/ppermute | solution.py:54
  31.8 0.2 arrange_body.2
  32.1 0.1 pad_maximum_fusion.own
  32.2 0.6 collective-permute-start.14
  32.7 12.5 %collective-permute-done.6.pv = bf16[576,512]{1,0:T(8,128)(2,1)S(1)} collective-permute-done((bf16[576,512]{1,0:T(8,128)(2,1)S(1)}, bf16[576,512]{1,0:T(8,128)(2,1)S(1)}, u32[]{:S(2)}, u32[]{:S(2)}) %collective-permute-start.6) | collective-permute-done | bytes 589856 | tf_op jit(solution)/shard_map/half/ppermute | solution.py:54
  45.3 7.9 %attention_body.2 = (bf16[512,512]{1,0:T(8,128)(2,1)S(1)}, f32[256,512]{1,0:T(8,128)S(1)}, bf16[256,512]{1,0:T(8,128)(2,1)S(1)}) custom-call(bf16[512,512]{1,0:T(8,128)(2,1)S(1)} %get-tuple-element.63.qs, bf16[512,512]{1,0:T(8,128)(2,1)S(1)} %get-tuple-element.64.gs, bf16[144,512]{1,0:T(8,128)(2,1)S(1)} %copy-done.2, ...), custom_call_target="tpu_custom_call" | custom-call | flops 12000000000 | bytes 1000000 | tf_op jit(solution)/shard_map/attention_body/pallas_call | solution.py:257
  53.2 0.5 arrange_body.3
  53.7 7.9 %attention_body.3 = (bf16[512,512]{1,0:T(8,128)(2,1)S(1)}, f32[256,512]{1,0:T(8,128)S(1)}, bf16[256,512]{1,0:T(8,128)(2,1)S(1)}) custom-call(bf16[512,512]{1,0:T(8,128)(2,1)S(1)} %get-tuple-element.73.qs, bf16[512,512]{1,0:T(8,128)(2,1)S(1)} %get-tuple-element.74.gs, bf16[144,512]{1,0:T(8,128)(2,1)S(1)} %copy-done.2, ...), custom_call_target="tpu_custom_call" | custom-call | flops 12000000000 | bytes 1000000 | tf_op jit(solution)/shard_map/attention_body/pallas_call | solution.py:257
  61.5 0.1 collective-permute-start.11
  61.7 3.1 %collective-permute-start.12 = (bf16[512,512]{1,0:T(8,128)(2,1)S(1)}, bf16[512,512]{1,0:T(8,128)(2,1)S(1)}, u32[]{:S(2)}, u32[]{:S(2)}) collective-permute-start(bf16[512,512]{1,0:T(8,128)(2,1)S(1)} %pad_maximum_fusion.2), channel_id=1, source_target_pairs={{0,4},{8,12},{1,5},{9,13},{2,6},{10,14},{3,7},{11,15},{16,20},{24,... | collective-permute-start | bytes 1572872 | tf_op jit(solution)/shard_map/back/ppermute | solution.py:54
  64.8 3.3 %collective-permute-start.15 = (bf16[128,2048]{1,0:T(8,128)(2,1)S(1)}, bf16[128,2048]{1,0:T(8,128)(2,1)S(1)}, u32[]{:S(2)}, u32[]{:S(2)}) collective-permute-start(bf16[128,2048]{1,0:T(8,128)(2,1)S(1)} %slice.8), channel_id=1, source_target_pairs={{0,1},{8,9},{1,2},{9,10},{2,3},{10,11},{3,0},{11,8},{16,17},{24,25... | collective-permute-start | bytes 1572872 | tf_op jit(solution)/shard_map/inputs_up2/ppermute | solution.py:54
  68.1 2.3 %collective-permute-done.16.r3 = bf16[256,2048]{1,0:T(8,128)(2,1)S(1)} collective-permute-done((bf16[256,2048]{1,0:T(8,128)(2,1)S(1)}, bf16[256,2048]{1,0:T(8,128)(2,1)S(1)}, u32[]{:S(2)}, u32[]{:S(2)}) %collective-permute-start.16) | collective-permute-done | bytes 1048608 | tf_op jit(solution)/shard_map/inputs_down/ppermute | solution.py:54
  70.5 0.1 collective-permute-start.17
  70.6 0.1 collective-permute-start.7
  70.7 6.9 %collective-permute-done.12 = bf16[512,512]{1,0:T(8,128)(2,1)S(1)} collective-permute-done((bf16[512,512]{1,0:T(8,128)(2,1)S(1)}, bf16[512,512]{1,0:T(8,128)(2,1)S(1)}, u32[]{:S(2)}, u32[]{:S(2)}) %collective-permute-start.12) | collective-permute-done | bytes 524320 | tf_op jit(solution)/shard_map/back/ppermute | solution.py:54
  77.6 2.1 %collective-permute-done.15.r2a = bf16[128,2048]{1,0:T(8,128)(2,1)S(1)} collective-permute-done((bf16[128,2048]{1,0:T(8,128)(2,1)S(1)}, bf16[128,2048]{1,0:T(8,128)(2,1)S(1)}, u32[]{:S(2)}, u32[]{:S(2)}) %collective-permute-start.15) | collective-permute-done | bytes 524320 | tf_op jit(solution)/shard_map/inputs_up2/ppermute | solution.py:54
  79.7 3.9 %collective-permute-done.17.r2b = bf16[128,2048]{1,0:T(8,128)(2,1)S(1)} collective-permute-done((bf16[128,2048]{1,0:T(8,128)(2,1)S(1)}, bf16[128,2048]{1,0:T(8,128)(2,1)S(1)}, u32[]{:S(2)}, u32[]{:S(2)}) %collective-permute-start.17) | collective-permute-done | bytes 524320 | tf_op jit(solution)/shard_map/inputs_down2/ppermute | solution.py:54
  83.6 0.2 fusion.k
  83.7 0.1 collective-permute-start.18
  83.8 0.2 gather_a_body.1.g
  84.0 1.4 %far_a_body.1 = (bf16[1024,2048]{1,0:T(8,128)(2,1)S(1)}, bf16[768,256]{1,0:T(8,128)(2,1)S(1)}, bf16[768,256]{1,0:T(8,128)(2,1)S(1)}) custom-call(bf16[768,1024]{1,0:T(8,128)(2,1)S(1)} %gather_a_body.1.g, bf16[256,2048]{1,0:T(8,128)(2,1)S(1)} %pad_maximum_fusion.own, bf16[256,2048]{1,0:T(8,128)(2,1)S(1)} %collective-permute-done.14.r1, ...), custom_call_target="tpu_custom_call" | custom-call | flops 1000000000 | bytes 1000000 | tf_op jit(solution)/shard_map/far_a_body/pallas_call | solution.py:350
  85.4 2.0 %collective-permute-start.19 = (bf16[768,256]{1,0:T(8,128)(2,1)S(1)}, bf16[768,256]{1,0:T(8,128)(2,1)S(1)}, u32[]{:S(2)}, u32[]{:S(2)}) collective-permute-start(bf16[768,256]{1,0:T(8,128)(2,1)S(1)} %get-tuple-element.87), channel_id=1, source_target_pairs={{0,32},{8,40},{1,33},{9,41},{2,34},{10,42},{3,35},{11,43},{16,48},... | collective-permute-start | bytes 1179656 | tf_op jit(solution)/shard_map/reduce_a_far_up/ppermute | solution.py:54
  87.4 2.2 %collective-permute-start.20 = (bf16[768,256]{1,0:T(8,128)(2,1)S(1)}, bf16[768,256]{1,0:T(8,128)(2,1)S(1)}, u32[]{:S(2)}, u32[]{:S(2)}) collective-permute-start(bf16[768,256]{1,0:T(8,128)(2,1)S(1)} %get-tuple-element.95), channel_id=1, source_target_pairs={{0,96},{8,104},{1,97},{9,105},{2,98},{10,106},{3,99},{11,107},{16,... | collective-permute-start | bytes 1179656 | tf_op jit(solution)/shard_map/reduce_a_far_down/ppermute | solution.py:54
  89.6 0.2 gather_b_body.1.g
  89.9 1.0 far_b_body.1
  90.9 1.8 %collective-permute-start.26 = (bf16[384,512]{1,0:T(8,128)(2,1)S(1)}, bf16[384,512]{1,0:T(8,128)(2,1)S(1)}, u32[]{:S(2)}, u32[]{:S(2)}) collective-permute-start(bf16[384,512]{1,0:T(8,128)(2,1)S(1)} %get-tuple-element.90), channel_id=1, source_target_pairs={{0,16},{8,24},{1,17},{9,25},{2,18},{10,26},{3,19},{11,27},{16,4},{... | collective-permute-start | bytes 1179656 | tf_op jit(solution)/shard_map/reduce_b_far_up/ppermute | solution.py:54
  92.7 1.7 %collective-permute-start.27 = (bf16[384,512]{1,0:T(8,128)(2,1)S(1)}, bf16[384,512]{1,0:T(8,128)(2,1)S(1)}, u32[]{:S(2)}, u32[]{:S(2)}) collective-permute-start(bf16[384,512]{1,0:T(8,128)(2,1)S(1)} %get-tuple-element.106), channel_id=1, source_target_pairs={{0,20},{8,28},{1,21},{9,29},{2,22},{10,30},{3,23},{11,31},{16,0},{... | collective-permute-start | bytes 1179656 | tf_op jit(solution)/shard_map/reduce_b_far_down/ppermute | solution.py:54
  94.4 2.6 %near_a_body.1 = (f32[768,512]{1,0:T(8,128)S(1)}, f32[768,512]{1,0:T(8,128)S(1)}, f32[768,512]{1,0:T(8,128)S(1)}) custom-call(bf16[768,1024]{1,0:T(8,128)(2,1)S(1)} %gather_a_body.1.g, bf16[1024,2048]{1,0:T(8,128)(2,1)S(1)} %get-tuple-element.89.x), custom_call_target="tpu_custom_call" | custom-call | flops 1000000000 | bytes 1000000 | tf_op jit(solution)/shard_map/near_a_body/pallas_call | solution.py:389
  97.1 2.2 %collective-permute-done.19.gu = bf16[768,256]{1,0:T(8,128)(2,1)S(1)} collective-permute-done((bf16[768,256]{1,0:T(8,128)(2,1)S(1)}, bf16[768,256]{1,0:T(8,128)(2,1)S(1)}, u32[]{:S(2)}, u32[]{:S(2)}) %collective-permute-start.19) | collective-permute-done | bytes 393248 | tf_op jit(solution)/shard_map/reduce_a_far_up/ppermute | solution.py:54
  99.3 0.2 add_near_body.2
  99.5 1.3 collective-permute-start.21
  100.8 2.0 %collective-permute-start.22 = (bf16[768,512]{1,0:T(8,128)(2,1)S(1)}, bf16[768,512]{1,0:T(8,128)(2,1)S(1)}, u32[]{:S(2)}, u32[]{:S(2)}) collective-permute-start(bf16[768,512]{1,0:T(8,128)(2,1)S(1)} %get-tuple-element.97), channel_id=1, source_target_pairs={{0,96},{8,104},{1,97},{9,105},{2,98},{10,106},{3,99},{11,107},{16,... | collective-permute-start | bytes 2359304 | tf_op jit(solution)/shard_map/reduce_a_down/ppermute | solution.py:54
  102.8 2.6 %near_b_body.1 = (f32[384,1024]{1,0:T(8,128)S(1)}, f32[384,1024]{1,0:T(8,128)S(1)}, f32[384,1024]{1,0:T(8,128)S(1)}) custom-call(bf16[768,1024]{1,0:T(8,128)(2,1)S(1)} %gather_b_body.1.g, bf16[1024,2048]{1,0:T(8,128)(2,1)S(1)} %get-tuple-element.89.x), custom_call_target="tpu_custom_call" | custom-call | flops 1000000000 | bytes 1000000 | tf_op jit(solution)/shard_map/near_b_body/pallas_call | solution.py:405
  105.5 0.2 add_near_body.3
  105.7 1.6 %collective-permute-start.28 = (bf16[384,1024]{1,0:T(8,128)(2,1)S(1)}, bf16[384,1024]{1,0:T(8,128)(2,1)S(1)}, u32[]{:S(2)}, u32[]{:S(2)}) collective-permute-start(bf16[384,1024]{1,0:T(8,128)(2,1)S(1)} %get-tuple-element.107), channel_id=1, source_target_pairs={{0,16},{8,24},{1,17},{9,25},{2,18},{10,26},{3,19},{11,27},{16,4},{... | collective-permute-start | bytes 2359304 | tf_op jit(solution)/shard_map/reduce_b_up/ppermute | solution.py:54
  107.2 1.7 %collective-permute-start.29 = (bf16[384,1024]{1,0:T(8,128)(2,1)S(1)}, bf16[384,1024]{1,0:T(8,128)(2,1)S(1)}, u32[]{:S(2)}, u32[]{:S(2)}) collective-permute-start(bf16[384,1024]{1,0:T(8,128)(2,1)S(1)} %get-tuple-element.108), channel_id=1, source_target_pairs={{0,20},{8,28},{1,21},{9,29},{2,22},{10,30},{3,23},{11,31},{16,0},{... | collective-permute-start | bytes 2359304 | tf_op jit(solution)/shard_map/reduce_b_down/ppermute | solution.py:54
  109.0 11.2 %collective-permute-done.21.refs_1_ = bf16[768,512]{1,0:T(8,128)(2,1)S(1)} collective-permute-done((bf16[768,512]{1,0:T(8,128)(2,1)S(1)}, bf16[768,512]{1,0:T(8,128)(2,1)S(1)}, u32[]{:S(2)}, u32[]{:S(2)}) %collective-permute-start.21) | collective-permute-done | bytes 786464 | tf_op jit(solution)/shard_map/reduce_a_up/ppermute | solution.py:54
  120.2 0.5 add_a_body.1
  120.6 1.6 %collective-permute-start.23 = (bf16[384,256]{1,0:T(8,128)(2,1)S(1)}, bf16[384,256]{1,0:T(8,128)(2,1)S(1)}, u32[]{:S(2)}, u32[]{:S(2)}) collective-permute-start(bf16[384,256]{1,0:T(8,128)(2,1)S(1)} %get-tuple-element.99), channel_id=1, source_target_pairs={{0,16},{8,24},{1,17},{9,25},{2,18},{10,26},{3,19},{11,27},{16,4},{... | collective-permute-start | bytes 589832 | tf_op jit(solution)/shard_map/second_a_x1/ppermute | solution.py:54
  122.2 1.7 %collective-permute-start.24 = (bf16[384,256]{1,0:T(8,128)(2,1)S(1)}, bf16[384,256]{1,0:T(8,128)(2,1)S(1)}, u32[]{:S(2)}, u32[]{:S(2)}) collective-permute-start(bf16[384,256]{1,0:T(8,128)(2,1)S(1)} %get-tuple-element.100), channel_id=1, source_target_pairs={{0,20},{8,28},{1,21},{9,29},{2,22},{10,30},{3,23},{11,31},{16,0},{... | collective-permute-start | bytes 589832 | tf_op jit(solution)/shard_map/second_a_x3/ppermute | solution.py:54
  123.9 1.8 %collective-permute-start.25 = (bf16[384,256]{1,0:T(8,128)(2,1)S(1)}, bf16[384,256]{1,0:T(8,128)(2,1)S(1)}, u32[]{:S(2)}, u32[]{:S(2)}) collective-permute-start(bf16[384,256]{1,0:T(8,128)(2,1)S(1)} %get-tuple-element.101), channel_id=1, source_target_pairs={{0,4},{8,12},{1,5},{9,13},{2,6},{10,14},{3,7},{11,15},{16,20},{24,... | collective-permute-start | bytes 589832 | tf_op jit(solution)/shard_map/second_a_x2/ppermute | solution.py:54
  125.7 1.7 %collective-permute-done.28.refs_1_ = bf16[384,1024]{1,0:T(8,128)(2,1)S(1)} collective-permute-done((bf16[384,1024]{1,0:T(8,128)(2,1)S(1)}, bf16[384,1024]{1,0:T(8,128)(2,1)S(1)}, u32[]{:S(2)}, u32[]{:S(2)}) %collective-permute-start.28) | collective-permute-done | bytes 786464 | tf_op jit(solution)/shard_map/reduce_b_up/ppermute | solution.py:54
  127.4 0.3 collective-permute-done.29.refs_2_
  127.7 0.5 add_b_body.1
  128.2 0.1 collective-permute-start.30
  128.3 3.2 %collective-permute-start.31 = (bf16[384,256]{1,0:T(8,128)(2,1)S(1)}, bf16[384,256]{1,0:T(8,128)(2,1)S(1)}, u32[]{:S(2)}, u32[]{:S(2)}) collective-permute-start(bf16[384,256]{1,0:T(8,128)(2,1)S(1)} %get-tuple-element.111), channel_id=1, source_target_pairs={{0,96},{8,104},{1,97},{9,105},{2,98},{10,106},{3,99},{11,107},{16,... | collective-permute-start | bytes 589832 | tf_op jit(solution)/shard_map/second_b_z3/ppermute | solution.py:54
  131.5 0.4 collective-permute-done.24.refs_2_
  131.9 3.2 %collective-permute-done.25.refs_3_ = bf16[384,256]{1,0:T(8,128)(2,1)S(1)} collective-permute-done((bf16[384,256]{1,0:T(8,128)(2,1)S(1)}, bf16[384,256]{1,0:T(8,128)(2,1)S(1)}, u32[]{:S(2)}, u32[]{:S(2)}) %collective-permute-start.25) | collective-permute-done | bytes 196640 | tf_op jit(solution)/shard_map/second_a_x2/ppermute | solution.py:54
  135.2 3.9 %collective-permute-done.30.refs_5_ = bf16[384,256]{1,0:T(8,128)(2,1)S(1)} collective-permute-done((bf16[384,256]{1,0:T(8,128)(2,1)S(1)}, bf16[384,256]{1,0:T(8,128)(2,1)S(1)}, u32[]{:S(2)}, u32[]{:S(2)}) %collective-permute-start.30) | collective-permute-done | bytes 196640 | tf_op jit(solution)/shard_map/second_b_z1/ppermute | solution.py:54
  139.1 1.1 finish_body.1
  (38 shorter events, 0.2 us)
Async XLA Ops:
  3.2 9.1 %collective-permute-start.3 = (bf16[144,512]{1,0:T(8,128)(2,1)}, bf16[144,512]{1,0:T(8,128)(2,1)S(1)}, u32[]{:S(2)}, u32[]{:S(2)}) collective-permute-start(bf16[144,512]{1,0:T(8,128)(2,1)} %get-tuple-element.65), channel_id=1, source_target_pairs={{0,1},{8,9},{1,2},{9,10},{2,3},{10,11},{3,0},{11,8},{16,17},{24,25... | collective-permute-start | bytes 442376 | tf_op jit(solution)/shard_map/keys_y1/ppermute | solution.py:54
  3.5 12.7 %collective-permute-start.4 = (bf16[144,512]{1,0:T(8,128)(2,1)}, bf16[144,512]{1,0:T(8,128)(2,1)S(1)}, u32[]{:S(2)}, u32[]{:S(2)}) collective-permute-start(bf16[144,512]{1,0:T(8,128)(2,1)} %get-tuple-element.66), channel_id=1, source_target_pairs={{0,2},{8,10},{1,3},{9,11},{2,0},{10,8},{3,1},{11,9},{16,18},{24,26... | collective-permute-start | bytes 442376 | tf_op jit(solution)/shard_map/keys_y2/ppermute | solution.py:54
  6.1 12.0 %collective-permute-start.5 = (bf16[144,512]{1,0:T(8,128)(2,1)}, bf16[144,512]{1,0:T(8,128)(2,1)S(1)}, u32[]{:S(2)}, u32[]{:S(2)}) collective-permute-start(bf16[144,512]{1,0:T(8,128)(2,1)} %get-tuple-element.67), channel_id=1, source_target_pairs={{0,3},{8,11},{1,0},{9,8},{2,1},{10,9},{3,2},{11,10},{16,19},{24,27... | collective-permute-start | bytes 442376 | tf_op jit(solution)/shard_map/keys_y3/ppermute | solution.py:54
  8.8 15.5 %collective-permute-start = (bf16[128,1024]{1,0:T(8,128)(2,1)}, bf16[128,1024]{1,0:T(8,128)(2,1)S(1)}, u32[]{:S(2)}, u32[]{:S(2)}) collective-permute-start(bf16[128,1024]{1,0:T(8,128)(2,1)} %get-tuple-element.60), channel_id=1, source_target_pairs={{0,1},{8,9},{1,2},{9,10},{2,3},{10,11},{3,0},{11,8},{16,17},{24,25... | collective-permute-start | bytes 786440 | tf_op jit(solution)/shard_map/queries0_y1/ppermute | solution.py:54
  12.1 12.2 %collective-permute-start.1 = (bf16[128,1024]{1,0:T(8,128)(2,1)}, bf16[128,1024]{1,0:T(8,128)(2,1)S(1)}, u32[]{:S(2)}, u32[]{:S(2)}) collective-permute-start(bf16[128,1024]{1,0:T(8,128)(2,1)} %get-tuple-element.61), channel_id=1, source_target_pairs={{0,2},{8,10},{1,3},{9,11},{2,0},{10,8},{3,1},{11,9},{16,18},{24,26... | collective-permute-start | bytes 786440 | tf_op jit(solution)/shard_map/queries0_y2/ppermute | solution.py:54
  12.3 5.8 %copy-start.5 = (bf16[128,1024]{1,0:T(8,128)(2,1)S(1)}, bf16[128,1024]{1,0:T(8,128)(2,1)}, u32[]{:S(2)}) copy-start(bf16[128,1024]{1,0:T(8,128)(2,1)} %get-tuple-element.71) | copy-start | bytes 786436
  12.3 7.9 %copy-start.2 = (bf16[144,512]{1,0:T(8,128)(2,1)S(1)}, bf16[144,512]{1,0:T(8,128)(2,1)}, u32[]{:S(2)}) copy-start(bf16[144,512]{1,0:T(8,128)(2,1)} %get-tuple-element.58.kv) | copy-start | bytes 442372
  12.3 12.0 %copy-start.4 = (bf16[128,1024]{1,0:T(8,128)(2,1)S(1)}, bf16[128,1024]{1,0:T(8,128)(2,1)}, u32[]{:S(2)}) copy-start(bf16[128,1024]{1,0:T(8,128)(2,1)} %get-tuple-element.72) | copy-start | bytes 786436
  12.3 19.4 %copy-start = (bf16[1,128,4096]{2,1,0:T(8,128)(2,1)S(1)}, bf16[1,128,4096]{2,1,0:T(8,128)(2,1)}, u32[]{:S(2)}) copy-start(bf16[1,128,4096]{2,1,0:T(8,128)(2,1)} %q.2) | copy-start | bytes 3145732
  12.4 19.4 %copy-start.1 = (bf16[1,128,4096]{2,1,0:T(8,128)(2,1)S(1)}, bf16[1,128,4096]{2,1,0:T(8,128)(2,1)}, u32[]{:S(2)}) copy-start(bf16[1,128,4096]{2,1,0:T(8,128)(2,1)} %g.5) | copy-start | bytes 3145732
  12.4 16.4 %collective-permute-start.2 = (bf16[128,1024]{1,0:T(8,128)(2,1)}, bf16[128,1024]{1,0:T(8,128)(2,1)S(1)}, u32[]{:S(2)}, u32[]{:S(2)}) collective-permute-start(bf16[128,1024]{1,0:T(8,128)(2,1)} %get-tuple-element.62), channel_id=1, source_target_pairs={{0,3},{8,11},{1,0},{9,8},{2,1},{10,9},{3,2},{11,10},{16,19},{24,27... | collective-permute-start | bytes 786440 | tf_op jit(solution)/shard_map/queries0_y3/ppermute | solution.py:54
  16.1 37.0 %collective-permute-start.8 = (bf16[128,1024]{1,0:T(8,128)(2,1)}, bf16[128,1024]{1,0:T(8,128)(2,1)S(1)}, u32[]{:S(2)}, u32[]{:S(2)}) collective-permute-start(bf16[128,1024]{1,0:T(8,128)(2,1)} %get-tuple-element.70), channel_id=1, source_target_pairs={{0,1},{8,9},{1,2},{9,10},{2,3},{10,11},{3,0},{11,8},{16,17},{24,25... | collective-permute-start | bytes 786440 | tf_op jit(solution)/shard_map/queries1_y1/ppermute | solution.py:54
  18.1 35.0 %collective-permute-start.9 = (bf16[128,1024]{1,0:T(8,128)(2,1)S(1)}, bf16[128,1024]{1,0:T(8,128)(2,1)S(1)}, u32[]{:S(2)}, u32[]{:S(2)}) collective-permute-start(bf16[128,1024]{1,0:T(8,128)(2,1)S(1)} %copy-done.5), channel_id=1, source_target_pairs={{0,2},{8,10},{1,3},{9,11},{2,0},{10,8},{3,1},{11,9},{16,18},{24,26... | collective-permute-start | bytes 786440 | tf_op jit(solution)/shard_map/queries1_y2/ppermute | solution.py:54
  24.3 28.9 %collective-permute-start.10 = (bf16[128,1024]{1,0:T(8,128)(2,1)S(1)}, bf16[128,1024]{1,0:T(8,128)(2,1)S(1)}, u32[]{:S(2)}, u32[]{:S(2)}) collective-permute-start(bf16[128,1024]{1,0:T(8,128)(2,1)S(1)} %copy-done.4), channel_id=1, source_target_pairs={{0,3},{8,11},{1,0},{9,8},{2,1},{10,9},{3,2},{11,10},{16,19},{24,27... | collective-permute-start | bytes 786440 | tf_op jit(solution)/shard_map/queries1_y3/ppermute | solution.py:54
  24.3 7.7 %copy-start.3 = (bf16[128,2048]{1,0:T(8,128)(2,1)S(1)}, bf16[128,2048]{1,0:T(8,128)(2,1)}, u32[]{:S(2)}) copy-start(bf16[128,2048]{1,0:T(8,128)(2,1)} %get-tuple-element.81) | copy-start | bytes 1572868
  24.3 7.7 %collective-permute-start.13 = (bf16[128,2048]{1,0:T(8,128)(2,1)}, bf16[128,2048]{1,0:T(8,128)(2,1)S(1)}, u32[]{:S(2)}, u32[]{:S(2)}) collective-permute-start(bf16[128,2048]{1,0:T(8,128)(2,1)} %get-tuple-element.82), channel_id=1, source_target_pairs={{0,8},{8,0},{1,9},{9,1},{2,10},{10,2},{3,11},{11,3},{16,24},{24,16... | collective-permute-start | bytes 1572872 | tf_op jit(solution)/shard_map/swap_inputs/ppermute | solution.py:54
  28.8 16.5 %collective-permute-start.6 = (bf16[576,512]{1,0:T(8,128)(2,1)S(1)}, bf16[576,512]{1,0:T(8,128)(2,1)S(1)}, u32[]{:S(2)}, u32[]{:S(2)}) collective-permute-start(bf16[576,512]{1,0:T(8,128)(2,1)S(1)} %pad_maximum_fusion.1), channel_id=1, source_target_pairs={{0,4},{8,12},{1,5},{9,13},{2,6},{10,14},{3,7},{11,15},{16,20},{24,... | collective-permute-start | bytes 1769480 | tf_op jit(solution)/shard_map/half/ppermute | solution.py:54
  32.2 32.6 %collective-permute-start.14 = (bf16[256,2048]{1,0:T(8,128)(2,1)S(1)}, bf16[256,2048]{1,0:T(8,128)(2,1)S(1)}, u32[]{:S(2)}, u32[]{:S(2)}) collective-permute-start(bf16[256,2048]{1,0:T(8,128)(2,1)S(1)} %pad_maximum_fusion.own), channel_id=1, source_target_pairs={{0,1},{8,9},{1,2},{9,10},{2,3},{10,11},{3,0},{11,8},{16,17},{24,25... | collective-permute-start | bytes 3145736 | tf_op jit(solution)/shard_map/inputs_up/ppermute | solution.py:54
  45.3 25.2 %collective-permute-start.16 = (bf16[256,2048]{1,0:T(8,128)(2,1)S(1)}, bf16[256,2048]{1,0:T(8,128)(2,1)S(1)}, u32[]{:S(2)}, u32[]{:S(2)}) collective-permute-start(bf16[256,2048]{1,0:T(8,128)(2,1)S(1)} %pad_maximum_fusion.own), channel_id=1, source_target_pairs={{0,3},{8,11},{1,0},{9,8},{2,1},{10,9},{3,2},{11,10},{16,19},{24,27... | collective-permute-start | bytes 3145736 | tf_op jit(solution)/shard_map/inputs_down/ppermute | solution.py:54
  61.5 9.1 %collective-permute-start.11 = (bf16[512,512]{1,0:T(8,128)(2,1)S(1)}, bf16[512,512]{1,0:T(8,128)(2,1)S(1)}, u32[]{:S(2)}, u32[]{:S(2)}) collective-permute-start(bf16[512,512]{1,0:T(8,128)(2,1)S(1)} %get-tuple-element.75.a1), channel_id=1, source_target_pairs={{0,8},{8,0},{1,9},{9,1},{2,10},{10,2},{3,11},{11,3},{16,24},{24,16... | collective-permute-start | bytes 1572872 | tf_op jit(solution)/shard_map/swap_dq1/ppermute | solution.py:54
  61.7 15.9 %collective-permute-start.12 = (bf16[512,512]{1,0:T(8,128)(2,1)S(1)}, bf16[512,512]{1,0:T(8,128)(2,1)S(1)}, u32[]{:S(2)}, u32[]{:S(2)}) collective-permute-start(bf16[512,512]{1,0:T(8,128)(2,1)S(1)} %pad_maximum_fusion.2), channel_id=1, source_target_pairs={{0,4},{8,12},{1,5},{9,13},{2,6},{10,14},{3,7},{11,15},{16,20},{24,... | collective-permute-start | bytes 1572872 | tf_op jit(solution)/shard_map/back/ppermute | solution.py:54
  64.8 14.8 %collective-permute-start.15 = (bf16[128,2048]{1,0:T(8,128)(2,1)S(1)}, bf16[128,2048]{1,0:T(8,128)(2,1)S(1)}, u32[]{:S(2)}, u32[]{:S(2)}) collective-permute-start(bf16[128,2048]{1,0:T(8,128)(2,1)S(1)} %slice.8), channel_id=1, source_target_pairs={{0,1},{8,9},{1,2},{9,10},{2,3},{10,11},{3,0},{11,8},{16,17},{24,25... | collective-permute-start | bytes 1572872 | tf_op jit(solution)/shard_map/inputs_up2/ppermute | solution.py:54
  70.5 13.1 %collective-permute-start.17 = (bf16[128,2048]{1,0:T(8,128)(2,1)S(1)}, bf16[128,2048]{1,0:T(8,128)(2,1)S(1)}, u32[]{:S(2)}, u32[]{:S(2)}) collective-permute-start(bf16[128,2048]{1,0:T(8,128)(2,1)S(1)} %slice.9), channel_id=1, source_target_pairs={{0,3},{8,11},{1,0},{9,8},{2,1},{10,9},{3,2},{11,10},{16,19},{24,27... | collective-permute-start | bytes 1572872 | tf_op jit(solution)/shard_map/inputs_down2/ppermute | solution.py:54
  70.6 13.3 %collective-permute-start.7 = (bf16[512,512]{1,0:T(8,128)(2,1)S(1)}, bf16[512,512]{1,0:T(8,128)(2,1)S(1)}, u32[]{:S(2)}, u32[]{:S(2)}) collective-permute-start(bf16[512,512]{1,0:T(8,128)(2,1)S(1)} %get-tuple-element.68.a0), channel_id=1, source_target_pairs={{0,8},{8,0},{1,9},{9,1},{2,10},{10,2},{3,11},{11,3},{16,24},{24,16... | collective-permute-start | bytes 1572872 | tf_op jit(solution)/shard_map/swap_dq0/ppermute | solution.py:54
  83.7 5.9 %collective-permute-start.18 = (bf16[512,512]{1,0:T(8,128)(2,1)S(1)}, bf16[512,512]{1,0:T(8,128)(2,1)S(1)}, u32[]{:S(2)}, u32[]{:S(2)}) collective-permute-start(bf16[512,512]{1,0:T(8,128)(2,1)S(1)} %fusion.k), channel_id=1, source_target_pairs={{0,8},{8,0},{1,9},{9,1},{2,10},{10,2},{3,11},{11,3},{16,24},{24,16... | collective-permute-start | bytes 1572872 | tf_op jit(solution)/shard_map/swap_dkv/ppermute | solution.py:54
  85.4 13.9 %collective-permute-start.19 = (bf16[768,256]{1,0:T(8,128)(2,1)S(1)}, bf16[768,256]{1,0:T(8,128)(2,1)S(1)}, u32[]{:S(2)}, u32[]{:S(2)}) collective-permute-start(bf16[768,256]{1,0:T(8,128)(2,1)S(1)} %get-tuple-element.87), channel_id=1, source_target_pairs={{0,32},{8,40},{1,33},{9,41},{2,34},{10,42},{3,35},{11,43},{16,48},... | collective-permute-start | bytes 1179656 | tf_op jit(solution)/shard_map/reduce_a_far_up/ppermute | solution.py:54
  87.4 11.9 %collective-permute-start.20 = (bf16[768,256]{1,0:T(8,128)(2,1)S(1)}, bf16[768,256]{1,0:T(8,128)(2,1)S(1)}, u32[]{:S(2)}, u32[]{:S(2)}) collective-permute-start(bf16[768,256]{1,0:T(8,128)(2,1)S(1)} %get-tuple-element.95), channel_id=1, source_target_pairs={{0,96},{8,104},{1,97},{9,105},{2,98},{10,106},{3,99},{11,107},{16,... | collective-permute-start | bytes 1179656 | tf_op jit(solution)/shard_map/reduce_a_far_down/ppermute | solution.py:54
  90.9 14.6 %collective-permute-start.26 = (bf16[384,512]{1,0:T(8,128)(2,1)S(1)}, bf16[384,512]{1,0:T(8,128)(2,1)S(1)}, u32[]{:S(2)}, u32[]{:S(2)}) collective-permute-start(bf16[384,512]{1,0:T(8,128)(2,1)S(1)} %get-tuple-element.90), channel_id=1, source_target_pairs={{0,16},{8,24},{1,17},{9,25},{2,18},{10,26},{3,19},{11,27},{16,4},{... | collective-permute-start | bytes 1179656 | tf_op jit(solution)/shard_map/reduce_b_far_up/ppermute | solution.py:54
  92.7 12.7 %collective-permute-start.27 = (bf16[384,512]{1,0:T(8,128)(2,1)S(1)}, bf16[384,512]{1,0:T(8,128)(2,1)S(1)}, u32[]{:S(2)}, u32[]{:S(2)}) collective-permute-start(bf16[384,512]{1,0:T(8,128)(2,1)S(1)} %get-tuple-element.106), channel_id=1, source_target_pairs={{0,20},{8,28},{1,21},{9,29},{2,22},{10,30},{3,23},{11,31},{16,0},{... | collective-permute-start | bytes 1179656 | tf_op jit(solution)/shard_map/reduce_b_far_down/ppermute | solution.py:54
  99.5 20.6 %collective-permute-start.21 = (bf16[768,512]{1,0:T(8,128)(2,1)S(1)}, bf16[768,512]{1,0:T(8,128)(2,1)S(1)}, u32[]{:S(2)}, u32[]{:S(2)}) collective-permute-start(bf16[768,512]{1,0:T(8,128)(2,1)S(1)} %get-tuple-element.96), channel_id=1, source_target_pairs={{0,32},{8,40},{1,33},{9,41},{2,34},{10,42},{3,35},{11,43},{16,48},... | collective-permute-start | bytes 2359304 | tf_op jit(solution)/shard_map/reduce_a_up/ppermute | solution.py:54
  100.8 19.3 %collective-permute-start.22 = (bf16[768,512]{1,0:T(8,128)(2,1)S(1)}, bf16[768,512]{1,0:T(8,128)(2,1)S(1)}, u32[]{:S(2)}, u32[]{:S(2)}) collective-permute-start(bf16[768,512]{1,0:T(8,128)(2,1)S(1)} %get-tuple-element.97), channel_id=1, source_target_pairs={{0,96},{8,104},{1,97},{9,105},{2,98},{10,106},{3,99},{11,107},{16,... | collective-permute-start | bytes 2359304 | tf_op jit(solution)/shard_map/reduce_a_down/ppermute | solution.py:54
  105.7 21.8 %collective-permute-start.28 = (bf16[384,1024]{1,0:T(8,128)(2,1)S(1)}, bf16[384,1024]{1,0:T(8,128)(2,1)S(1)}, u32[]{:S(2)}, u32[]{:S(2)}) collective-permute-start(bf16[384,1024]{1,0:T(8,128)(2,1)S(1)} %get-tuple-element.107), channel_id=1, source_target_pairs={{0,16},{8,24},{1,17},{9,25},{2,18},{10,26},{3,19},{11,27},{16,4},{... | collective-permute-start | bytes 2359304 | tf_op jit(solution)/shard_map/reduce_b_up/ppermute | solution.py:54
  107.2 20.5 %collective-permute-start.29 = (bf16[384,1024]{1,0:T(8,128)(2,1)S(1)}, bf16[384,1024]{1,0:T(8,128)(2,1)S(1)}, u32[]{:S(2)}, u32[]{:S(2)}) collective-permute-start(bf16[384,1024]{1,0:T(8,128)(2,1)S(1)} %get-tuple-element.108), channel_id=1, source_target_pairs={{0,20},{8,28},{1,21},{9,29},{2,22},{10,30},{3,23},{11,31},{16,0},{... | collective-permute-start | bytes 2359304 | tf_op jit(solution)/shard_map/reduce_b_down/ppermute | solution.py:54
  120.6 10.9 %collective-permute-start.23 = (bf16[384,256]{1,0:T(8,128)(2,1)S(1)}, bf16[384,256]{1,0:T(8,128)(2,1)S(1)}, u32[]{:S(2)}, u32[]{:S(2)}) collective-permute-start(bf16[384,256]{1,0:T(8,128)(2,1)S(1)} %get-tuple-element.99), channel_id=1, source_target_pairs={{0,16},{8,24},{1,17},{9,25},{2,18},{10,26},{3,19},{11,27},{16,4},{... | collective-permute-start | bytes 589832 | tf_op jit(solution)/shard_map/second_a_x1/ppermute | solution.py:54
  122.2 9.7 %collective-permute-start.24 = (bf16[384,256]{1,0:T(8,128)(2,1)S(1)}, bf16[384,256]{1,0:T(8,128)(2,1)S(1)}, u32[]{:S(2)}, u32[]{:S(2)}) collective-permute-start(bf16[384,256]{1,0:T(8,128)(2,1)S(1)} %get-tuple-element.100), channel_id=1, source_target_pairs={{0,20},{8,28},{1,21},{9,29},{2,22},{10,30},{3,23},{11,31},{16,0},{... | collective-permute-start | bytes 589832 | tf_op jit(solution)/shard_map/second_a_x3/ppermute | solution.py:54
  123.9 11.2 %collective-permute-start.25 = (bf16[384,256]{1,0:T(8,128)(2,1)S(1)}, bf16[384,256]{1,0:T(8,128)(2,1)S(1)}, u32[]{:S(2)}, u32[]{:S(2)}) collective-permute-start(bf16[384,256]{1,0:T(8,128)(2,1)S(1)} %get-tuple-element.101), channel_id=1, source_target_pairs={{0,4},{8,12},{1,5},{9,13},{2,6},{10,14},{3,7},{11,15},{16,20},{24,... | collective-permute-start | bytes 589832 | tf_op jit(solution)/shard_map/second_a_x2/ppermute | solution.py:54
  128.2 10.9 %collective-permute-start.30 = (bf16[384,256]{1,0:T(8,128)(2,1)S(1)}, bf16[384,256]{1,0:T(8,128)(2,1)S(1)}, u32[]{:S(2)}, u32[]{:S(2)}) collective-permute-start(bf16[384,256]{1,0:T(8,128)(2,1)S(1)} %get-tuple-element.110), channel_id=1, source_target_pairs={{0,32},{8,40},{1,33},{9,41},{2,34},{10,42},{3,35},{11,43},{16,48},... | collective-permute-start | bytes 589832 | tf_op jit(solution)/shard_map/second_b_z1/ppermute | solution.py:54
  128.3 10.8 %collective-permute-start.31 = (bf16[384,256]{1,0:T(8,128)(2,1)S(1)}, bf16[384,256]{1,0:T(8,128)(2,1)S(1)}, u32[]{:S(2)}, u32[]{:S(2)}) collective-permute-start(bf16[384,256]{1,0:T(8,128)(2,1)S(1)} %get-tuple-element.111), channel_id=1, source_target_pairs={{0,96},{8,104},{1,97},{9,105},{2,98},{10,106},{3,99},{11,107},{16,... | collective-permute-start | bytes 589832 | tf_op jit(solution)/shard_map/second_b_z3/ppermute | solution.py:54
  131.5 7.6 %collective-permute-start.32 = (bf16[384,256]{1,0:T(8,128)(2,1)S(1)}, bf16[384,256]{1,0:T(8,128)(2,1)S(1)}, u32[]{:S(2)}, u32[]{:S(2)}) collective-permute-start(bf16[384,256]{1,0:T(8,128)(2,1)S(1)} %get-tuple-element.112), channel_id=1, source_target_pairs={{0,64},{8,72},{1,65},{9,73},{2,66},{10,74},{3,67},{11,75},{16,80},... | collective-permute-start | bytes 589832 | tf_op jit(solution)/shard_map/second_b_z2/ppermute | solution.py:54
